TPU v7x, 256 devices: a whole 4x4x8 slice. The times are simulated.
256 devices in a mesh: dp: 16 (over y, z_lo, core), ctx: 16 (over x, z_hi).
Axes of the slice: x: 4, y: 4, z: 8 (z_hi: 4, z_lo: 2; z = z_hi * 2 + z_lo), core: 2. Of those that a mesh axis runs over, the one named last changes fastest.
Arguments:
- text: bfloat16 [16, 2, 128, 2048], P('dp', None, None, 'ctx'), may hold values from -6 to 6
- src: int32 [16], replicated, may hold values from 0 to 15, each once
- lengths: int32 [16, 2], replicated, may hold values from 1 to 128
- kv_weight: bfloat16 [2048, 2, 8192], P('dp', None, 'ctx'), may hold values from -0.125 to 0.125
- queries: bfloat16 [16, 4096, 4096], P('dp', 'ctx'), may hold values from -160 to 160
- grad_out: bfloat16 [16, 4096, 4096], P('dp', 'ctx'), may hold values from -6 to 6
Outputs:
- attended: bfloat16 [16, 4096, 4096], P('dp', 'ctx')
- grad_queries: bfloat16 [16, 4096, 4096], P('dp', 'ctx')
- grad_weight: float32 [2048, 2, 8192], P('dp', None, 'ctx')
Inputs may be any that keep to these rules, and one draw needn't show every extreme that they name: `src`: each text sample is used by exactly one latent sample. `lengths`: tokens of an encoder output at or beyond its length are padding.
All inputs are finite; a program needn't handle non-finite values.
Results may differ from a plain program's by a relative error of at most 0.018.
The roundings to bfloat16 on the way count: a program that leaves them out, or rounds other values in their place, can miss the bound.
Values may be sent and summed in bfloat16 or wider, within the bound.
No kernel may reach another device: no remote copies, remote signals or barrier semaphores. Data moves between devices by JAX's collectives and lax.ppermute only.
A program may use at most 128 MiB of HBM per device.

v0:
```python
import math

import jax
import jax.numpy as jnp
from jax import lax
from jax.sharding import PartitionSpec as P

HEAD = 128


def from_everyone(x, axis):
    copies = jnp.broadcast_to(x, (lax.axis_size(axis), *x.shape))
    return lax.all_to_all(copies, axis, split_axis=0, concat_axis=0, tiled=True)


def joined_along(pieces, dim):
    shape = list(pieces.shape[1:])
    shape[dim] *= pieces.shape[0]
    return jnp.moveaxis(pieces, 0, dim).reshape(shape)


def collect(x, axis, dim):
    pieces = from_everyone(x, axis)
    return joined_along(pieces, dim)


def in_one_piece(arrays, axis, split_dim, concat_dim, along):
    ends, at = ([], 0)
    for a in arrays[:-1]:
        at += a.shape[along]
        ends.append(at)
    both = jnp.concatenate(arrays, axis=along)
    return tuple(
        jnp.split(
            lax.all_to_all(both, axis, split_axis=split_dim, concat_axis=concat_dim, tiled=True),
            ends,
            axis=along,
        )
    )


def attend(queries, key_value, valid, grad_out):
    batch, length, width = queries.shape
    heads = width // HEAD
    keys = key_value.shape[1] * key_value.shape[2]
    scale = 1.0 / math.sqrt(HEAD)
    paired = key_value.reshape(batch, keys, heads, 2, HEAD)
    key = paired[:, :, :, 0]
    value = paired[:, :, :, 1]
    q_rows = queries.reshape(batch, length, heads, HEAD)
    g_rows = grad_out.reshape(batch, length, heads, HEAD)
    scores = jnp.einsum("blhd,bjhd->bhlj", q_rows, key, preferred_element_type=jnp.float32) * scale
    scores = jnp.where(valid[:, None, None, :], scores, -1e30)
    top = jnp.max(scores, axis=-1, keepdims=True)
    weights = jnp.exp(scores - top)
    probs = weights / jnp.sum(weights, axis=-1, keepdims=True)
    probs_low = probs.astype(jnp.bfloat16)
    attended = jnp.einsum("bhlj,bjhd->blhd", probs_low, value, preferred_element_type=jnp.float32)
    attended = attended.reshape(batch, length, width).astype(jnp.bfloat16)
    grad_probs = jnp.einsum("blhd,bjhd->bhlj", g_rows, value, preferred_element_type=jnp.float32)
    delta = jnp.sum(probs * grad_probs, axis=-1, keepdims=True)
    grad_scores = (probs * (grad_probs - delta) * scale).astype(jnp.bfloat16)
    grad_queries = jnp.einsum(
        "bhlj,bjhd->blhd", grad_scores, key, preferred_element_type=jnp.float32
    )
    grad_queries = grad_queries.reshape(batch, length, width).astype(jnp.bfloat16)
    grad_key = jnp.einsum(
        "bhlj,blhd->bjhd", grad_scores, q_rows, preferred_element_type=jnp.float32
    )
    grad_value = jnp.einsum(
        "bhlj,blhd->bjhd", probs_low, g_rows, preferred_element_type=jnp.float32
    )
    grad_kv = jnp.stack([grad_key, grad_value], axis=3).reshape(
        batch, 2, keys // 2, heads * 2 * HEAD
    )
    return (attended, grad_queries, grad_kv)


def per_device(text, src, lengths, kv_weight, queries, grad_out):
    per_group = queries.shape[0]
    group = lax.axis_index("dp")
    everyone = collect(text, "dp", 0)
    chosen_ids = lax.dynamic_slice_in_dim(src, group * per_group, per_group, 0)
    picked = jnp.take(everyone, chosen_ids, axis=0)
    full_text = collect(picked, "ctx", 3)
    tokens = full_text.shape[2]
    kv_local = jnp.einsum(
        "betf,fec->betc",
        full_text,
        lax.all_gather(kv_weight, "dp", axis=0, tiled=True),
        preferred_element_type=jnp.float32,
    ).astype(jnp.bfloat16)
    chosen_lengths = jnp.take(lengths, chosen_ids, axis=0)
    positions = jnp.arange(tokens, dtype=jnp.int32)
    valid = (positions[None, None, :] < chosen_lengths[:, :, None]).reshape(per_group, 2 * tokens)
    moved_queries, moved_grads = in_one_piece((queries, grad_out), "ctx", 2, 1, 0)
    head_out, head_grad, grad_kv = attend(moved_queries, kv_local, valid, moved_grads)
    attended, grad_queries = in_one_piece((head_out, head_grad), "ctx", 1, 2, 0)
    grad_low = grad_kv.astype(jnp.bfloat16)
    every_grad = lax.all_gather(grad_low, "dp", axis=0, tiled=True)
    own_rows = lax.all_to_all(full_text, "dp", split_axis=3, concat_axis=0, tiled=True)
    grad_weight = jnp.einsum(
        "betf,betc->fec", own_rows, every_grad, preferred_element_type=jnp.float32
    )
    return (attended, grad_queries, grad_weight)


def solution(mesh):
    placed = (
        P("dp", None, None, "ctx"),
        P(),
        P(),
        P("dp", None, "ctx"),
        P("dp", "ctx", None),
        P("dp", "ctx", None),
    )
    return jax.shard_map(
        per_device,
        mesh=mesh,
        in_specs=placed,
        out_specs=(P("dp", "ctx", None), P("dp", "ctx", None), P("dp", None, "ctx")),
        check_vma=False,
    )
```

profile of v0, /device:TPU:11, one launch (start us, length us, event | category | flops | bytes accessed | tf_op | source)
XLA Modules:
  0.0 409.2 jit_solution(5309346918254861322)
XLA Ops:
  7.2 2.1 broadcast_in_dim.43
  9.3 6.6 %all-to-all-start = ((bf16[16,1,2,128,128]{4,3,2,1,0:T(8,128)(2,1)}), bf16[16,1,2,128,128]{4,3,2,1,0:T(8,128)(2,1)S(1)}, u32[]{:S(2)}, u32[]{:S(2)}) async-start(bf16[16,1,2,128,128]{4,3,2,1,0:T(8,128)(2,1)} %broadcast_in_dim.43), calls=%async_computation | async-start | bytes 2097152 | tf_op jit(solution)/shard_map/all_to_all | solution.py:13
  15.9 1.2 dynamic_slice.3
  19.1 10.7 %all-to-all-done = bf16[16,1,2,128,128]{4,3,2,1,0:T(8,128)(2,1)S(1)} async-done(((bf16[16,1,2,128,128]{4,3,2,1,0:T(8,128)(2,1)}), bf16[16,1,2,128,128]{4,3,2,1,0:T(8,128)(2,1)S(1)}, u32[]{:S(2)}, u32[]{:S(2)}) %all-to-all-start) | async-done | bytes 1048608 | tf_op jit(solution)/shard_map/all_to_all | solution.py:13
  29.7 1.2 broadcast_in_dim.45
  31.0 10.0 %all-to-all-start.1 = ((bf16[16,1,2,128,128]{4,3,2,1,0:T(8,128)(2,1)}), bf16[16,1,2,128,128]{4,3,2,1,0:T(8,128)(2,1)S(1)}, u32[]{:S(2)}, u32[]{:S(2)}) async-start(bf16[16,1,2,128,128]{4,3,2,1,0:T(8,128)(2,1)} %broadcast_in_dim.45), calls=%async_computation.1 | async-start | bytes 2097152 | tf_op jit(solution)/shard_map/all_to_all | solution.py:13
  41.0 0.7 copy.92
  41.8 4.6 %pad_maximum_fusion = bf16[2,256,4096]{2,1,0:T(8,128)(2,1)} fusion(bf16[1,256,4096]{2,1,0:T(8,128)(2,1)} %param.11, bf16[1,256,4096]{2,1,0:T(8,128)(2,1)} %param.10), kind=kLoop, calls=%fused_computation.10 | loop fusion | flops 2097152 | bytes 8388608 | tf_op jit(solution)/shard_map/concatenate | solution.py:32
  46.4 11.1 %copy.94 = bf16[2,256,4096]{1,0,2:T(2,128)(2,1)} copy(bf16[2,256,4096]{2,1,0:T(8,128)(2,1)} %pad_maximum_fusion) | data formatting | bytes 8388608 | tf_op jit(solution)/shard_map/concatenate | solution.py:32
  57.5 5.9 %all-to-all-done.1 = bf16[16,1,2,128,128]{4,3,2,1,0:T(8,128)(2,1)S(1)} async-done(((bf16[16,1,2,128,128]{4,3,2,1,0:T(8,128)(2,1)}), bf16[16,1,2,128,128]{4,3,2,1,0:T(8,128)(2,1)S(1)}, u32[]{:S(2)}, u32[]{:S(2)}) %all-to-all-start.1) | async-done | bytes 1048608 | tf_op jit(solution)/shard_map/all_to_all | solution.py:13
  63.4 9.8 %all-to-all-start.2 = ((bf16[2,256,4096]{1,0,2:T(2,128)(2,1)}), bf16[2,256,4096]{1,0,2:T(2,128)(2,1)}, u32[]{:S(2)}, u32[]{:S(2)}) async-start(bf16[2,256,4096]{1,0,2:T(2,128)(2,1)} %copy.94), calls=%async_computation.2 | async-start | bytes 8388608 | tf_op jit(solution)/shard_map/all_to_all | solution.py:35
  73.2 0.2 fusion.36
  73.4 0.1 lt.36
  73.5 0.7 copy.90
  74.2 9.4 %copy.111 = bf16[1,2,128,2048]{2,1,0,3:T(2,128)(2,1)} copy(bf16[1,2,128,2048]{2,3,1,0:T(8,128)(2,1)S(1)} %bitcast.93) | data formatting | bytes 2097152 | tf_op jit(solution)/shard_map/reshape | solution.py:19
  83.6 35.8 %all-gather.3.cloned.1.call-done = bf16[2048,2,512]{2,0,1:T(8,128)(2,1)} async-done(((bf16[128,2,512]{2,0,1:T(8,128)(2,1)}), bf16[2048,2,512]{2,0,1:T(8,128)(2,1)}) %all-gather.3.cloned.1.call-update) | async-done | bytes 4194320 | tf_op jit(solution)/shard_map/all_gather | solution.py:90
  119.4 3.0 fusion.19
  122.4 0.1 reshape.187
  122.4 0.4 fusion.45
  122.8 0.1 copy.127
  122.9 39.4 %all-to-all-done.2 = bf16[2,256,4096]{1,0,2:T(2,128)(2,1)} async-done(((bf16[2,256,4096]{1,0,2:T(2,128)(2,1)}), bf16[2,256,4096]{1,0,2:T(2,128)(2,1)}, u32[]{:S(2)}, u32[]{:S(2)}) %all-to-all-start.2) | async-done | bytes 4194336 | tf_op jit(solution)/shard_map/all_to_all | solution.py:35
  162.3 22.4 %all-to-all-start.4 = ((bf16[1,2,128,2048]{2,1,0,3:T(2,128)(2,1)}), bf16[1,2,128,2048]{2,1,0,3:T(2,128)(2,1)S(1)}, u32[]{:S(2)}, u32[]{:S(2)}) async-start(bf16[1,2,128,2048]{2,1,0,3:T(2,128)(2,1)} %copy.111), calls=%async_computation.4 | async-start | bytes 2097152 | tf_op jit(solution)/shard_map/all_to_all | solution.py:101
  184.8 4.6 %copy.137 = bf16[2,256,16,256]{1,2,3,0:T(8,128)(2,1)S(1)} copy(bf16[2,256,16,256]{1,0,3,2:T(2,128)(2,1)} %bitcast.12) | data formatting | bytes 8388608 | tf_op jit(solution)/shard_map/all_to_all | solution.py:35
  189.4 1.6 fusion.44
  190.9 2.3 reshape.189
  193.3 3.1 reshape.191
  196.3 4.5 %fusion.33 = f32[2,4096,256]{1,2,0:T(8,128)} fusion(bf16[4096,2,128]{0,2,1:T(8,128)(2,1)S(1)} %reshape.191, bf16[1,256,2,1,128]{1,4,2,3,0:T(8,128)(2,1)S(1)} %copy.127), kind=kOutput, calls=%fused_computation.32 | convolution fusion | flops 536870912 | bytes 10616832 | tf_op jit(solution)/shard_map/blhd,bjhd->bhlj/dot_general | solution.py:60
  200.9 8.6 %fusion.46 = (f32[2,4096]{1,0:T(2,128)}, f32[2,4096,256]{1,2,0:T(8,128)}) fusion(pred[256]{0:T(512)(128)(4,1)S(1)} %bitcast_compare_fusion, bf16[4096,2,128]{0,2,1:T(8,128)(2,1)} %reshape.189, bf16[1,256,2,1,128]{4,3,2,1,0:T(2,128)(2,1)S(1)} %get-tuple-element.44), kind=kOutput, calls=%fused_computation.48 | convolution fusion | flops 545259776 | bytes 10649856 | tf_op jit(solution)/shard_map/sub | solution.py:55
  209.5 15.4 %fusion.29 = bf16[1,256,2,1,128]{1,4,2,3,0:T(8,128)(2,1)} fusion(bf16[4096,2,128]{0,2,1:T(8,128)(2,1)} %reshape.189, f32[2,4096,256]{1,2,0:T(8,128)} %fusion.33, f32[2,4096,256]{1,2,0:T(8,128)} %get-tuple-element.47, f32[2,4096]{1,0:T(2,128)} %get-tuple-element.46), kind=kOutput, calls=%fused_computation.28 | convolution fusion | flops 551624960 | bytes 19038208 | tf_op jit(solution)/shard_map/bhlj,blhd->bjhd/dot_general | solution.py:67
  224.9 15.3 %convolution_convert_fusion = bf16[2,128,4096]{2,1,0:T(8,128)(2,1)} fusion(f32[2,4096,256]{1,2,0:T(8,128)} %fusion.33, bf16[1,256,2,1,128]{4,3,2,1,0:T(2,128)(2,1)S(1)} %get-tuple-element.44, f32[2,4096,256]{1,2,0:T(8,128)} %get-tuple-element.47, f32[2,4096]{1,0:T(2,128)} %get-tuple-element.46), kind=kOutput, calls=%fused_computation.8 | convolution fusion | flops 552608000 | bytes 19038208 | tf_op jit(solution)/shard_map/bhlj,bjhd->blhd/dot_general | solution.py:63
  240.2 5.0 %fusion.26 = bf16[1,256,2,1,128]{1,4,2,3,0:T(8,128)(2,1)S(1)} fusion(bf16[4096,2,128]{0,2,1:T(8,128)(2,1)S(1)} %reshape.191, f32[2,4096,256]{1,2,0:T(8,128)} %get-tuple-element.47, f32[2,4096]{1,0:T(2,128)} %get-tuple-element.46), kind=kOutput, calls=%fused_computation.27 | convolution fusion | flops 541130752 | bytes 10649600 | tf_op jit(solution)/shard_map/bhlj,blhd->bjhd/dot_general | solution.py:70
  245.2 0.2 copy.109
  245.3 0.3 convert_element_type.86
  245.7 0.8 copy.110
  246.5 10.1 %copy.104 = bf16[1,4096,256]{2,0,1:T(2,128)(2,1)} copy(bf16[1,4096,256]{1,2,0:T(8,128)(2,1)} %bitcast.97) | data formatting | bytes 4194304 | tf_op jit(solution)/shard_map/convert_element_type | solution.py:66
  256.6 4.3 %convolution_convert_fusion.1 = bf16[2,128,4096]{2,1,0:T(8,128)(2,1)S(1)} fusion(bf16[1,256,2,1,128]{1,4,2,3,0:T(8,128)(2,1)S(1)} %copy.127, f32[2,4096,256]{1,2,0:T(8,128)} %get-tuple-element.47, f32[2,4096]{1,0:T(2,128)S(1)} %copy-done.3), kind=kOutput, calls=%fused_computation.9 | convolution fusion | flops 542113792 | bytes 10649600 | tf_op jit(solution)/shard_map/bhlj,bjhd->blhd/dot_general | solution.py:58
  260.9 7.4 %copy.103 = bf16[1,4096,256]{2,0,1:T(2,128)(2,1)} copy(bf16[1,4096,256]{1,2,0:T(8,128)(2,1)S(1)} %bitcast.98) | data formatting | bytes 4194304 | tf_op jit(solution)/shard_map/convert_element_type | solution.py:59
  268.3 10.8 %pad_maximum_fusion.1 = bf16[2,4096,256]{2,0,1:T(2,128)(2,1)} fusion(bf16[1,4096,256]{2,0,1:T(2,128)(2,1)} %copy.104, bf16[1,4096,256]{2,0,1:T(2,128)(2,1)} %copy.103), kind=kLoop, calls=%fused_computation.11 | loop fusion | flops 8388608 | bytes 8388608 | tf_op jit(solution)/shard_map/concatenate | solution.py:32
  279.2 6.2 %all-to-all-start.3 = ((bf16[2,4096,256]{2,0,1:T(2,128)(2,1)}), bf16[2,4096,256]{2,0,1:T(2,128)(2,1)}, u32[]{:S(2)}, u32[]{:S(2)}) async-start(bf16[2,4096,256]{2,0,1:T(2,128)(2,1)} %pad_maximum_fusion.1), calls=%async_computation.3 | async-start | bytes 8388608 | tf_op jit(solution)/shard_map/all_to_all | solution.py:35
  285.4 0.9 copy.113
  286.3 3.4 convolution_bitcast_fusion
  289.8 1.0 copy.114
  290.8 90.6 %all-to-all-done.3 = bf16[2,4096,256]{2,0,1:T(2,128)(2,1)} async-done(((bf16[2,4096,256]{2,0,1:T(2,128)(2,1)}), bf16[2,4096,256]{2,0,1:T(2,128)(2,1)}, u32[]{:S(2)}, u32[]{:S(2)}) %all-to-all-start.3) | async-done | bytes 4194336 | tf_op jit(solution)/shard_map/all_to_all | solution.py:35
  381.3 9.6 %fusion.43 = (bf16[1,256,16,256]{3,0,1,2:T(2,128)(2,1)S(1)}, bf16[1,256,16,256]{3,0,1,2:T(2,128)(2,1)}) fusion(bf16[2,256,16,256]{3,0,1,2:T(2,128)(2,1)} %bitcast.22), kind=kLoop, calls=%fused_computation.45 | loop fusion | bytes 8388608 | tf_op jit(solution)/shard_map/split | solution.py:34
  391.0 2.3 copy.106
  393.2 2.3 split.21
  395.5 4.4 %copy.105 = bf16[1,256,16,256]{3,2,1,0:T(8,128)(2,1)S(1)} copy(bf16[1,256,16,256]{3,0,1,2:T(2,128)(2,1)} %get-tuple-element.41) | data formatting | bytes 4194304 | tf_op jit(solution)/shard_map/split | solution.py:34
  400.0 2.3 split.19
  (17 shorter events, 0.2 us)
Async XLA Ops:
  7.2 33.9 %copy-start = (bf16[128,2,512]{2,1,0:T(2,128)(2,1)S(1)}, bf16[128,2,512]{2,1,0:T(2,128)(2,1)}, u32[]{:S(2)}) copy-start(bf16[128,2,512]{2,1,0:T(2,128)(2,1)} %param.9) | copy-start | bytes 786436
  9.3 20.5 %all-to-all-start = ((bf16[16,1,2,128,128]{4,3,2,1,0:T(8,128)(2,1)}), bf16[16,1,2,128,128]{4,3,2,1,0:T(8,128)(2,1)S(1)}, u32[]{:S(2)}, u32[]{:S(2)}) async-start(bf16[16,1,2,128,128]{4,3,2,1,0:T(8,128)(2,1)} %broadcast_in_dim.43), calls=%async_computation | async-start | bytes 2097152 | tf_op jit(solution)/shard_map/all_to_all | solution.py:13
  31.0 32.4 %all-to-all-start.1 = ((bf16[16,1,2,128,128]{4,3,2,1,0:T(8,128)(2,1)}), bf16[16,1,2,128,128]{4,3,2,1,0:T(8,128)(2,1)S(1)}, u32[]{:S(2)}, u32[]{:S(2)}) async-start(bf16[16,1,2,128,128]{4,3,2,1,0:T(8,128)(2,1)} %broadcast_in_dim.45), calls=%async_computation.1 | async-start | bytes 2097152 | tf_op jit(solution)/shard_map/all_to_all | solution.py:13
  41.0 78.4 %all-gather.3.cloned.1.call-start = ((), (), s32[]{:S(2)}) async-start(), calls=%async_computation.5 | async-start | bytes 4456448 | tf_op jit(solution)/shard_map/all_gather | solution.py:90
  57.5 15.7 %copy-start.2 = (s32[16,2]{0,1:T(2,128)S(1)}, s32[16,2]{0,1:T(2,128)}, u32[]{:S(2)}) copy-start(s32[16,2]{0,1:T(2,128)} %param.8) | copy-start | bytes 388
  63.4 98.9 %all-to-all-start.2 = ((bf16[2,256,4096]{1,0,2:T(2,128)(2,1)}), bf16[2,256,4096]{1,0,2:T(2,128)(2,1)}, u32[]{:S(2)}, u32[]{:S(2)}) async-start(bf16[2,256,4096]{1,0,2:T(2,128)(2,1)} %copy.94), calls=%async_computation.2 | async-start | bytes 8388608 | tf_op jit(solution)/shard_map/all_to_all | solution.py:35
  162.3 116.8 %all-to-all-start.4 = ((bf16[1,2,128,2048]{2,1,0,3:T(2,128)(2,1)}), bf16[1,2,128,2048]{2,1,0,3:T(2,128)(2,1)S(1)}, u32[]{:S(2)}, u32[]{:S(2)}) async-start(bf16[1,2,128,2048]{2,1,0,3:T(2,128)(2,1)} %copy.111), calls=%async_computation.4 | async-start | bytes 2097152 | tf_op jit(solution)/shard_map/all_to_all | solution.py:101
  184.7 101.6 %all-gather.5.cloned.1.call-start = ((), (), s32[]{:S(2)}) async-start(), calls=%async_computation.6 | async-start | bytes 4456448 | tf_op jit(solution)/shard_map/all_gather | solution.py:100
  240.2 5.0 %copy-start.1 = (bf16[1,256,2,1,128]{1,4,2,3,0:T(8,128)(2,1)S(1)}, bf16[1,256,2,1,128]{1,4,2,3,0:T(8,128)(2,1)}, u32[]{:S(2)}) copy-start(bf16[1,256,2,1,128]{1,4,2,3,0:T(8,128)(2,1)} %fusion.29) | copy-start | bytes 393220
  245.2 11.4 %copy-start.3 = (f32[2,4096]{1,0:T(2,128)S(1)}, f32[2,4096]{1,0:T(2,128)}, u32[]{:S(2)}) copy-start(f32[2,4096]{1,0:T(2,128)} %get-tuple-element.46) | copy-start | bytes 98308
  279.2 102.2 %all-to-all-start.3 = ((bf16[2,4096,256]{2,0,1:T(2,128)(2,1)}), bf16[2,4096,256]{2,0,1:T(2,128)(2,1)}, u32[]{:S(2)}, u32[]{:S(2)}) async-start(bf16[2,4096,256]{2,0,1:T(2,128)(2,1)} %pad_maximum_fusion.1), calls=%async_computation.3 | async-start | bytes 8388608 | tf_op jit(solution)/shard_map/all_to_all | solution.py:35
Sparse Core Ops, SparseCore 0:
  44.2 75.1 all-gather.2
  246.7 38.7 all-gather.4
where the time goes:
time: 415 us; the launch traced here: 409 us
  waiting for transfers between devices  182 us (44%)
  local copies, waits for them, and re-layouts  80.4 us (19%)
  matrix products  59.5 us (14%)
  starting transfers between devices  55.1 us (13%)
  between operations  16.1 us (4%)
  other arithmetic  15.7 us (4%)
    all_to_all x2, waiting for transfers between devices, in_one_piece(): lax.all_to_all(both, axis, split_axis=split_dim, concat_axis=concat_dim,...  130 us
    all_gather x1, waiting for transfers between devices, per_device(): lax.all_gather(kv_weight, 'dp', axis=0, tiled=True)  35.8 us
    split x6, local copies, waits for them, and re-layouts, in_one_piece(): jnp.split(lax.all_to_all(both, axis, split_axis=split_dim, concat_axis=co...  22.6 us
    all_to_all x1, starting transfers between devices, per_device(): lax.all_to_all(full_text, 'dp', split_axis=3, concat_axis=0, tiled=True)  22.4 us
    all_to_all x2, starting transfers between devices, from_everyone(): return lax.all_to_all(copies, axis, split_axis=0, concat_axis=0, tiled=True)  16.6 us
    all_to_all x2, waiting for transfers between devices, from_everyone(): return lax.all_to_all(copies, axis, split_axis=0, concat_axis=0, tiled=True)  16.6 us
    all_to_all x2, starting transfers between devices, in_one_piece(): lax.all_to_all(both, axis, split_axis=split_dim, concat_axis=concat_dim,...  16 us
    concatenate x2, other arithmetic, in_one_piece(): both = jnp.concatenate(arrays, axis=along)  15.4 us
  transfers between devices with their start and end apart: 7, of which 5 were waited for; matrix products, arithmetic and copies ran while one was open for 32% of the time, Pallas kernels for 0%

commit v1 on v0

v1 whole, which is shorter than its diff:
```python
import math

import jax
import jax.numpy as jnp
from jax import lax
from jax.experimental import pallas as pl
from jax.experimental.pallas import tpu as pltpu
from jax.sharding import PartitionSpec as P

HEAD = 128
N = 4
GROUPS = ((0, 1), (3, 2))
BF = jnp.bfloat16
F32 = jnp.float32


def x_shift(a, k):
    return lax.ppermute(
        a, "ctx", [(4 * x + z, 4 * ((x + k) % N) + z) for x in range(N) for z in range(N)]
    )


def z_shift(a, m):
    return lax.ppermute(
        a, "ctx", [(4 * x + z, 4 * x + (z + m) % N) for x in range(N) for z in range(N)]
    )


def dot(a, b, dims):
    return lax.dot_general(a, b, (dims, ((), ())), preferred_element_type=F32)


def pack(group, where, queries, grad_out):
    def body(s, q, g, *rest):
        outs, sem = rest[:-1], rest[-1]
        copies = []
        for k in (1, 2, 3):
            for a, src in enumerate((q, g)):
                for n, m in enumerate(group):
                    col = pl.multiple_of(
                        lax.rem(s[0] + k, N) * 1024 + lax.rem(s[1] + N - m, N) * 256, 256
                    )
                    copies.append(
                        pltpu.make_async_copy(
                            src.at[:, pl.ds(col, 256)],
                            outs[k - 1].at[a, n],
                            sem.at[len(copies)],
                        )
                    )
        for c in copies:
            c.start()
        for c in copies:
            c.wait()

    return pl.pallas_call(
        body,
        grid_spec=pltpu.PrefetchScalarGridSpec(
            num_scalar_prefetch=1,
            grid=(1,),
            in_specs=[pl.BlockSpec(memory_space=pl.ANY)] * 2,
            out_specs=[pl.BlockSpec(memory_space=pl.ANY)] * 3,
            scratch_shapes=[pltpu.SemaphoreType.DMA((6 * len(group),))],
        ),
        out_shape=[jax.ShapeDtypeStruct((2, len(group), 256, 256), BF)] * 3,
        name="pack",
    )(where, queries, grad_out)


def project(where, pieces, weight):
    def block(n, k, s):
        return lax.rem(s[0] + N - k, N) * N + lax.rem(s[1] + N - n, N)

    def body(s, t0, t1, t2, t3, w, kv, ordered, acc):
        n, k = pl.program_id(0), pl.program_id(1)

        @pl.when((n == 0) & (k == 0))
        def _():
            acc[...] = jnp.zeros_like(acc)

        for i, t in enumerate((t0, t1, t2, t3)):

            @pl.when(n == i)
            def _(t=t):
                ordered[...] = t[...]
                for e in range(2):
                    acc[e] += dot(t[0, e], w[0, e], ((1,), (0,)))

        @pl.when((n == N - 1) & (k == N - 1))
        def _():
            kv[...] = acc[...].astype(BF)

    return pl.pallas_call(
        body,
        grid_spec=pltpu.PrefetchScalarGridSpec(
            num_scalar_prefetch=1,
            grid=(N, N),
            in_specs=[pl.BlockSpec((1, 2, 128, 128), lambda n, k, s: (k, 0, 0, 0))] * 4
            + [pl.BlockSpec((1, 2, 128, 512), lambda n, k, s: (block(n, k, s), 0, 0, 0))],
            out_specs=[
                pl.BlockSpec((2, 128, 512), lambda n, k, s: (0, 0, 0)),
                pl.BlockSpec((1, 2, 128, 128), lambda n, k, s: (block(n, k, s), 0, 0, 0)),
            ],
            scratch_shapes=[pltpu.VMEM((2, 128, 512), F32)],
        ),
        out_shape=[
            jax.ShapeDtypeStruct((2, 128, 512), BF),
            jax.ShapeDtypeStruct((16, 2, 128, 128), BF),
        ],
        cost_estimate=pl.CostEstimate(
            flops=2 * 256 * 2048 * 512, bytes_accessed=6 << 20, transcendentals=0
        ),
        name="project",
    )(where, *pieces, weight)


def attend(group, where, queries, grad_out, moved, kvs):
    count = len(group)
    scale = 1.0 / math.sqrt(HEAD)

    def body(s, *refs):
        own_q, own_g = refs[:count], refs[count : 2 * count]
        sent = refs[2 * count : 2 * count + 3]
        kv = refs[2 * count + 3 : 3 * count + 3]
        outs = refs[3 * count + 3 : 3 * count + 7]
        grads = refs[3 * count + 7 :]
        row = lax.broadcasted_iota(jnp.int32, (256, 256), 0)
        valid = row < jnp.where(row < 128, s[2], s[3] + 128)
        for n in range(count):
            key, value = kv[n][:, :HEAD], kv[n][:, HEAD:]
            grad_key = grad_value = None
            for k in range(N):
                if k == 0:
                    q, g = own_q[n][...], own_g[n][...]
                else:
                    q, g = sent[k - 1][0, n], sent[k - 1][1, n]
                scores = dot(key, q, ((1,), (1,))) * scale
                scores = jnp.where(valid, scores, -1e30)
                weights = jnp.exp(scores - jnp.max(scores, axis=0, keepdims=True))
                probs = weights * (1.0 / jnp.sum(weights, axis=0, keepdims=True))
                low = probs.astype(BF)
                outs[k][0, n] = dot(low, value, ((0,), (0,))).astype(BF)
                grad_probs = dot(value, g, ((1,), (1,)))
                delta = jnp.sum(probs * grad_probs, axis=0, keepdims=True)
                grad_scores = (probs * (grad_probs - delta) * scale).astype(BF)
                outs[k][1, n] = dot(grad_scores, key, ((0,), (0,))).astype(BF)
                dk = dot(grad_scores, q, ((1,), (0,)))
                dv = dot(low, g, ((1,), (0,)))
                grad_key = dk if k == 0 else grad_key + dk
                grad_value = dv if k == 0 else grad_value + dv
            grads[n][:, :HEAD] = grad_key.astype(grads[n].dtype)
            grads[n][:, HEAD:] = grad_value.astype(grads[n].dtype)

    def own(m):
        return pl.BlockSpec(
            (256, HEAD), lambda l, s: (0, s[0] * 8 + lax.rem(s[1] + N - m, N) * 2 + l)
        )

    by_head = pl.BlockSpec((2, count, 256, HEAD), lambda l, s: (0, 0, 0, l))
    return pl.pallas_call(
        body,
        grid_spec=pltpu.PrefetchScalarGridSpec(
            num_scalar_prefetch=1,
            grid=(2,),
            in_specs=[own(m) for m in group] * 2
            + [by_head] * 3
            + [pl.BlockSpec((256, 256), lambda l, s: (0, l))] * count,
            out_specs=[by_head] * 4 + [pl.BlockSpec((256, 256), lambda l, s: (0, l))] * count,
        ),
        out_shape=[jax.ShapeDtypeStruct((2, count, 256, 256), BF)] * 4
        + [jax.ShapeDtypeStruct((256, 512), BF if m else F32) for m in group],
        cost_estimate=pl.CostEstimate(
            flops=12 * count * 2 * 1024 * 256 * 128,
            bytes_accessed=count * (4 << 20),
            transcendentals=count * 2 * 1024 * 256,
        ),
        compiler_params=pltpu.CompilerParams(vmem_limit_bytes=48 << 20),
        name="attend",
    )(where, *([queries] * count), *([grad_out] * count), *moved, *kvs)


def place(group, where, pieces, before):
    def body(s, p0, p1, p2, p3, *rest):
        outs, sem = rest[-3:-1], rest[-1]
        copies = []
        for k, p in enumerate((p0, p1, p2, p3)):
            for a in range(2):
                for n, m in enumerate(group):
                    col = pl.multiple_of(
                        lax.rem(s[0] + k, N) * 1024 + lax.rem(s[1] + N - m, N) * 256, 256
                    )
                    copies.append(
                        pltpu.make_async_copy(
                            p.at[a, n], outs[a].at[:, pl.ds(col, 256)], sem.at[len(copies)]
                        )
                    )
        for c in copies:
            c.start()
        for c in copies:
            c.wait()

    extra = [] if before is None else list(before)
    return pl.pallas_call(
        body,
        grid_spec=pltpu.PrefetchScalarGridSpec(
            num_scalar_prefetch=1,
            grid=(1,),
            in_specs=[pl.BlockSpec(memory_space=pl.ANY)] * (4 + len(extra)),
            out_specs=[pl.BlockSpec(memory_space=pl.ANY)] * 2,
            scratch_shapes=[pltpu.SemaphoreType.DMA((8 * len(group),))],
        ),
        out_shape=[jax.ShapeDtypeStruct((256, 4096), BF)] * 2,
        input_output_aliases={5: 0, 6: 1} if extra else {},
        name="place",
    )(where, *pieces, *extra)


def per_device(text, src, lengths, kv_weight, queries, grad_out):
    group = lax.axis_index("dp")
    ctx = lax.axis_index("ctx")
    sample = lax.dynamic_index_in_dim(src, group, 0, keepdims=False)
    limits = lax.dynamic_index_in_dim(lengths, sample, 0, keepdims=False)
    where = jnp.stack([ctx // N, ctx % N, limits[0], limits[1]]).astype(jnp.int32)
    q, g = queries[0], grad_out[0]

    everyone = lax.all_gather(text[0], "dp", axis=0)
    weight = lax.all_gather(jnp.swapaxes(kv_weight, 0, 1), "dp", axis=0)
    picked = lax.dynamic_index_in_dim(everyone, sample, 0, keepdims=False)
    along_x = jnp.stack([picked] + [x_shift(picked, k) for k in (1, 2, 3)])
    pieces = [along_x] + [z_shift(along_x, n) for n in (1, 2, 3)]

    moved = {}
    for ms in GROUPS:
        sends = pack(ms, where, q, g)
        moved[ms] = [x_shift(a, k + 1) for k, a in enumerate(sends)]

    kv, ordered = project(where, pieces, weight)
    kv = kv.reshape(256, 512)
    kvs = [kv] + [z_shift(kv, m) for m in (1, 2, 3)]
    own_rows = lax.all_to_all(ordered, "dp", split_axis=0, concat_axis=0, tiled=True)

    grads = [None] * N
    out = None
    for ms in GROUPS:
        res = attend(ms, where, q, g, moved[ms], [kvs[m] for m in ms])
        back = [res[0]] + [x_shift(res[k], N - k) for k in (1, 2, 3)]
        for m, d in zip(ms, res[4:]):
            grads[m] = d if m == 0 else z_shift(d, N - m)
        out = place(ms, where, back, out)

    total = grads[0] + sum(grads[m].astype(F32) for m in (1, 2, 3))
    every_grad = lax.all_gather(total.astype(BF).reshape(2, 128, 512), "dp", axis=0)
    grad_weight = jnp.einsum(
        "betf,betc->fec", own_rows, every_grad, preferred_element_type=F32
    )
    return (out[0][None], out[1][None], grad_weight)


def solution(mesh):
    placed = (
        P("dp", None, None, "ctx"),
        P(),
        P(),
        P("dp", None, "ctx"),
        P("dp", "ctx", None),
        P("dp", "ctx", None),
    )
    return jax.shard_map(
        per_device,
        mesh=mesh,
        in_specs=placed,
        out_specs=(P("dp", "ctx", None), P("dp", "ctx", None), P("dp", None, "ctx")),
        check_vma=False,
    )
```

time: 415 us -> 415 us (level)
  Pallas kernels: 0 us -> 261 us
  waiting for transfers between devices: 182 us -> 48.9 us
  local copies, waits for them, and re-layouts: 80.4 us -> 13.5 us
  matrix products: 59.5 us -> 3.72 us
  other arithmetic: 15.7 us -> 2.04 us
  starting transfers between devices: 55.1 us -> 65.9 us
    pallas_call x0 -> x7, Pallas kernels: none -> 261 us  [the longest x2 131 us: place(): pl.pallas_call(body, grid_spec=pltpu.PrefetchScalarGridSpec(num_scalar_pr...]
    all_to_all x5 -> x1, waiting for transfers between devices: 147 us -> 0.01 us  [per_device(): lax.all_to_all(ordered, 'dp', split_axis=0, concat_axis=0, tiled=True)]
    dot_general x6 -> x0, matrix products: 47.5 us -> none  [the longest x1 15.4 us: attend(): jnp.einsum('bhlj,blhd->bjhd', grad_scores, q_rows, preferred_element_type...]
    ppermute x0 -> x24, waiting for transfers between devices: none -> 47.3 us  [the longest x15 27.8 us: x_shift(): lax.ppermute(a, 'ctx', [(4 * x + z, 4 * ((x + k) % N) + z) for x in range...]
    ppermute x0 -> x24, starting transfers between devices: none -> 42.7 us  [the longest x9 22.4 us: z_shift(): lax.ppermute(a, 'ctx', [(4 * x + z, 4 * x + (z + m) % N) for x in range(N...]
    all_gather x2 -> x3, waiting for transfers between devices: 35.8 us -> 0.93 us  [the longest x1 0.91 us: per_device(): everyone = lax.all_gather(text[0], 'dp', axis=0)]
    all_to_all x5 -> x1, starting transfers between devices: 55.1 us -> 23.1 us  [per_device(): lax.all_to_all(ordered, 'dp', split_axis=0, concat_axis=0, tiled=True)]
    split x6 -> x0, local copies, waits for them, and re-layouts: 22.6 us -> none  [in_one_piece(): jnp.split(lax.all_to_all(both, axis, split_axis=split_dim, concat_axis=co...]
  transfers between devices with their start and end apart: 7 -> 28, of which waited for: 5 -> 9; matrix products, arithmetic and copies ran while one was open for 32% -> 2% of each run, Pallas kernels for 0% -> 63%
where the time goes in v1:
time: 415 us; the launch traced here: 411 us
  Pallas kernels  261 us (63%)
  starting transfers between devices  65.9 us (16%)
  waiting for transfers between devices  48.9 us (12%)
  between operations  16 us (4%)
  local copies, waits for them, and re-layouts  13.5 us (3%)
    pallas_call x2, Pallas kernels, place(): pl.pallas_call(body, grid_spec=pltpu.PrefetchScalarGridSpec(num_scalar_pr...  131 us
    pallas_call x2, Pallas kernels, pack(): pl.pallas_call(body, grid_spec=pltpu.PrefetchScalarGridSpec(num_scalar_pr...  99 us
    ppermute x15, waiting for transfers between devices, x_shift(): lax.ppermute(a, 'ctx', [(4 * x + z, 4 * ((x + k) % N) + z) for x in range...  27.8 us
    all_to_all x1, starting transfers between devices, per_device(): lax.all_to_all(ordered, 'dp', split_axis=0, concat_axis=0, tiled=True)  23.1 us
    ppermute x9, starting transfers between devices, z_shift(): lax.ppermute(a, 'ctx', [(4 * x + z, 4 * x + (z + m) % N) for x in range(N...  22.4 us
    ppermute x15, starting transfers between devices, x_shift(): lax.ppermute(a, 'ctx', [(4 * x + z, 4 * ((x + k) % N) + z) for x in range...  20.3 us
    ppermute x9, waiting for transfers between devices, z_shift(): lax.ppermute(a, 'ctx', [(4 * x + z, 4 * x + (z + m) % N) for x in range(N...  19.5 us
    pallas_call x2, Pallas kernels, attend(): pl.pallas_call(body, grid_spec=pltpu.PrefetchScalarGridSpec(num_scalar_pr...  17.7 us
  transfers between devices with their start and end apart: 28, of which 9 were waited for; matrix products, arithmetic and copies ran while one was open for 2% of the time, Pallas kernels for 63%

profile of v1, /device:TPU:11, one launch (start us, length us, event | category | flops | bytes accessed | tf_op | source)
XLA Modules:
  0.0 410.9 jit_solution(1206599436905201232)
XLA Ops:
  8.0 1.7 copy.23
  9.7 1.2 dynamic_slice.12
  13.5 1.9 pad_add_fusion.s
  15.4 49.5 %pack.3 = (bf16[2,2,256,256]{3,2,1,0:T(8,128)(2,1)}, bf16[2,2,256,256]{3,2,1,0:T(8,128)(2,1)}, bf16[2,2,256,256]{3,2,1,0:T(8,128)(2,1)}) custom-call(s32[4]{0:T(128)} %pad_add_fusion.s, bf16[256,4096]{1,0:T(8,128)(2,1)} %bitcast.30, bf16[256,4096]{1,0:T(8,128)(2,1)} %bitcast.36), custom_call_target="tpu_custom_call" | custom-call | tf_op jit(solution)/shard_map/pack/pallas_call | solution.py:55
  64.9 1.3 collective-permute-start.14
  66.2 0.9 all-gather.5.cloned.1.call-done
  67.1 0.8 fusion.3
  68.2 2.1 collective-permute-start.4
  70.4 1.5 collective-permute-start.3
  71.9 0.8 constant_dynamic-slice_fusion
  73.3 7.3 %collective-permute-done.3 = bf16[2,128,128]{2,1,0:T(8,128)(2,1)S(1)} collective-permute-done((bf16[2,128,128]{2,1,0:T(8,128)(2,1)S(1)}, bf16[2,128,128]{2,1,0:T(8,128)(2,1)S(1)}, u32[]{:S(2)}, u32[]{:S(2)}) %collective-permute-start.3) | collective-permute-done | bytes 65568 | tf_op jit(solution)/shard_map/ppermute | solution.py:18
  80.6 6.1 %collective-permute-start.8 = (bf16[4,2,128,128]{3,2,1,0:T(8,128)(2,1)S(1)}, bf16[4,2,128,128]{3,2,1,0:T(8,128)(2,1)S(1)}, u32[]{:S(2)}, u32[]{:S(2)}) collective-permute-start(bf16[4,2,128,128]{3,2,1,0:T(8,128)(2,1)S(1)} %pad_maximum_fusion.t0), channel_id=1, source_target_pairs={{0,3},{1,0},{2,1},{3,2},{4,7},{5,4},{6,5},{7,6},{8,11},{9,8},{10,9... | collective-permute-start | bytes 786440 | tf_op jit(solution)/shard_map/ppermute | solution.py:24
  86.7 1.8 collective-permute-start.15
  88.5 1.0 collective-permute-start.7
  89.5 2.3 collective-permute-start.6
  91.8 5.9 %collective-permute-done.8.t3 = bf16[4,2,128,128]{3,2,1,0:T(8,128)(2,1)S(1)} collective-permute-done((bf16[4,2,128,128]{3,2,1,0:T(8,128)(2,1)S(1)}, bf16[4,2,128,128]{3,2,1,0:T(8,128)(2,1)S(1)}, u32[]{:S(2)}, u32[]{:S(2)}) %collective-permute-start.8) | collective-permute-done | bytes 262176 | tf_op jit(solution)/shard_map/ppermute | solution.py:24
  97.7 1.1 collective-permute-start.16
  98.7 49.5 %pack.2 = (bf16[2,2,256,256]{3,2,1,0:T(8,128)(2,1)}, bf16[2,2,256,256]{3,2,1,0:T(8,128)(2,1)}, bf16[2,2,256,256]{3,2,1,0:T(8,128)(2,1)}) custom-call(s32[4]{0:T(128)} %pad_add_fusion.s, bf16[256,4096]{1,0:T(8,128)(2,1)} %bitcast.31, bf16[256,4096]{1,0:T(8,128)(2,1)} %bitcast.37), custom_call_target="tpu_custom_call" | custom-call | tf_op jit(solution)/shard_map/pack/pallas_call | solution.py:55
  149.5 3.1 collective-permute-start.1
  152.6 13.2 %project.1 = (bf16[2,128,512]{2,1,0:T(8,128)(2,1)}, bf16[16,2,128,128]{3,2,1,0:T(8,128)(2,1)}) custom-call(s32[4]{0:T(128)} %pad_add_fusion.s, bf16[4,2,128,128]{3,2,1,0:T(8,128)(2,1)} %copy-done.11, bf16[4,2,128,128]{3,2,1,0:T(8,128)(2,1)} %copy-done.18, bf16[4,2,128,128]{3,2,1,0:T(8,128)(2,1)} %copy-done.17, bf16[4,2,128,128]{3,2,1,0:T(8,128)(2,1)} %copy-done.16, ...), custom_call_target="tpu_custom_call" | custom-call | flops 536870912 | bytes 6291456 | tf_op jit(solution)/shard_map/project/pallas_call | solution.py:92
  165.9 4.2 %collective-permute-start.17 = (bf16[256,512]{1,0:T(8,128)(2,1)}, bf16[256,512]{1,0:T(8,128)(2,1)S(1)}, u32[]{:S(2)}, u32[]{:S(2)}) collective-permute-start(bf16[256,512]{1,0:T(8,128)(2,1)} %bitcast.26), channel_id=1, source_target_pairs={{0,1},{1,2},{2,3},{3,0},{4,5},{5,6},{6,7},{7,4},{8,9},{9,10},{10,1... | collective-permute-start | bytes 786440 | tf_op jit(solution)/shard_map/ppermute | solution.py:24
  170.1 2.6 collective-permute-start.10
  172.7 3.9 collective-permute-done.17.refs_8_
  177.2 1.0 copy-done.3
  178.1 8.8 %attend.3 = (bf16[2,2,256,256]{3,2,1,0:T(8,128)(2,1)S(1)}, bf16[2,2,256,256]{3,2,1,0:T(8,128)(2,1)S(1)}, bf16[2,2,256,256]{3,2,1,0:T(8,128)(2,1)S(1)}, bf16[2,2,...) custom-call(s32[4]{0:T(128)S(1)} %copy-done.4, bf16[256,4096]{1,0:T(8,128)(2,1)} %bitcast.32, ...), custom_call_target="tpu_custom_call" | custom-call | flops 1610612736 | bytes 8388608 | tf_op jit(solution)/shard_map/attend/pallas_call | solution.py:159
  187.0 0.8 copy-done.1
  187.8 0.8 copy-done.7
  188.6 3.3 collective-permute-start.21
  191.9 8.8 %attend.2 = (bf16[2,2,256,256]{3,2,1,0:T(8,128)(2,1)S(1)}, bf16[2,2,256,256]{3,2,1,0:T(8,128)(2,1)S(1)}, bf16[2,2,256,256]{3,2,1,0:T(8,128)(2,1)S(1)}, bf16[2,2,...) custom-call(s32[4]{0:T(128)S(1)} %copy-done.4, ...), custom_call_target="tpu_custom_call" | custom-call | flops 1610612736 | bytes 8388608 | tf_op jit(solution)/shard_map/attend/pallas_call | solution.py:159
  201.5 0.8 copy-done.9
  202.3 1.8 collective-permute-start.22
  204.7 9.7 %collective-permute-done.22 = bf16[256,512]{1,0:T(8,128)(2,1)S(1)} collective-permute-done((bf16[256,512]{1,0:T(8,128)(2,1)S(1)}, bf16[256,512]{1,0:T(8,128)(2,1)S(1)}, u32[]{:S(2)}, u32[]{:S(2)}) %collective-permute-start.22) | collective-permute-done | bytes 262176 | tf_op jit(solution)/shard_map/ppermute | solution.py:24
  214.6 0.9 copy.16
  215.4 23.1 %all-to-all-start = ((bf16[16,2,128,128]{3,2,1,0:T(8,128)(2,1)}), bf16[16,2,128,128]{3,2,1,0:T(8,128)(2,1)}, u32[]{:S(2)}, u32[]{:S(2)}) async-start(bf16[16,2,128,128]{3,2,1,0:T(8,128)(2,1)} %get-tuple-element.50), calls=%async_computation | async-start | bytes 2097152 | tf_op jit(solution)/shard_map/all_to_all | solution.py:239
  238.5 2.9 collective-permute-start.18
  241.5 1.8 collective-permute-start.19
  243.4 1.3 collective-permute-start.11
  244.8 1.2 collective-permute-start.12
  245.9 8.3 %collective-permute-done.18.p1 = bf16[2,2,256,256]{3,2,1,0:T(8,128)(2,1)S(1)} collective-permute-done((bf16[2,2,256,256]{3,2,1,0:T(8,128)(2,1)S(1)}, bf16[2,2,256,256]{3,2,1,0:T(8,128)(2,1)S(1)}, u32[]{:S(2)}, u32[]{:S(2)}) %collective-permute-start.18) | collective-permute-done | bytes 524320 | tf_op jit(solution)/shard_map/ppermute | solution.py:18
  254.2 1.1 collective-permute-start.13
  255.4 10.9 %collective-permute-done.19.p2 = bf16[2,2,256,256]{3,2,1,0:T(8,128)(2,1)S(1)} collective-permute-done((bf16[2,2,256,256]{3,2,1,0:T(8,128)(2,1)S(1)}, bf16[2,2,256,256]{3,2,1,0:T(8,128)(2,1)S(1)}, u32[]{:S(2)}, u32[]{:S(2)}) %collective-permute-start.19) | collective-permute-done | bytes 524320 | tf_op jit(solution)/shard_map/ppermute | solution.py:18
  266.2 0.8 collective-permute-done.20.p3
  267.1 0.8 copy-done.15
  267.9 65.4 %place.2 = (bf16[256,4096]{1,0:T(8,128)(2,1)}, bf16[256,4096]{1,0:T(8,128)(2,1)}) custom-call(s32[4]{0:T(128)} %pad_add_fusion.s, bf16[2,2,256,256]{3,2,1,0:T(8,128)(2,1)} %copy-done.1, bf16[2,2,256,256]{3,2,1,0:T(8,128)(2,1)} %copy-done.12, bf16[2,2,256,256]{3,2,1,0:T(8,128)(2,1)} %copy-done.14, bf16[2,2,256,256]{3,2,1,0:T(8,128)(2,1)} %copy-done.15), custom_call_target="tpu_custom_call" | custom-call | tf_op jit(solution)/shard_map/place/pallas_call | solution.py:202
  333.3 0.8 copy-done.13
  334.1 65.4 %place.3 = (bf16[256,4096]{1,0:T(8,128)(2,1)}, bf16[256,4096]{1,0:T(8,128)(2,1)}) custom-call(s32[4]{0:T(128)} %pad_add_fusion.s, bf16[2,2,256,256]{3,2,1,0:T(8,128)(2,1)} %copy-done.2, bf16[2,2,256,256]{3,2,1,0:T(8,128)(2,1)} %collective-permute-done.11.p1, ...), custom_call_target="tpu_custom_call", output_to_operand_aliasing={{0}: (5, {}), {1}: (6, {})} | custom-call | tf_op jit(solution)/shard_map/place/pallas_call | solution.py:202
  399.6 3.7 convolution_bitcast_fusion
  403.4 1.0 copy.18
  (68 shorter events, 5.9 us)
Async XLA Ops:
  7.2 5.8 %copy-start = (s32[16,2]{0,1:T(2,128)S(1)}, s32[16,2]{0,1:T(2,128)}, u32[]{:S(2)}) copy-start(s32[16,2]{0,1:T(2,128)} %param.8) | copy-start | bytes 388
  7.2 60.0 %all-gather.5.cloned.1.call-start = ((), (), s32[]{:S(2)}) async-start(), calls=%async_computation.1 | async-start | bytes 1114112 | tf_op jit(solution)/shard_map/all_gather | solution.py:225
  7.9 144.7 %all-gather.9.cloned.1.call-start = ((), (), s32[]{:S(2)}) async-start(), calls=%async_computation.3 | async-start | bytes 4456448 | tf_op jit(solution)/shard_map/all_gather | solution.py:226
  9.7 390.0 %all-gather.7.cloned.1.call-start = ((), (), s32[]{:S(2)}) async-start(), calls=%async_computation.2 | async-start | bytes 4456448 | tf_op jit(solution)/shard_map/all_gather | solution.py:251
  64.9 100.8 %collective-permute-start.14 = (bf16[2,2,256,256]{3,2,1,0:T(8,128)(2,1)}, bf16[2,2,256,256]{3,2,1,0:T(8,128)(2,1)S(1)}, u32[]{:S(2)}, u32[]{:S(2)}) collective-permute-start(bf16[2,2,256,256]{3,2,1,0:T(8,128)(2,1)} %get-tuple-element.35), channel_id=1, source_target_pairs={{0,4},{1,5},{2,6},{3,7},{4,8},{5,9},{6,10},{7,11},{8,12},{9,13},{1... | collective-permute-start | bytes 1572872 | tf_op jit(solution)/shard_map/ppermute | solution.py:18
  68.0 4.8 %collective-permute-start.5 = (bf16[2,128,128]{2,1,0:T(8,128)(2,1)S(1)}, bf16[2,128,128]{2,1,0:T(8,128)(2,1)S(1)}, u32[]{:S(2)}, u32[]{:S(2)}) collective-permute-start(bf16[2,128,128]{2,1,0:T(8,128)(2,1)S(1)} %fusion.3), channel_id=1, source_target_pairs={{0,12},{1,13},{2,14},{3,15},{4,0},{5,1},{6,2},{7,3},{8,4},{9,5},{1... | collective-permute-start | bytes 196616 | tf_op jit(solution)/shard_map/ppermute | solution.py:18
  68.2 5.0 %collective-permute-start.4 = (bf16[2,128,128]{2,1,0:T(8,128)(2,1)S(1)}, bf16[2,128,128]{2,1,0:T(8,128)(2,1)S(1)}, u32[]{:S(2)}, u32[]{:S(2)}) collective-permute-start(bf16[2,128,128]{2,1,0:T(8,128)(2,1)S(1)} %fusion.3), channel_id=1, source_target_pairs={{0,8},{1,9},{2,10},{3,11},{4,12},{5,13},{6,14},{7,15},{8,0},{9,1},... | collective-permute-start | bytes 196616 | tf_op jit(solution)/shard_map/ppermute | solution.py:18
  70.4 10.2 %collective-permute-start.3 = (bf16[2,128,128]{2,1,0:T(8,128)(2,1)S(1)}, bf16[2,128,128]{2,1,0:T(8,128)(2,1)S(1)}, u32[]{:S(2)}, u32[]{:S(2)}) collective-permute-start(bf16[2,128,128]{2,1,0:T(8,128)(2,1)S(1)} %fusion.3), channel_id=1, source_target_pairs={{0,4},{1,5},{2,6},{3,7},{4,8},{5,9},{6,10},{7,11},{8,12},{9,13},{1... | collective-permute-start | bytes 196616 | tf_op jit(solution)/shard_map/ppermute | solution.py:18
  80.6 67.7 %copy-start.11 = (bf16[4,2,128,128]{3,2,1,0:T(8,128)(2,1)}, bf16[4,2,128,128]{3,2,1,0:T(8,128)(2,1)S(1)}, u32[]{:S(2)}) copy-start(bf16[4,2,128,128]{3,2,1,0:T(8,128)(2,1)S(1)} %pad_maximum_fusion.t0) | copy-start | bytes 786436
  80.6 17.1 %collective-permute-start.8 = (bf16[4,2,128,128]{3,2,1,0:T(8,128)(2,1)S(1)}, bf16[4,2,128,128]{3,2,1,0:T(8,128)(2,1)S(1)}, u32[]{:S(2)}, u32[]{:S(2)}) collective-permute-start(bf16[4,2,128,128]{3,2,1,0:T(8,128)(2,1)S(1)} %pad_maximum_fusion.t0), channel_id=1, source_target_pairs={{0,3},{1,0},{2,1},{3,2},{4,7},{5,4},{6,5},{7,6},{8,11},{9,8},{10,9... | collective-permute-start | bytes 786440 | tf_op jit(solution)/shard_map/ppermute | solution.py:24
  86.7 79.2 %collective-permute-start.15 = (bf16[2,2,256,256]{3,2,1,0:T(8,128)(2,1)}, bf16[2,2,256,256]{3,2,1,0:T(8,128)(2,1)S(1)}, u32[]{:S(2)}, u32[]{:S(2)}) collective-permute-start(bf16[2,2,256,256]{3,2,1,0:T(8,128)(2,1)} %get-tuple-element.36), channel_id=1, source_target_pairs={{0,8},{1,9},{2,10},{3,11},{4,12},{5,13},{6,14},{7,15},{8,0},{9,1},... | collective-permute-start | bytes 1572872 | tf_op jit(solution)/shard_map/ppermute | solution.py:18
  88.5 59.8 %collective-permute-start.7 = (bf16[4,2,128,128]{3,2,1,0:T(8,128)(2,1)S(1)}, bf16[4,2,128,128]{3,2,1,0:T(8,128)(2,1)S(1)}, u32[]{:S(2)}, u32[]{:S(2)}) collective-permute-start(bf16[4,2,128,128]{3,2,1,0:T(8,128)(2,1)S(1)} %pad_maximum_fusion.t0), channel_id=1, source_target_pairs={{0,2},{1,3},{2,0},{3,1},{4,6},{5,7},{6,4},{7,5},{8,10},{9,11},{10,... | collective-permute-start | bytes 786440 | tf_op jit(solution)/shard_map/ppermute | solution.py:24
  89.5 59.3 %collective-permute-start.6 = (bf16[4,2,128,128]{3,2,1,0:T(8,128)(2,1)S(1)}, bf16[4,2,128,128]{3,2,1,0:T(8,128)(2,1)S(1)}, u32[]{:S(2)}, u32[]{:S(2)}) collective-permute-start(bf16[4,2,128,128]{3,2,1,0:T(8,128)(2,1)S(1)} %pad_maximum_fusion.t0), channel_id=1, source_target_pairs={{0,1},{1,2},{2,3},{3,0},{4,5},{5,6},{6,7},{7,4},{8,9},{9,10},{10,1... | collective-permute-start | bytes 786440 | tf_op jit(solution)/shard_map/ppermute | solution.py:24
  97.7 50.6 %copy-start.16 = (bf16[4,2,128,128]{3,2,1,0:T(8,128)(2,1)}, bf16[4,2,128,128]{3,2,1,0:T(8,128)(2,1)S(1)}, u32[]{:S(2)}) copy-start(bf16[4,2,128,128]{3,2,1,0:T(8,128)(2,1)S(1)} %collective-permute-done.8.t3) | copy-start | bytes 786436
  97.7 72.4 %collective-permute-start.16 = (bf16[2,2,256,256]{3,2,1,0:T(8,128)(2,1)}, bf16[2,2,256,256]{3,2,1,0:T(8,128)(2,1)S(1)}, u32[]{:S(2)}, u32[]{:S(2)}) collective-permute-start(bf16[2,2,256,256]{3,2,1,0:T(8,128)(2,1)} %get-tuple-element.37), channel_id=1, source_target_pairs={{0,12},{1,13},{2,14},{3,15},{4,0},{5,1},{6,2},{7,3},{8,4},{9,5},{1... | collective-permute-start | bytes 1572872 | tf_op jit(solution)/shard_map/ppermute | solution.py:18
  148.3 4.3 %copy-start.17 = (bf16[4,2,128,128]{3,2,1,0:T(8,128)(2,1)}, bf16[4,2,128,128]{3,2,1,0:T(8,128)(2,1)S(1)}, u32[]{:S(2)}) copy-start(bf16[4,2,128,128]{3,2,1,0:T(8,128)(2,1)S(1)} %collective-permute-done.7.t2) | copy-start | bytes 786436
  148.3 40.3 %collective-permute-start = (bf16[2,2,256,256]{3,2,1,0:T(8,128)(2,1)}, bf16[2,2,256,256]{3,2,1,0:T(8,128)(2,1)S(1)}, u32[]{:S(2)}, u32[]{:S(2)}) collective-permute-start(bf16[2,2,256,256]{3,2,1,0:T(8,128)(2,1)} %get-tuple-element.27), channel_id=1, source_target_pairs={{0,4},{1,5},{2,6},{3,7},{4,8},{5,9},{6,10},{7,11},{8,12},{9,13},{1... | collective-permute-start | bytes 1572872 | tf_op jit(solution)/shard_map/ppermute | solution.py:18
  148.8 0.7 copy-start.18
  149.5 42.4 %collective-permute-start.1 = (bf16[2,2,256,256]{3,2,1,0:T(8,128)(2,1)}, bf16[2,2,256,256]{3,2,1,0:T(8,128)(2,1)S(1)}, u32[]{:S(2)}, u32[]{:S(2)}) collective-permute-start(bf16[2,2,256,256]{3,2,1,0:T(8,128)(2,1)} %get-tuple-element.28), channel_id=1, source_target_pairs={{0,8},{1,9},{2,10},{3,11},{4,12},{5,13},{6,14},{7,15},{8,0},{9,1},... | collective-permute-start | bytes 1572872 | tf_op jit(solution)/shard_map/ppermute | solution.py:18
  152.6 24.6 %copy-start.4 = (s32[4]{0:T(128)S(1)}, s32[4]{0:T(128)}, u32[]{:S(2)}) copy-start(s32[4]{0:T(128)} %pad_add_fusion.s) | copy-start | bytes 52
  165.8 26.1 %collective-permute-start.2 = (bf16[2,2,256,256]{3,2,1,0:T(8,128)(2,1)}, bf16[2,2,256,256]{3,2,1,0:T(8,128)(2,1)S(1)}, u32[]{:S(2)}, u32[]{:S(2)}) collective-permute-start(bf16[2,2,256,256]{3,2,1,0:T(8,128)(2,1)} %get-tuple-element.29), channel_id=1, source_target_pairs={{0,12},{1,13},{2,14},{3,15},{4,0},{5,1},{6,2},{7,3},{8,4},{9,5},{1... | collective-permute-start | bytes 1572872 | tf_op jit(solution)/shard_map/ppermute | solution.py:18
  165.9 10.7 %collective-permute-start.17 = (bf16[256,512]{1,0:T(8,128)(2,1)}, bf16[256,512]{1,0:T(8,128)(2,1)S(1)}, u32[]{:S(2)}, u32[]{:S(2)}) collective-permute-start(bf16[256,512]{1,0:T(8,128)(2,1)} %bitcast.26), channel_id=1, source_target_pairs={{0,1},{1,2},{2,3},{3,0},{4,5},{5,6},{6,7},{7,4},{8,9},{9,10},{10,1... | collective-permute-start | bytes 786440 | tf_op jit(solution)/shard_map/ppermute | solution.py:24
  170.1 21.8 %collective-permute-start.10 = (bf16[256,512]{1,0:T(8,128)(2,1)}, bf16[256,512]{1,0:T(8,128)(2,1)S(1)}, u32[]{:S(2)}, u32[]{:S(2)}) collective-permute-start(bf16[256,512]{1,0:T(8,128)(2,1)} %bitcast.27), channel_id=1, source_target_pairs={{0,2},{1,3},{2,0},{3,1},{4,6},{5,7},{6,4},{7,5},{8,10},{9,11},{10,... | collective-permute-start | bytes 786440 | tf_op jit(solution)/shard_map/ppermute | solution.py:24
  176.6 15.3 %collective-permute-start.9 = (bf16[256,512]{1,0:T(8,128)(2,1)}, bf16[256,512]{1,0:T(8,128)(2,1)S(1)}, u32[]{:S(2)}, u32[]{:S(2)}) collective-permute-start(bf16[256,512]{1,0:T(8,128)(2,1)} %bitcast.28), channel_id=1, source_target_pairs={{0,3},{1,0},{2,1},{3,2},{4,7},{5,4},{6,5},{7,6},{8,11},{9,8},{10,9... | collective-permute-start | bytes 786440 | tf_op jit(solution)/shard_map/ppermute | solution.py:24
  177.2 1.0 copy-start.3
  187.0 0.8 copy-start.1
  187.8 0.8 copy-start.7
  188.6 12.2 %copy-start.5 = (bf16[2,2,256,256]{3,2,1,0:T(8,128)(2,1)}, bf16[2,2,256,256]{3,2,1,0:T(8,128)(2,1)S(1)}, u32[]{:S(2)}) copy-start(bf16[2,2,256,256]{3,2,1,0:T(8,128)(2,1)S(1)} %get-tuple-element.40) | copy-start | bytes 1572868
  188.6 16.1 %collective-permute-start.21 = (bf16[256,512]{1,0:T(8,128)(2,1)S(1)}, bf16[256,512]{1,0:T(8,128)(2,1)S(1)}, u32[]{:S(2)}, u32[]{:S(2)}) collective-permute-start(bf16[256,512]{1,0:T(8,128)(2,1)S(1)} %get-tuple-element.47), channel_id=1, source_target_pairs={{0,3},{1,0},{2,1},{3,2},{4,7},{5,4},{6,5},{7,6},{8,11},{9,8},{10,9... | collective-permute-start | bytes 786440 | tf_op jit(solution)/shard_map/ppermute | solution.py:24
  200.7 0.8 copy-start.2
  201.5 0.8 copy-start.9
  202.3 12.0 %collective-permute-start.22 = (bf16[256,512]{1,0:T(8,128)(2,1)S(1)}, bf16[256,512]{1,0:T(8,128)(2,1)S(1)}, u32[]{:S(2)}, u32[]{:S(2)}) collective-permute-start(bf16[256,512]{1,0:T(8,128)(2,1)S(1)} %get-tuple-element.48), channel_id=1, source_target_pairs={{0,2},{1,3},{2,0},{3,1},{4,6},{5,7},{6,4},{7,5},{8,10},{9,11},{10,... | collective-permute-start | bytes 786440 | tf_op jit(solution)/shard_map/ppermute | solution.py:24
  204.2 10.3 %collective-permute-start.23 = (bf16[256,512]{1,0:T(8,128)(2,1)S(1)}, bf16[256,512]{1,0:T(8,128)(2,1)S(1)}, u32[]{:S(2)}, u32[]{:S(2)}) collective-permute-start(bf16[256,512]{1,0:T(8,128)(2,1)S(1)} %get-tuple-element.49), channel_id=1, source_target_pairs={{0,1},{1,2},{2,3},{3,0},{4,5},{5,6},{6,7},{7,4},{8,9},{9,10},{10,1... | collective-permute-start | bytes 786440 | tf_op jit(solution)/shard_map/ppermute | solution.py:24
  214.4 24.1 %copy-start.8 = (bf16[2,2,256,256]{3,2,1,0:T(8,128)(2,1)S(1)}, bf16[2,2,256,256]{3,2,1,0:T(8,128)(2,1)}, u32[]{:S(2)}) copy-start(bf16[2,2,256,256]{3,2,1,0:T(8,128)(2,1)} %copy-done.7) | copy-start | bytes 1572868
  214.4 27.1 %copy-start.6 = (bf16[2,2,256,256]{3,2,1,0:T(8,128)(2,1)S(1)}, bf16[2,2,256,256]{3,2,1,0:T(8,128)(2,1)}, u32[]{:S(2)}) copy-start(bf16[2,2,256,256]{3,2,1,0:T(8,128)(2,1)} %copy-done.5) | copy-start | bytes 1572868
  214.4 29.0 %copy-start.10 = (bf16[2,2,256,256]{3,2,1,0:T(8,128)(2,1)S(1)}, bf16[2,2,256,256]{3,2,1,0:T(8,128)(2,1)}, u32[]{:S(2)}) copy-start(bf16[2,2,256,256]{3,2,1,0:T(8,128)(2,1)} %copy-done.9) | copy-start | bytes 1572868
  215.4 184.1 %all-to-all-start = ((bf16[16,2,128,128]{3,2,1,0:T(8,128)(2,1)}), bf16[16,2,128,128]{3,2,1,0:T(8,128)(2,1)}, u32[]{:S(2)}, u32[]{:S(2)}) async-start(bf16[16,2,128,128]{3,2,1,0:T(8,128)(2,1)} %get-tuple-element.50), calls=%async_computation | async-start | bytes 2097152 | tf_op jit(solution)/shard_map/all_to_all | solution.py:239
  238.5 15.7 %collective-permute-start.18 = (bf16[2,2,256,256]{3,2,1,0:T(8,128)(2,1)S(1)}, bf16[2,2,256,256]{3,2,1,0:T(8,128)(2,1)S(1)}, u32[]{:S(2)}, u32[]{:S(2)}) collective-permute-start(bf16[2,2,256,256]{3,2,1,0:T(8,128)(2,1)S(1)} %copy-done.8), channel_id=1, source_target_pairs={{0,12},{1,13},{2,14},{3,15},{4,0},{5,1},{6,2},{7,3},{8,4},{9,5},{1... | collective-permute-start | bytes 1572872 | tf_op jit(solution)/shard_map/ppermute | solution.py:18
  241.5 24.7 %collective-permute-start.19 = (bf16[2,2,256,256]{3,2,1,0:T(8,128)(2,1)S(1)}, bf16[2,2,256,256]{3,2,1,0:T(8,128)(2,1)S(1)}, u32[]{:S(2)}, u32[]{:S(2)}) collective-permute-start(bf16[2,2,256,256]{3,2,1,0:T(8,128)(2,1)S(1)} %copy-done.6), channel_id=1, source_target_pairs={{0,8},{1,9},{2,10},{3,11},{4,12},{5,13},{6,14},{7,15},{8,0},{9,1},... | collective-permute-start | bytes 1572872 | tf_op jit(solution)/shard_map/ppermute | solution.py:18
  243.3 23.8 %collective-permute-start.20 = (bf16[2,2,256,256]{3,2,1,0:T(8,128)(2,1)S(1)}, bf16[2,2,256,256]{3,2,1,0:T(8,128)(2,1)S(1)}, u32[]{:S(2)}, u32[]{:S(2)}) collective-permute-start(bf16[2,2,256,256]{3,2,1,0:T(8,128)(2,1)S(1)} %get-tuple-element.41), channel_id=1, source_target_pairs={{0,4},{1,5},{2,6},{3,7},{4,8},{5,9},{6,10},{7,11},{8,12},{9,13},{1... | collective-permute-start | bytes 1572872 | tf_op jit(solution)/shard_map/ppermute | solution.py:18
  243.4 89.9 %collective-permute-start.11 = (bf16[2,2,256,256]{3,2,1,0:T(8,128)(2,1)S(1)}, bf16[2,2,256,256]{3,2,1,0:T(8,128)(2,1)}, u32[]{:S(2)}, u32[]{:S(2)}) collective-permute-start(bf16[2,2,256,256]{3,2,1,0:T(8,128)(2,1)S(1)} %copy-done.10), channel_id=1, source_target_pairs={{0,12},{1,13},{2,14},{3,15},{4,0},{5,1},{6,2},{7,3},{8,4},{9,5},{1... | collective-permute-start | bytes 1572872 | tf_op jit(solution)/shard_map/ppermute | solution.py:18
  244.8 88.6 %collective-permute-start.12 = (bf16[2,2,256,256]{3,2,1,0:T(8,128)(2,1)S(1)}, bf16[2,2,256,256]{3,2,1,0:T(8,128)(2,1)}, u32[]{:S(2)}, u32[]{:S(2)}) collective-permute-start(bf16[2,2,256,256]{3,2,1,0:T(8,128)(2,1)S(1)} %get-tuple-element.33), channel_id=1, source_target_pairs={{0,8},{1,9},{2,10},{3,11},{4,12},{5,13},{6,14},{7,15},{8,0},{9,1},... | collective-permute-start | bytes 1572872 | tf_op jit(solution)/shard_map/ppermute | solution.py:18
  254.2 12.9 %copy-start.12 = (bf16[2,2,256,256]{3,2,1,0:T(8,128)(2,1)}, bf16[2,2,256,256]{3,2,1,0:T(8,128)(2,1)S(1)}, u32[]{:S(2)}) copy-start(bf16[2,2,256,256]{3,2,1,0:T(8,128)(2,1)S(1)} %collective-permute-done.18.p1) | copy-start | bytes 1572868
  254.2 79.1 %collective-permute-start.13 = (bf16[2,2,256,256]{3,2,1,0:T(8,128)(2,1)S(1)}, bf16[2,2,256,256]{3,2,1,0:T(8,128)(2,1)S(1)}, u32[]{:S(2)}, u32[]{:S(2)}) collective-permute-start(bf16[2,2,256,256]{3,2,1,0:T(8,128)(2,1)S(1)} %get-tuple-element.34), channel_id=1, source_target_pairs={{0,4},{1,5},{2,6},{3,7},{4,8},{5,9},{6,10},{7,11},{8,12},{9,13},{1... | collective-permute-start | bytes 1572872 | tf_op jit(solution)/shard_map/ppermute | solution.py:18
  266.2 0.8 copy-start.14
  267.1 0.8 copy-start.15
  333.3 0.8 copy-start.13
Sparse Core Ops, SparseCore 0:
  9.9 57.2 all-gather.4
  69.0 61.7 all-gather.8
  215.6 62.8 all-gather.6

commit v2 on v1

--- a/solution.py
+++ b/solution.py
@@ -31,86 +31,154 @@
 
 
 def pack(group, where, queries, grad_out):
-    def body(s, q, g, *rest):
-        outs, sem = rest[:-1], rest[-1]
-        copies = []
-        for k in (1, 2, 3):
-            for a, src in enumerate((q, g)):
-                for n, m in enumerate(group):
-                    col = pl.multiple_of(
-                        lax.rem(s[0] + k, N) * 1024 + lax.rem(s[1] + N - m, N) * 256, 256
-                    )
-                    copies.append(
-                        pltpu.make_async_copy(
-                            src.at[:, pl.ds(col, 256)],
-                            outs[k - 1].at[a, n],
-                            sem.at[len(copies)],
-                        )
-                    )
-        for c in copies:
-            c.start()
-        for c in copies:
-            c.wait()
-
+    count = len(group)
+
+    def body(s, *refs):
+        ins, outs = refs[: 6 * count], refs[6 * count :]
+        for k in range(3):
+            for n in range(count):
+                for a in range(2):
+                    outs[k][a, n] = ins[(k * count + n) * 2 + a][...]
+
+    def columns(k, m):
+        return pl.BlockSpec(
+            (256, 256), lambda i, s: (0, lax.rem(s[0] + k, N) * 4 + lax.rem(s[1] + N - m, N))
+        )
+
+    whole = pl.BlockSpec((2, count, 256, 256), lambda i, s: (0, 0, 0, 0))
     return pl.pallas_call(
         body,
         grid_spec=pltpu.PrefetchScalarGridSpec(
             num_scalar_prefetch=1,
             grid=(1,),
-            in_specs=[pl.BlockSpec(memory_space=pl.ANY)] * 2,
-            out_specs=[pl.BlockSpec(memory_space=pl.ANY)] * 3,
-            scratch_shapes=[pltpu.SemaphoreType.DMA((6 * len(group),))],
-        ),
-        out_shape=[jax.ShapeDtypeStruct((2, len(group), 256, 256), BF)] * 3,
+            in_specs=[columns(k, m) for k in (1, 2, 3) for m in group for _ in range(2)],
+            out_specs=[whole] * 3,
+        ),
+        out_shape=[jax.ShapeDtypeStruct((2, count, 256, 256), BF)] * 3,
+        cost_estimate=pl.CostEstimate(
+            flops=0, bytes_accessed=count * (3 << 20) // 2, transcendentals=0
+        ),
+        compiler_params=pltpu.CompilerParams(vmem_limit_bytes=32 << 20),
         name="pack",
-    )(where, queries, grad_out)
+    )(where, *([queries, grad_out] * (3 * count)))
 
 
 def project(where, pieces, weight):
-    def block(n, k, s):
-        return lax.rem(s[0] + N - k, N) * N + lax.rem(s[1] + N - n, N)
-
     def body(s, t0, t1, t2, t3, w, kv, ordered, acc):
-        n, k = pl.program_id(0), pl.program_id(1)
-
-        @pl.when((n == 0) & (k == 0))
-        def _():
-            acc[...] = jnp.zeros_like(acc)
-
+        n = pl.program_id(0)
         for i, t in enumerate((t0, t1, t2, t3)):
 
             @pl.when(n == i)
-            def _(t=t):
-                ordered[...] = t[...]
+            def _(t=t, i=i):
                 for e in range(2):
-                    acc[e] += dot(t[0, e], w[0, e], ((1,), (0,)))
-
-        @pl.when((n == N - 1) & (k == N - 1))
-        def _():
-            kv[...] = acc[...].astype(BF)
-
-    return pl.pallas_call(
-        body,
-        grid_spec=pltpu.PrefetchScalarGridSpec(
-            num_scalar_prefetch=1,
-            grid=(N, N),
-            in_specs=[pl.BlockSpec((1, 2, 128, 128), lambda n, k, s: (k, 0, 0, 0))] * 4
-            + [pl.BlockSpec((1, 2, 128, 512), lambda n, k, s: (block(n, k, s), 0, 0, 0))],
+                    part = None
+                    for k in range(N):
+                        at = lax.rem(s[0] + N - k, N)
+                        d = dot(t[k, e], w[at, 0, e], ((1,), (0,)))
+                        part = d if part is None else part + d
+                    if i == 0:
+                        acc[e] = part
+                    elif i < N - 1:
+                        acc[e] += part
+                    else:
+                        kv[e] = (acc[e] + part).astype(BF)
+                for k in range(N):
+                    ordered[lax.rem(s[0] + N - k, N), 0] = t[k]
+
+    whole = pl.BlockSpec((N, 2, 128, 128), lambda n, s: (0, 0, 0, 0))
+    return pl.pallas_call(
+        body,
+        grid_spec=pltpu.PrefetchScalarGridSpec(
+            num_scalar_prefetch=1,
+            grid=(N,),
+            in_specs=[whole] * 4
+            + [
+                pl.BlockSpec(
+                    (N, 1, 2, 128, 512), lambda n, s: (0, lax.rem(s[1] + N - n, N), 0, 0, 0)
+                )
+            ],
             out_specs=[
-                pl.BlockSpec((2, 128, 512), lambda n, k, s: (0, 0, 0)),
-                pl.BlockSpec((1, 2, 128, 128), lambda n, k, s: (block(n, k, s), 0, 0, 0)),
+                pl.BlockSpec((2, 128, 512), lambda n, s: (0, 0, 0)),
+                pl.BlockSpec(
+                    (N, 1, 2, 128, 128), lambda n, s: (0, lax.rem(s[1] + N - n, N), 0, 0, 0)
+                ),
             ],
             scratch_shapes=[pltpu.VMEM((2, 128, 512), F32)],
         ),
         out_shape=[
             jax.ShapeDtypeStruct((2, 128, 512), BF),
-            jax.ShapeDtypeStruct((16, 2, 128, 128), BF),
+            jax.ShapeDtypeStruct((N, N, 2, 128, 128), BF),
         ],
         cost_estimate=pl.CostEstimate(
             flops=2 * 256 * 2048 * 512, bytes_accessed=6 << 20, transcendentals=0
         ),
+        compiler_params=pltpu.CompilerParams(vmem_limit_bytes=32 << 20),
         name="project",
-    )(where, *pieces, weight)
+    )(where, *pieces, weight.reshape(N, N, 2, 128, 512))
+
+
+def weight_gradient(where, pieces, grads):
+    def body(s, t0, t1, t2, t3, d, out):
+        n = pl.program_id(0)
+        for i, t in enumerate((t0, t1, t2, t3)):
+
+            @pl.when(n == i)
+            def _(t=t, i=i):
+                for e in range(2):
+                    part = None
+                    for k in range(N):
+                        at = lax.rem(s[4] + N - k, N)
+                        p = dot(t[k, e], d[at, 0, e], ((0,), (0,)))
+                        part = p if part is None else part + p
+                    if i == 0:
+                        out[e] = part
+                    else:
+                        out[e] += part
+
+    whole = pl.BlockSpec((N, 2, 128, 128), lambda n, s: (0, 0, 0, 0))
+    return pl.pallas_call(
+        body,
+        grid_spec=pltpu.PrefetchScalarGridSpec(
+            num_scalar_prefetch=1,
+            grid=(N,),
+            in_specs=[whole] * 4
+            + [
+                pl.BlockSpec(
+                    (N, 1, 2, 128, 512), lambda n, s: (0, lax.rem(s[5] + n, N), 0, 0, 0)
+                )
+            ],
+            out_specs=pl.BlockSpec((2, 128, 512), lambda n, s: (0, 0, 0)),
+        ),
+        out_shape=jax.ShapeDtypeStruct((2, 128, 512), F32),
+        cost_estimate=pl.CostEstimate(
+            flops=2 * 256 * 2048 * 512, bytes_accessed=6 << 20, transcendentals=0
+        ),
+        compiler_params=pltpu.CompilerParams(vmem_limit_bytes=32 << 20),
+        name="weight_gradient",
+    )(where, *pieces, grads.reshape(N, N, 2, 128, 512))
+
+
+def own_text(where, ordered):
+    y, r = where[4], where[5]
+
+    def shift(a, step):
+        return lax.ppermute(a, "dp", [(i, step(i)) for i in range(16)])
+
+    def block(a, at):
+        return lax.dynamic_index_in_dim(a, at, 0, keepdims=False)
+
+    arrived = [block(ordered, y)]
+    for k in (1, 2, 3):
+        arrived.append(
+            shift(block(ordered, (y + k) % N), lambda i, k=k: (i // N + k) % N * N + i % N)
+        )
+    by_r = jnp.stack(arrived, axis=1)
+    pieces = [block(by_r, r)]
+    for n in (1, 2, 3):
+        pieces.append(
+            shift(block(by_r, (r + N - n) % N), lambda i, n=n: i // N * N + (i % N - n) % N)
+        )
+    return pieces
 
 
 def attend(group, where, queries, grad_out, moved, kvs):
@@ -179,37 +247,38 @@
 
 
 def place(group, where, pieces, before):
+    count = len(group)
+
     def body(s, p0, p1, p2, p3, *rest):
-        outs, sem = rest[-3:-1], rest[-1]
-        copies = []
+        outs = rest[-2:]
         for k, p in enumerate((p0, p1, p2, p3)):
-            for a in range(2):
-                for n, m in enumerate(group):
-                    col = pl.multiple_of(
-                        lax.rem(s[0] + k, N) * 1024 + lax.rem(s[1] + N - m, N) * 256, 256
-                    )
-                    copies.append(
-                        pltpu.make_async_copy(
-                            p.at[a, n], outs[a].at[:, pl.ds(col, 256)], sem.at[len(copies)]
-                        )
-                    )
-        for c in copies:
-            c.start()
-        for c in copies:
-            c.wait()
+
+            @pl.when(pl.program_id(1) == k)
+            def _(p=p):
+                for a in range(2):
+                    outs[a][...] = p[a, 0]
+
+    def column(n, k, s):
+        m = group[0]
+        for i in range(1, count):
+            m = jnp.where(n == i, group[i], m)
+        return (0, lax.rem(s[0] + k, N) * 4 + lax.rem(s[1] + N - m, N))
 
     extra = [] if before is None else list(before)
     return pl.pallas_call(
         body,
         grid_spec=pltpu.PrefetchScalarGridSpec(
             num_scalar_prefetch=1,
-            grid=(1,),
-            in_specs=[pl.BlockSpec(memory_space=pl.ANY)] * (4 + len(extra)),
-            out_specs=[pl.BlockSpec(memory_space=pl.ANY)] * 2,
-            scratch_shapes=[pltpu.SemaphoreType.DMA((8 * len(group),))],
+            grid=(count, N),
+            in_specs=[pl.BlockSpec((2, 1, 256, 256), lambda n, k, s: (0, n, 0, 0))] * 4
+            + [pl.BlockSpec(memory_space=pl.ANY)] * len(extra),
+            out_specs=[pl.BlockSpec((256, 256), column)] * 2,
         ),
         out_shape=[jax.ShapeDtypeStruct((256, 4096), BF)] * 2,
         input_output_aliases={5: 0, 6: 1} if extra else {},
+        cost_estimate=pl.CostEstimate(
+            flops=0, bytes_accessed=count * (2 << 20), transcendentals=0
+        ),
         name="place",
     )(where, *pieces, *extra)
 
@@ -219,7 +288,8 @@
     ctx = lax.axis_index("ctx")
     sample = lax.dynamic_index_in_dim(src, group, 0, keepdims=False)
     limits = lax.dynamic_index_in_dim(lengths, sample, 0, keepdims=False)
-    where = jnp.stack([ctx // N, ctx % N, limits[0], limits[1]]).astype(jnp.int32)
+    where = jnp.stack([ctx // N, ctx % N, limits[0], limits[1], group // N, group % N])
+    where = where.astype(jnp.int32)
     q, g = queries[0], grad_out[0]
 
     everyone = lax.all_gather(text[0], "dp", axis=0)
@@ -236,7 +306,7 @@
     kv, ordered = project(where, pieces, weight)
     kv = kv.reshape(256, 512)
     kvs = [kv] + [z_shift(kv, m) for m in (1, 2, 3)]
-    own_rows = lax.all_to_all(ordered, "dp", split_axis=0, concat_axis=0, tiled=True)
+    own_rows = own_text(where, ordered)
 
     grads = [None] * N
     out = None
@@ -249,9 +319,7 @@
 
     total = grads[0] + sum(grads[m].astype(F32) for m in (1, 2, 3))
     every_grad = lax.all_gather(total.astype(BF).reshape(2, 128, 512), "dp", axis=0)
-    grad_weight = jnp.einsum(
-        "betf,betc->fec", own_rows, every_grad, preferred_element_type=F32
-    )
+    grad_weight = jnp.swapaxes(weight_gradient(where, own_rows, every_grad), 0, 1)
     return (out[0][None], out[1][None], grad_weight)
 
 

time: 415 us -> 267 us (0.64)
  Pallas kernels: 261 us -> 38.7 us
  waiting for transfers between devices: 48.9 us -> 127 us
  local copies, waits for them, and re-layouts: 13.5 us -> 30 us
  starting transfers between devices: 65.9 us -> 52.7 us
    pallas_call x2, Pallas kernels: 131 us -> 11.4 us  [place(): pl.pallas_call(body, grid_spec=pltpu.PrefetchScalarGridSpec(num_scalar_pr...]
    pallas_call x2, Pallas kernels: 99 us -> 3.29 us  [pack(): pl.pallas_call(body, grid_spec=pltpu.PrefetchScalarGridSpec(num_scalar_pr...]
    all_gather x1, waiting for transfers between devices: 0.91 us -> 25.5 us  [per_device(): everyone = lax.all_gather(text[0], 'dp', axis=0)]
    all_gather x1, waiting for transfers between devices: 0.01 us -> 23.3 us  [per_device(): weight = lax.all_gather(jnp.swapaxes(kv_weight, 0, 1), 'dp', axis=0)]
    ppermute x9, waiting for transfers between devices: 19.5 us -> 42.8 us  [z_shift(): lax.ppermute(a, 'ctx', [(4 * x + z, 4 * x + (z + m) % N) for x in range(N...]
    all_to_all x1 -> x0, starting transfers between devices: 23.1 us -> none  [per_device(): lax.all_to_all(ordered, 'dp', split_axis=0, concat_axis=0, tiled=True)]
    ppermute x0 -> x6, waiting for transfers between devices: none -> 17.2 us  [shift(): return lax.ppermute(a, 'dp', [(i, step(i)) for i in range(16)])]
    unnamed x40 -> x56, local copies, waits for them, and re-layouts: 9.17 us -> 23.5 us
  transfers between devices with their start and end apart: 28 -> 33, of which waited for: 9 -> 12; matrix products, arithmetic and copies ran while one was open for 2% -> 3% of each run, Pallas kernels for 63% -> 13%
where the time goes in v2:
time: 267 us; the launch traced here: 266 us
  waiting for transfers between devices  127 us (48%)
  starting transfers between devices  52.7 us (20%)
  Pallas kernels  38.7 us (14%)
  local copies, waits for them, and re-layouts  30 us (11%)
  between operations  16.1 us (6%)
    ppermute x9, waiting for transfers between devices, z_shift(): lax.ppermute(a, 'ctx', [(4 * x + z, 4 * x + (z + m) % N) for x in range(N...  42.8 us
    ppermute x9, starting transfers between devices, z_shift(): lax.ppermute(a, 'ctx', [(4 * x + z, 4 * x + (z + m) % N) for x in range(N...  29.1 us
    all_gather x1, waiting for transfers between devices, per_device(): everyone = lax.all_gather(text[0], 'dp', axis=0)  25.5 us
    unnamed x56, local copies, waits for them, and re-layouts  23.5 us
    all_gather x1, waiting for transfers between devices, per_device(): weight = lax.all_gather(jnp.swapaxes(kv_weight, 0, 1), 'dp', axis=0)  23.3 us
    pallas_call x2, Pallas kernels, attend(): pl.pallas_call(body, grid_spec=pltpu.PrefetchScalarGridSpec(num_scalar_pr...  18.3 us
    ppermute x15, waiting for transfers between devices, x_shift(): lax.ppermute(a, 'ctx', [(4 * x + z, 4 * ((x + k) % N) + z) for x in range...  17.4 us
    ppermute x6, waiting for transfers between devices, shift(): return lax.ppermute(a, 'dp', [(i, step(i)) for i in range(16)])  17.2 us
  transfers between devices with their start and end apart: 33, of which 12 were waited for; matrix products, arithmetic and copies ran while one was open for 3% of the time, Pallas kernels for 13%

profile of v2, /device:TPU:11, one launch (start us, length us, event | category | flops | bytes accessed | tf_op | source)
XLA Modules:
  0.0 266.4 jit_solution(3749912310246125675)
XLA Ops:
  8.0 1.7 copy.16
  9.7 1.2 dynamic_slice.37
  13.6 1.3 stack.47.s
  14.9 1.6 copy-done.1
  16.5 1.6 copy-done.3
  18.1 1.6 pack.3
  21.2 1.2 collective-permute-start.14
  22.5 25.5 %all-gather.5.cloned.1.call-done = bf16[16,2,128,128]{3,2,1,0:T(8,128)(2,1)} async-done(((bf16[1,2,128,128]{3,2,1,0:T(8,128)(2,1)}), bf16[16,2,128,128]{3,2,1,0:T(8,128)(2,1)}) %all-gather.5.cloned.1.call-update) | async-done | bytes 1048592 | tf_op jit(solution)/shard_map/all_gather | solution.py:295
  49.1 2.1 collective-permute-start.4
  51.1 1.5 collective-permute-start.3
  53.5 1.2 collective-permute-done.4
  55.1 3.2 %collective-permute-start.8 = (bf16[4,2,128,128]{3,2,1,0:T(8,128)(2,1)S(1)}, bf16[4,2,128,128]{3,2,1,0:T(8,128)(2,1)S(1)}, u32[]{:S(2)}, u32[]{:S(2)}) collective-permute-start(bf16[4,2,128,128]{3,2,1,0:T(8,128)(2,1)S(1)} %pad_maximum_fusion.1.t0), channel_id=1, source_target_pairs={{0,3},{1,0},{2,1},{3,2},{4,7},{5,4},{6,5},{7,6},{8,11},{9,8},{10,9... | collective-permute-start | bytes 786440 | tf_op jit(solution)/shard_map/ppermute | solution.py:24
  58.3 1.8 collective-permute-start.15
  60.1 2.4 collective-permute-start.7
  62.5 1.5 collective-permute-start.6
  64.1 11.1 %collective-permute-done.8.t3 = bf16[4,2,128,128]{3,2,1,0:T(8,128)(2,1)S(1)} collective-permute-done((bf16[4,2,128,128]{3,2,1,0:T(8,128)(2,1)S(1)}, bf16[4,2,128,128]{3,2,1,0:T(8,128)(2,1)S(1)}, u32[]{:S(2)}, u32[]{:S(2)}) %collective-permute-start.8) | collective-permute-done | bytes 262176 | tf_op jit(solution)/shard_map/ppermute | solution.py:24
  75.9 3.0 %collective-permute-start.16 = (bf16[2,2,256,256]{3,2,1,0:T(8,128)(2,1)}, bf16[2,2,256,256]{3,2,1,0:T(8,128)(2,1)}, u32[]{:S(2)}, u32[]{:S(2)}) collective-permute-start(bf16[2,2,256,256]{3,2,1,0:T(8,128)(2,1)} %copy-done.22), channel_id=1, source_target_pairs={{0,12},{1,13},{2,14},{3,15},{4,0},{5,1},{6,2},{7,3},{8,4},{9,5},{1... | collective-permute-start | bytes 1572872 | tf_op jit(solution)/shard_map/ppermute | solution.py:18
  78.9 1.6 copy-done.4
  80.5 1.7 pack.2
  84.5 1.8 collective-permute-start.1
  86.3 23.3 %all-gather.9.cloned.1.call-done = bf16[32,128,512]{2,1,0:T(8,128)(2,1)} async-done(((bf16[2,128,512]{2,1,0:T(8,128)(2,1)}), bf16[32,128,512]{2,1,0:T(8,128)(2,1)}) %all-gather.9.cloned.1.call-update) | async-done | bytes 4194320 | tf_op jit(solution)/shard_map/all_gather | solution.py:296
  109.6 2.2 copy-done.6
  112.7 0.9 copy-done.12
  113.7 0.9 copy-done.14
  114.6 2.8 %project.1 = (bf16[2,128,512]{2,1,0:T(8,128)(2,1)S(1)}, bf16[4,4,2,128,128]{4,3,2,1,0:T(8,128)(2,1)S(1)}) custom-call(s32[6]{0:T(128)S(1)} %stack.47.s, bf16[4,2,128,128]{3,2,1,0:T(8,128)(2,1)S(1)} %pad_maximum_fusion.1.t0, bf16[4,2,128,128]{3,2,1,0:T(8,128)(2,1)S(1)} %copy-done.14, bf16[4,2,128,128]{3,2,1,0:T(8,128)(2,1)S(1)} %copy-done.12, ...), custom_call_target="tpu_custom_call" | custom-call | flops 536870912 | bytes 6291456 | tf_op jit(solution)/shard_map/project/pallas_call | solution.py:89
  118.5 3.8 %collective-permute-start.10 = (bf16[256,512]{1,0:T(8,128)(2,1)S(1)}, bf16[256,512]{1,0:T(8,128)(2,1)S(1)}, u32[]{:S(2)}, u32[]{:S(2)}) collective-permute-start(bf16[256,512]{1,0:T(8,128)(2,1)S(1)} %bitcast.79), channel_id=1, source_target_pairs={{0,2},{1,3},{2,0},{3,1},{4,6},{5,7},{6,4},{7,5},{8,10},{9,11},{10,... | collective-permute-start | bytes 786440 | tf_op jit(solution)/shard_map/ppermute | solution.py:24
  122.3 7.0 %collective-permute-done.17.refs_8_ = bf16[256,512]{1,0:T(8,128)(2,1)S(1)} collective-permute-done((bf16[256,512]{1,0:T(8,128)(2,1)S(1)}, bf16[256,512]{1,0:T(8,128)(2,1)S(1)}, u32[]{:S(2)}, u32[]{:S(2)}) %collective-permute-start.17) | collective-permute-done | bytes 262176 | tf_op jit(solution)/shard_map/ppermute | solution.py:24
  130.1 9.0 %attend.3 = (bf16[2,2,256,256]{3,2,1,0:T(8,128)(2,1)S(1)}, bf16[2,2,256,256]{3,2,1,0:T(8,128)(2,1)S(1)}, bf16[2,2,256,256]{3,2,1,0:T(8,128)(2,1)S(1)}, bf16[2,2,...) custom-call(s32[6]{0:T(128)S(1)} %stack.47.s, bf16[256,4096]{1,0:T(8,128)(2,1)} %bitcast.43, ...), custom_call_target="tpu_custom_call" | custom-call | flops 1610612736 | bytes 8388608 | tf_op jit(solution)/shard_map/attend/pallas_call | solution.py:227
  141.5 13.6 %collective-permute-start.27 = (bf16[256,512]{1,0:T(8,128)(2,1)S(1)}, bf16[256,512]{1,0:T(8,128)(2,1)S(1)}, u32[]{:S(2)}, u32[]{:S(2)}) collective-permute-start(bf16[256,512]{1,0:T(8,128)(2,1)S(1)} %get-tuple-element.48), channel_id=1, source_target_pairs={{0,3},{1,0},{2,1},{3,2},{4,7},{5,4},{6,5},{7,6},{8,11},{9,8},{10,9... | collective-permute-start | bytes 786440 | tf_op jit(solution)/shard_map/ppermute | solution.py:24
  155.1 9.3 %attend.2 = (bf16[2,2,256,256]{3,2,1,0:T(8,128)(2,1)S(1)}, bf16[2,2,256,256]{3,2,1,0:T(8,128)(2,1)}, bf16[2,2,256,256]{3,2,1,0:T(8,128)(2,1)S(1)}, bf16[2,2,256,...) custom-call(s32[6]{0:T(128)S(1)} %stack.47.s, bf16[256,4096]{1,0:T(8,128)(2,1)} %bitcast.45, ...), custom_call_target="tpu_custom_call" | custom-call | flops 1610612736 | bytes 8388608 | tf_op jit(solution)/shard_map/attend/pallas_call | solution.py:227
  165.3 2.4 collective-permute-start.28
  168.1 16.9 %collective-permute-done.28 = bf16[256,512]{1,0:T(8,128)(2,1)S(1)} collective-permute-done((bf16[256,512]{1,0:T(8,128)(2,1)S(1)}, bf16[256,512]{1,0:T(8,128)(2,1)S(1)}, u32[]{:S(2)}, u32[]{:S(2)}) %collective-permute-start.28) | collective-permute-done | bytes 262176 | tf_op jit(solution)/shard_map/ppermute | solution.py:24
  185.0 7.8 %collective-permute-done.29 = bf16[256,512]{1,0:T(8,128)(2,1)S(1)} collective-permute-done((bf16[256,512]{1,0:T(8,128)(2,1)S(1)}, bf16[256,512]{1,0:T(8,128)(2,1)S(1)}, u32[]{:S(2)}, u32[]{:S(2)}) %collective-permute-start.29) | collective-permute-done | bytes 262176 | tf_op jit(solution)/shard_map/ppermute | solution.py:24
  194.6 1.5 collective-permute-start.21
  196.0 1.3 collective-permute-start.19
  197.3 13.4 %collective-permute-done.23 = bf16[4,2,128,128]{3,2,1,0:T(8,128)(2,1)S(1)} collective-permute-done((bf16[4,2,128,128]{3,2,1,0:T(8,128)(2,1)S(1)}, bf16[4,2,128,128]{3,2,1,0:T(8,128)(2,1)S(1)}, u32[]{:S(2)}, u32[]{:S(2)}) %collective-permute-start.23) | collective-permute-done | bytes 262176 | tf_op jit(solution)/shard_map/ppermute | solution.py:165
  212.2 3.8 %collective-permute-done.21 = bf16[4,2,128,128]{3,2,1,0:T(8,128)(2,1)} collective-permute-done((bf16[4,2,128,128]{3,2,1,0:T(8,128)(2,1)}, bf16[4,2,128,128]{3,2,1,0:T(8,128)(2,1)}, u32[]{:S(2)}, u32[]{:S(2)}) %collective-permute-start.21) | collective-permute-done | bytes 262176 | tf_op jit(solution)/shard_map/ppermute | solution.py:165
  216.1 2.2 collective-permute-done.18.p1
  218.3 1.1 pad_maximum_fusion
  221.1 5.0 %collective-permute-start.26 = (bf16[4,2,128,128]{3,2,1,0:T(8,128)(2,1)}, bf16[4,2,128,128]{3,2,1,0:T(8,128)(2,1)S(1)}, u32[]{:S(2)}, u32[]{:S(2)}) collective-permute-start(bf16[4,2,128,128]{3,2,1,0:T(8,128)(2,1)} %get-tuple-element.57), channel_id=1, source_target_pairs={{0,16},{16,32},{32,48},{48,0},{64,80},{80,96},{96,112},{112,64},{1... | collective-permute-start | bytes 786440 | tf_op jit(solution)/shard_map/ppermute | solution.py:165
  226.2 1.1 collective-permute-start.25
  227.2 13.6 %collective-permute-done.11.p1 = bf16[2,2,256,256]{3,2,1,0:T(8,128)(2,1)} collective-permute-done((bf16[2,2,256,256]{3,2,1,0:T(8,128)(2,1)}, bf16[2,2,256,256]{3,2,1,0:T(8,128)(2,1)}, u32[]{:S(2)}, u32[]{:S(2)}) %collective-permute-start.11) | collective-permute-done | bytes 524320 | tf_op jit(solution)/shard_map/ppermute | solution.py:18
  240.8 1.3 collective-permute-start.24
  242.1 5.7 %place.2 = (bf16[256,4096]{1,0:T(8,128)(2,1)}, bf16[256,4096]{1,0:T(8,128)(2,1)}) custom-call(s32[6]{0:T(128)} %copy-done.15, bf16[2,2,256,256]{3,2,1,0:T(8,128)(2,1)} %copy-done.7, bf16[2,2,256,256]{3,2,1,0:T(8,128)(2,1)} %collective-permute-done.18.p1, bf16[2,2,256,256]{3,2,1,0:T(8,128)(2,1)} %copy-done.26, bf16[2,2,256,256]{3,2,1,0:T(8,128)(2,1)} %collective-permute-done.20.p3), custom_call_target="tpu_custom_call" | custom-call | bytes 4194304 | tf_op jit(solution)/shard_map/place/pallas_call | solution.py:268
  247.8 5.7 %place.3 = (bf16[256,4096]{1,0:T(8,128)(2,1)}, bf16[256,4096]{1,0:T(8,128)(2,1)}) custom-call(s32[6]{0:T(128)} %copy-done.15, bf16[2,2,256,256]{3,2,1,0:T(8,128)(2,1)} %copy-done.8, bf16[2,2,256,256]{3,2,1,0:T(8,128)(2,1)} %collective-permute-done.11.p1, ...), custom_call_target="tpu_custom_call", output_to_operand_aliasing={{0}: (5, {}), {1}: (6, {})} | custom-call | bytes 4194304 | tf_op jit(solution)/shard_map/place/pallas_call | solution.py:268
  253.6 2.2 copy-done.5
  255.8 2.9 %weight_gradient.1 = f32[2,128,512]{2,1,0:T(8,128)S(1)} custom-call(s32[6]{0:T(128)S(1)} %copy-done.16, bf16[4,2,128,128]{3,2,1,0:T(8,128)(2,1)S(1)} %get-tuple-element.60.t0, bf16[4,2,128,128]{3,2,1,0:T(8,128)(2,1)S(1)} %collective-permute-done.24.t1, bf16[4,2,128,128]{3,2,1,0:T(8,128)(2,1)S(1)} %collective-permute-done.25.t2, ...), custom_call_target="tpu_custom_call" | custom-call | flops 536870912 | bytes 6291456 | tf_op jit(solution)/shard_map/weight_gradient/pallas_call | solution.py:139
  258.6 1.2 copy.14
  (96 shorter events, 19.7 us)
Async XLA Ops:
  7.2 5.8 %copy-start = (s32[16,2]{0,1:T(2,128)S(1)}, s32[16,2]{0,1:T(2,128)}, u32[]{:S(2)}) copy-start(s32[16,2]{0,1:T(2,128)} %param.8) | copy-start | bytes 388
  7.2 40.7 %all-gather.5.cloned.1.call-start = ((), (), s32[]{:S(2)}) async-start(), calls=%async_computation | async-start | bytes 1114112 | tf_op jit(solution)/shard_map/all_gather | solution.py:295
  7.9 101.7 %all-gather.9.cloned.1.call-start = ((), (), s32[]{:S(2)}) async-start(), calls=%async_computation.2 | async-start | bytes 4456448 | tf_op jit(solution)/shard_map/all_gather | solution.py:296
  9.7 243.9 %all-gather.7.cloned.1.call-start = ((), (), s32[]{:S(2)}) async-start(), calls=%async_computation.1 | async-start | bytes 4456448 | tf_op jit(solution)/shard_map/all_gather | solution.py:321
  14.9 140.3 %copy-start.15 = (s32[6]{0:T(128)}, s32[6]{0:T(128)S(1)}, u32[]{:S(2)}) copy-start(s32[6]{0:T(128)S(1)} %stack.47.s) | copy-start | bytes 76
  14.9 1.6 copy-start.1
  16.5 1.6 copy-start.3
  18.1 60.8 %copy-start.2 = (bf16[1,256,4096]{2,1,0:T(8,128)(2,1)S(1)}, bf16[1,256,4096]{2,1,0:T(8,128)(2,1)}, u32[]{:S(2)}) copy-start(bf16[1,256,4096]{2,1,0:T(8,128)(2,1)} %param.10) | copy-start | bytes 6291460
  21.2 96.2 %collective-permute-start.14 = (bf16[2,2,256,256]{3,2,1,0:T(8,128)(2,1)}, bf16[2,2,256,256]{3,2,1,0:T(8,128)(2,1)S(1)}, u32[]{:S(2)}, u32[]{:S(2)}) collective-permute-start(bf16[2,2,256,256]{3,2,1,0:T(8,128)(2,1)} %get-tuple-element.35), channel_id=1, source_target_pairs={{0,4},{1,5},{2,6},{3,7},{4,8},{5,9},{6,10},{7,11},{8,12},{9,13},{1... | collective-permute-start | bytes 1572872 | tf_op jit(solution)/shard_map/ppermute | solution.py:18
  48.8 4.7 %collective-permute-start.5 = (bf16[2,128,128]{2,1,0:T(8,128)(2,1)S(1)}, bf16[2,128,128]{2,1,0:T(8,128)(2,1)S(1)}, u32[]{:S(2)}, u32[]{:S(2)}) collective-permute-start(bf16[2,128,128]{2,1,0:T(8,128)(2,1)S(1)} %fusion.1), channel_id=1, source_target_pairs={{0,12},{1,13},{2,14},{3,15},{4,0},{5,1},{6,2},{7,3},{8,4},{9,5},{1... | collective-permute-start | bytes 196616 | tf_op jit(solution)/shard_map/ppermute | solution.py:18
  49.1 5.6 %collective-permute-start.4 = (bf16[2,128,128]{2,1,0:T(8,128)(2,1)S(1)}, bf16[2,128,128]{2,1,0:T(8,128)(2,1)S(1)}, u32[]{:S(2)}, u32[]{:S(2)}) collective-permute-start(bf16[2,128,128]{2,1,0:T(8,128)(2,1)S(1)} %fusion.1), channel_id=1, source_target_pairs={{0,8},{1,9},{2,10},{3,11},{4,12},{5,13},{6,14},{7,15},{8,0},{9,1},... | collective-permute-start | bytes 196616 | tf_op jit(solution)/shard_map/ppermute | solution.py:18
  51.1 3.9 %collective-permute-start.3 = (bf16[2,128,128]{2,1,0:T(8,128)(2,1)S(1)}, bf16[2,128,128]{2,1,0:T(8,128)(2,1)S(1)}, u32[]{:S(2)}, u32[]{:S(2)}) collective-permute-start(bf16[2,128,128]{2,1,0:T(8,128)(2,1)S(1)} %fusion.1), channel_id=1, source_target_pairs={{0,4},{1,5},{2,6},{3,7},{4,8},{5,9},{6,10},{7,11},{8,12},{9,13},{1... | collective-permute-start | bytes 196616 | tf_op jit(solution)/shard_map/ppermute | solution.py:18
  55.1 20.1 %collective-permute-start.8 = (bf16[4,2,128,128]{3,2,1,0:T(8,128)(2,1)S(1)}, bf16[4,2,128,128]{3,2,1,0:T(8,128)(2,1)S(1)}, u32[]{:S(2)}, u32[]{:S(2)}) collective-permute-start(bf16[4,2,128,128]{3,2,1,0:T(8,128)(2,1)S(1)} %pad_maximum_fusion.1.t0), channel_id=1, source_target_pairs={{0,3},{1,0},{2,1},{3,2},{4,7},{5,4},{6,5},{7,6},{8,11},{9,8},{10,9... | collective-permute-start | bytes 786440 | tf_op jit(solution)/shard_map/ppermute | solution.py:24
  58.3 59.3 %collective-permute-start.15 = (bf16[2,2,256,256]{3,2,1,0:T(8,128)(2,1)}, bf16[2,2,256,256]{3,2,1,0:T(8,128)(2,1)S(1)}, u32[]{:S(2)}, u32[]{:S(2)}) collective-permute-start(bf16[2,2,256,256]{3,2,1,0:T(8,128)(2,1)} %copy-done.23), channel_id=1, source_target_pairs={{0,8},{1,9},{2,10},{3,11},{4,12},{5,13},{6,14},{7,15},{8,0},{9,1},... | collective-permute-start | bytes 1572872 | tf_op jit(solution)/shard_map/ppermute | solution.py:18
  60.1 23.0 %collective-permute-start.7 = (bf16[4,2,128,128]{3,2,1,0:T(8,128)(2,1)S(1)}, bf16[4,2,128,128]{3,2,1,0:T(8,128)(2,1)S(1)}, u32[]{:S(2)}, u32[]{:S(2)}) collective-permute-start(bf16[4,2,128,128]{3,2,1,0:T(8,128)(2,1)S(1)} %pad_maximum_fusion.1.t0), channel_id=1, source_target_pairs={{0,2},{1,3},{2,0},{3,1},{4,6},{5,7},{6,4},{7,5},{8,10},{9,11},{10,... | collective-permute-start | bytes 786440 | tf_op jit(solution)/shard_map/ppermute | solution.py:24
  62.5 21.3 %collective-permute-start.6 = (bf16[4,2,128,128]{3,2,1,0:T(8,128)(2,1)S(1)}, bf16[4,2,128,128]{3,2,1,0:T(8,128)(2,1)S(1)}, u32[]{:S(2)}, u32[]{:S(2)}) collective-permute-start(bf16[4,2,128,128]{3,2,1,0:T(8,128)(2,1)S(1)} %pad_maximum_fusion.1.t0), channel_id=1, source_target_pairs={{0,1},{1,2},{2,3},{3,0},{4,5},{5,6},{6,7},{7,4},{8,9},{9,10},{10,1... | collective-permute-start | bytes 786440 | tf_op jit(solution)/shard_map/ppermute | solution.py:24
  75.9 42.7 %collective-permute-start.16 = (bf16[2,2,256,256]{3,2,1,0:T(8,128)(2,1)}, bf16[2,2,256,256]{3,2,1,0:T(8,128)(2,1)}, u32[]{:S(2)}, u32[]{:S(2)}) collective-permute-start(bf16[2,2,256,256]{3,2,1,0:T(8,128)(2,1)} %copy-done.22), channel_id=1, source_target_pairs={{0,12},{1,13},{2,14},{3,15},{4,0},{5,1},{6,2},{7,3},{8,4},{9,5},{1... | collective-permute-start | bytes 1572872 | tf_op jit(solution)/shard_map/ppermute | solution.py:18
  78.9 1.6 copy-start.4
  83.8 57.7 %collective-permute-start = (bf16[2,2,256,256]{3,2,1,0:T(8,128)(2,1)}, bf16[2,2,256,256]{3,2,1,0:T(8,128)(2,1)S(1)}, u32[]{:S(2)}, u32[]{:S(2)}) collective-permute-start(bf16[2,2,256,256]{3,2,1,0:T(8,128)(2,1)} %get-tuple-element.27), channel_id=1, source_target_pairs={{0,4},{1,5},{2,6},{3,7},{4,8},{5,9},{6,10},{7,11},{8,12},{9,13},{1... | collective-permute-start | bytes 1572872 | tf_op jit(solution)/shard_map/ppermute | solution.py:18
  84.5 70.6 %collective-permute-start.1 = (bf16[2,2,256,256]{3,2,1,0:T(8,128)(2,1)}, bf16[2,2,256,256]{3,2,1,0:T(8,128)(2,1)S(1)}, u32[]{:S(2)}, u32[]{:S(2)}) collective-permute-start(bf16[2,2,256,256]{3,2,1,0:T(8,128)(2,1)} %get-tuple-element.28), channel_id=1, source_target_pairs={{0,8},{1,9},{2,10},{3,11},{4,12},{5,13},{6,14},{7,15},{8,0},{9,1},... | collective-permute-start | bytes 1572872 | tf_op jit(solution)/shard_map/ppermute | solution.py:18
  109.6 2.2 copy-start.6
  111.8 0.9 copy-start.10
  112.7 0.9 copy-start.12
  114.6 2.9 %copy-start.25 = (bf16[2,2,256,256]{3,2,1,0:T(8,128)(2,1)S(1)}, bf16[2,2,256,256]{3,2,1,0:T(8,128)(2,1)}, u32[]{:S(2)}) copy-start(bf16[2,2,256,256]{3,2,1,0:T(8,128)(2,1)} %copy-done.24) | copy-start | bytes 1572868
  117.5 37.6 %collective-permute-start.2 = (bf16[2,2,256,256]{3,2,1,0:T(8,128)(2,1)S(1)}, bf16[2,2,256,256]{3,2,1,0:T(8,128)(2,1)S(1)}, u32[]{:S(2)}, u32[]{:S(2)}) collective-permute-start(bf16[2,2,256,256]{3,2,1,0:T(8,128)(2,1)S(1)} %copy-done.25), channel_id=1, source_target_pairs={{0,12},{1,13},{2,14},{3,15},{4,0},{5,1},{6,2},{7,3},{8,4},{9,5},{1... | collective-permute-start | bytes 1572872 | tf_op jit(solution)/shard_map/ppermute | solution.py:18
  117.6 11.8 %collective-permute-start.17 = (bf16[256,512]{1,0:T(8,128)(2,1)S(1)}, bf16[256,512]{1,0:T(8,128)(2,1)S(1)}, u32[]{:S(2)}, u32[]{:S(2)}) collective-permute-start(bf16[256,512]{1,0:T(8,128)(2,1)S(1)} %bitcast.78), channel_id=1, source_target_pairs={{0,1},{1,2},{2,3},{3,0},{4,5},{5,6},{6,7},{7,4},{8,9},{9,10},{10,1... | collective-permute-start | bytes 786440 | tf_op jit(solution)/shard_map/ppermute | solution.py:24
  118.5 36.6 %collective-permute-start.10 = (bf16[256,512]{1,0:T(8,128)(2,1)S(1)}, bf16[256,512]{1,0:T(8,128)(2,1)S(1)}, u32[]{:S(2)}, u32[]{:S(2)}) collective-permute-start(bf16[256,512]{1,0:T(8,128)(2,1)S(1)} %bitcast.79), channel_id=1, source_target_pairs={{0,2},{1,3},{2,0},{3,1},{4,6},{5,7},{6,4},{7,5},{8,10},{9,11},{10,... | collective-permute-start | bytes 786440 | tf_op jit(solution)/shard_map/ppermute | solution.py:24
  129.4 25.7 %collective-permute-start.9 = (bf16[256,512]{1,0:T(8,128)(2,1)S(1)}, bf16[256,512]{1,0:T(8,128)(2,1)S(1)}, u32[]{:S(2)}, u32[]{:S(2)}) collective-permute-start(bf16[256,512]{1,0:T(8,128)(2,1)S(1)} %bitcast.80), channel_id=1, source_target_pairs={{0,3},{1,0},{2,1},{3,2},{4,7},{5,4},{6,5},{7,6},{8,11},{9,8},{10,9... | collective-permute-start | bytes 786440 | tf_op jit(solution)/shard_map/ppermute | solution.py:24
  141.5 13.6 %copy-start.21 = (bf16[2,2,256,256]{3,2,1,0:T(8,128)(2,1)}, bf16[2,2,256,256]{3,2,1,0:T(8,128)(2,1)S(1)}, u32[]{:S(2)}) copy-start(bf16[2,2,256,256]{3,2,1,0:T(8,128)(2,1)S(1)} %get-tuple-element.39) | copy-start | bytes 1572868
  141.5 26.6 %collective-permute-start.27 = (bf16[256,512]{1,0:T(8,128)(2,1)S(1)}, bf16[256,512]{1,0:T(8,128)(2,1)S(1)}, u32[]{:S(2)}, u32[]{:S(2)}) collective-permute-start(bf16[256,512]{1,0:T(8,128)(2,1)S(1)} %get-tuple-element.48), channel_id=1, source_target_pairs={{0,3},{1,0},{2,1},{3,2},{4,7},{5,4},{6,5},{7,6},{8,11},{9,8},{10,9... | collective-permute-start | bytes 786440 | tf_op jit(solution)/shard_map/ppermute | solution.py:24
  165.3 30.8 %copy-start.20 = (bf16[2,2,256,256]{3,2,1,0:T(8,128)(2,1)S(1)}, bf16[2,2,256,256]{3,2,1,0:T(8,128)(2,1)}, u32[]{:S(2)}) copy-start(bf16[2,2,256,256]{3,2,1,0:T(8,128)(2,1)} %copy-done.19) | copy-start | bytes 1572868
  165.3 45.5 %copy-start.18 = (bf16[2,2,256,256]{3,2,1,0:T(8,128)(2,1)S(1)}, bf16[2,2,256,256]{3,2,1,0:T(8,128)(2,1)}, u32[]{:S(2)}) copy-start(bf16[2,2,256,256]{3,2,1,0:T(8,128)(2,1)} %copy-done.17) | copy-start | bytes 1572868
  165.3 19.7 %collective-permute-start.28 = (bf16[256,512]{1,0:T(8,128)(2,1)S(1)}, bf16[256,512]{1,0:T(8,128)(2,1)S(1)}, u32[]{:S(2)}, u32[]{:S(2)}) collective-permute-start(bf16[256,512]{1,0:T(8,128)(2,1)S(1)} %get-tuple-element.49), channel_id=1, source_target_pairs={{0,2},{1,3},{2,0},{3,1},{4,6},{5,7},{6,4},{7,5},{8,10},{9,11},{10,... | collective-permute-start | bytes 786440 | tf_op jit(solution)/shard_map/ppermute | solution.py:24
  167.7 25.1 %collective-permute-start.29 = (bf16[256,512]{1,0:T(8,128)(2,1)S(1)}, bf16[256,512]{1,0:T(8,128)(2,1)S(1)}, u32[]{:S(2)}, u32[]{:S(2)}) collective-permute-start(bf16[256,512]{1,0:T(8,128)(2,1)S(1)} %get-tuple-element.50), channel_id=1, source_target_pairs={{0,1},{1,2},{2,3},{3,0},{4,5},{5,6},{6,7},{7,4},{8,9},{9,10},{10,1... | collective-permute-start | bytes 786440 | tf_op jit(solution)/shard_map/ppermute | solution.py:24
  193.7 24.6 %collective-permute-start.18 = (bf16[2,2,256,256]{3,2,1,0:T(8,128)(2,1)}, bf16[2,2,256,256]{3,2,1,0:T(8,128)(2,1)}, u32[]{:S(2)}, u32[]{:S(2)}) collective-permute-start(bf16[2,2,256,256]{3,2,1,0:T(8,128)(2,1)} %copy-done.21), channel_id=1, source_target_pairs={{0,12},{1,13},{2,14},{3,15},{4,0},{5,1},{6,2},{7,3},{8,4},{9,5},{1... | collective-permute-start | bytes 1572872 | tf_op jit(solution)/shard_map/ppermute | solution.py:18
  194.6 16.2 %collective-permute-start.23 = (bf16[4,2,128,128]{3,2,1,0:T(8,128)(2,1)S(1)}, bf16[4,2,128,128]{3,2,1,0:T(8,128)(2,1)S(1)}, u32[]{:S(2)}, u32[]{:S(2)}) collective-permute-start(bf16[4,2,128,128]{3,2,1,0:T(8,128)(2,1)S(1)} %get-tuple-element.62), channel_id=1, source_target_pairs={{0,192},{16,208},{32,224},{48,240},{64,0},{80,16},{96,32},{112,48}... | collective-permute-start | bytes 786440 | tf_op jit(solution)/shard_map/ppermute | solution.py:165
  194.6 17.0 %collective-permute-start.22 = (bf16[4,2,128,128]{3,2,1,0:T(8,128)(2,1)S(1)}, bf16[4,2,128,128]{3,2,1,0:T(8,128)(2,1)S(1)}, u32[]{:S(2)}, u32[]{:S(2)}) collective-permute-start(bf16[4,2,128,128]{3,2,1,0:T(8,128)(2,1)S(1)} %get-tuple-element.63), channel_id=1, source_target_pairs={{0,128},{16,144},{32,160},{48,176},{64,192},{80,208},{96,224},{112... | collective-permute-start | bytes 786440 | tf_op jit(solution)/shard_map/ppermute | solution.py:165
  194.6 21.5 %collective-permute-start.21 = (bf16[4,2,128,128]{3,2,1,0:T(8,128)(2,1)}, bf16[4,2,128,128]{3,2,1,0:T(8,128)(2,1)}, u32[]{:S(2)}, u32[]{:S(2)}) collective-permute-start(bf16[4,2,128,128]{3,2,1,0:T(8,128)(2,1)} %get-tuple-element.64), channel_id=1, source_target_pairs={{0,64},{16,80},{32,96},{48,112},{64,128},{80,144},{96,160},{112,17... | collective-permute-start | bytes 786440 | tf_op jit(solution)/shard_map/ppermute | solution.py:165
  196.0 24.3 %collective-permute-start.19 = (bf16[2,2,256,256]{3,2,1,0:T(8,128)(2,1)S(1)}, bf16[2,2,256,256]{3,2,1,0:T(8,128)(2,1)S(1)}, u32[]{:S(2)}, u32[]{:S(2)}) collective-permute-start(bf16[2,2,256,256]{3,2,1,0:T(8,128)(2,1)S(1)} %copy-done.20), channel_id=1, source_target_pairs={{0,8},{1,9},{2,10},{3,11},{4,12},{5,13},{6,14},{7,15},{8,0},{9,1},... | collective-permute-start | bytes 1572872 | tf_op jit(solution)/shard_map/ppermute | solution.py:18
  210.7 15.4 %collective-permute-start.20 = (bf16[2,2,256,256]{3,2,1,0:T(8,128)(2,1)S(1)}, bf16[2,2,256,256]{3,2,1,0:T(8,128)(2,1)}, u32[]{:S(2)}, u32[]{:S(2)}) collective-permute-start(bf16[2,2,256,256]{3,2,1,0:T(8,128)(2,1)S(1)} %copy-done.18), channel_id=1, source_target_pairs={{0,4},{1,5},{2,6},{3,7},{4,8},{5,9},{6,10},{7,11},{8,12},{9,13},{1... | collective-permute-start | bytes 1572872 | tf_op jit(solution)/shard_map/ppermute | solution.py:18
  211.5 29.2 %collective-permute-start.11 = (bf16[2,2,256,256]{3,2,1,0:T(8,128)(2,1)}, bf16[2,2,256,256]{3,2,1,0:T(8,128)(2,1)}, u32[]{:S(2)}, u32[]{:S(2)}) collective-permute-start(bf16[2,2,256,256]{3,2,1,0:T(8,128)(2,1)} %get-tuple-element.32), channel_id=1, source_target_pairs={{0,12},{1,13},{2,14},{3,15},{4,0},{5,1},{6,2},{7,3},{8,4},{9,5},{1... | collective-permute-start | bytes 1572872 | tf_op jit(solution)/shard_map/ppermute | solution.py:18
  216.1 31.7 %collective-permute-start.12 = (bf16[2,2,256,256]{3,2,1,0:T(8,128)(2,1)S(1)}, bf16[2,2,256,256]{3,2,1,0:T(8,128)(2,1)}, u32[]{:S(2)}, u32[]{:S(2)}) collective-permute-start(bf16[2,2,256,256]{3,2,1,0:T(8,128)(2,1)S(1)} %get-tuple-element.33), channel_id=1, source_target_pairs={{0,8},{1,9},{2,10},{3,11},{4,12},{5,13},{6,14},{7,15},{8,0},{9,1},... | collective-permute-start | bytes 1572872 | tf_op jit(solution)/shard_map/ppermute | solution.py:18
  218.3 29.5 %collective-permute-start.13 = (bf16[2,2,256,256]{3,2,1,0:T(8,128)(2,1)S(1)}, bf16[2,2,256,256]{3,2,1,0:T(8,128)(2,1)}, u32[]{:S(2)}, u32[]{:S(2)}) collective-permute-start(bf16[2,2,256,256]{3,2,1,0:T(8,128)(2,1)S(1)} %get-tuple-element.34), channel_id=1, source_target_pairs={{0,4},{1,5},{2,6},{3,7},{4,8},{5,9},{6,10},{7,11},{8,12},{9,13},{1... | collective-permute-start | bytes 1572872 | tf_op jit(solution)/shard_map/ppermute | solution.py:18
  221.1 32.4 %collective-permute-start.26 = (bf16[4,2,128,128]{3,2,1,0:T(8,128)(2,1)}, bf16[4,2,128,128]{3,2,1,0:T(8,128)(2,1)S(1)}, u32[]{:S(2)}, u32[]{:S(2)}) collective-permute-start(bf16[4,2,128,128]{3,2,1,0:T(8,128)(2,1)} %get-tuple-element.57), channel_id=1, source_target_pairs={{0,16},{16,32},{32,48},{48,0},{64,80},{80,96},{96,112},{112,64},{1... | collective-permute-start | bytes 786440 | tf_op jit(solution)/shard_map/ppermute | solution.py:165
  226.2 27.4 %collective-permute-start.25 = (bf16[4,2,128,128]{3,2,1,0:T(8,128)(2,1)}, bf16[4,2,128,128]{3,2,1,0:T(8,128)(2,1)S(1)}, u32[]{:S(2)}, u32[]{:S(2)}) collective-permute-start(bf16[4,2,128,128]{3,2,1,0:T(8,128)(2,1)} %get-tuple-element.58), channel_id=1, source_target_pairs={{0,32},{16,48},{32,0},{48,16},{64,96},{80,112},{96,64},{112,80},{1... | collective-permute-start | bytes 786440 | tf_op jit(solution)/shard_map/ppermute | solution.py:165
  240.8 12.8 %collective-permute-start.24 = (bf16[4,2,128,128]{3,2,1,0:T(8,128)(2,1)S(1)}, bf16[4,2,128,128]{3,2,1,0:T(8,128)(2,1)S(1)}, u32[]{:S(2)}, u32[]{:S(2)}) collective-permute-start(bf16[4,2,128,128]{3,2,1,0:T(8,128)(2,1)S(1)} %get-tuple-element.59), channel_id=1, source_target_pairs={{0,48},{16,0},{32,16},{48,32},{64,112},{80,64},{96,80},{112,96},{1... | collective-permute-start | bytes 786440 | tf_op jit(solution)/shard_map/ppermute | solution.py:165
  247.8 5.8 %copy-start.16 = (s32[6]{0:T(128)S(1)}, s32[6]{0:T(128)}, u32[]{:S(2)}) copy-start(s32[6]{0:T(128)} %copy-done.15) | copy-start | bytes 76
  253.6 2.2 copy-start.5
  (12 other events, 9.5 us)
Sparse Core Ops, SparseCore 0:
  9.9 38.0 all-gather.4
  49.8 59.7 all-gather.8
  193.7 40.8 all-gather.6

commit v3 on v0

v3 whole, which is shorter than its diff:
```python
import math

import jax
import jax.numpy as jnp
from jax import lax
from jax.experimental import pallas as pl
from jax.experimental.pallas import tpu as pltpu
from jax.sharding import PartitionSpec as P

HEAD = 128
N = 4
ALONG_X = [[4 * x + z for x in range(N)] for z in range(N)]
BF = jnp.bfloat16
F32 = jnp.float32
PARAMS = pltpu.CompilerParams(vmem_limit_bytes=60 << 20)
ANY = pl.BlockSpec(memory_space=pl.ANY)
ORDER = (0, 1, 3, 2)
PARTS = ((0, 0, 1), (0, 1, 1), (1, 0, 1), (1, 1, 1))


def x_shift(a, k):
    return lax.ppermute(
        a, "ctx", [(4 * x + z, 4 * ((x + k) % N) + z) for x in range(N) for z in range(N)]
    )


def z_shift(a, m):
    return lax.ppermute(
        a, "ctx", [(4 * x + z, 4 * x + (z + m) % N) for x in range(N) for z in range(N)]
    )


def y_shift(a, k):
    return lax.ppermute(a, "dp", [(i, (i // N + k) % N * N + i % N) for i in range(16)])


def r_shift(a, n):
    return lax.ppermute(a, "dp", [(i, i // N * N + (i % N + n) % N) for i in range(16)])


def exchange_x(a):
    return lax.all_to_all(
        a, "ctx", split_axis=0, concat_axis=0, tiled=True, axis_index_groups=ALONG_X
    )


def dot(a, b, dims):
    return lax.dot_general(a, b, (dims, ((), ())), preferred_element_type=F32)


def minus(a, b):
    return lax.rem(a + N - b, N)


def whole(shape):
    return pl.BlockSpec(shape, lambda *_: (0,) * len(shape))


def call(body, scalars, grid, in_specs, out_specs, out_shape, name, cost, scratch=(), alias=()):
    return pl.pallas_call(
        body,
        grid_spec=pltpu.PrefetchScalarGridSpec(
            num_scalar_prefetch=len(scalars),
            grid=grid,
            in_specs=in_specs,
            out_specs=out_specs,
            scratch_shapes=list(scratch),
        ),
        out_shape=out_shape,
        input_output_aliases=dict(alias),
        cost_estimate=pl.CostEstimate(flops=cost[0], bytes_accessed=cost[1], transcendentals=0),
        compiler_params=PARAMS,
        name=name,
    )


def small(body, scalars, arrays, after, out_shape, name):
    here = pl.BlockSpec(memory_space=pltpu.VMEM)
    return pl.pallas_call(
        body,
        in_specs=[pl.BlockSpec(memory_space=pltpu.SMEM)] * len(scalars)
        + [here] * len(arrays) + [ANY] * len(after),
        out_specs=jax.tree.map(lambda _: here, out_shape),
        out_shape=out_shape,
        cost_estimate=pl.CostEstimate(flops=0, bytes_accessed=1 << 19, transcendentals=0),
        compiler_params=pltpu.CompilerParams(vmem_limit_bytes=16 << 20),
        name=name,
    )(*scalars, *arrays, *after)


def text_to_send(where, src, near):
    def body(w, src, *refs):
        for k in range(N):
            sample = src[lax.rem(w[2] + k, N) * N + w[3]]
            at = minus(lax.rem(sample, N), w[3])
            for n in range(N):

                @pl.when(at == n)
                def _(n=n, k=k):
                    refs[N + k][...] = refs[n][...]

    one = jax.ShapeDtypeStruct((2, 128, 128), BF)
    return small(body, (where, src), near, (), [one] * N, "text_to_send")


def text_that_came(where, src, came):
    def body(w, src, *refs):
        at = minus(w[2], src[w[2] * N + w[3]] // N)
        for k in range(N):

            @pl.when(at == k)
            def _(k=k):
                refs[N][...] = refs[k][...]

    one = jax.ShapeDtypeStruct((2, 128, 128), BF)
    return small(body, (where, src), came, (), one, "text_that_came")


def tiny(a):
    return a[(0,) * (a.ndim - 2)][:16, :128]


def pack(order, where, queries, grad_out, after):
    rows = 64

    def body(w, q, g, *rest):
        out = rest[-1]
        for x in range(N):
            for i, m in enumerate(order):
                col = pl.multiple_of((x * N + minus(w[1], m)) * 256, 256)
                out[x, 0, i] = q[:, pl.ds(col, 256)]
                out[x, 1, i] = g[:, pl.ds(col, 256)]

    return call(
        body, (where,), (256 // rows,),
        [pl.BlockSpec((rows, 4096), lambda i, w: (i, 0))] * 2 + [ANY] * len(after),
        pl.BlockSpec((N, 2, len(order), rows, 256), lambda i, w: (0, 0, 0, i, 0)),
        jax.ShapeDtypeStruct((N, 2, len(order), 256, 256), BF), "pack", (0, 6 << 20),
    )(where, queries, grad_out, *after)


def project(where, pieces, weight):
    def body(w, t0, t1, t2, t3, wt, kv, *rest):
        rows, acc = rest[:N], rest[N]
        k = pl.program_id(0)
        for i, t in enumerate((t0, t1, t2, t3)):

            @pl.when(k == i)
            def _(t=t, i=i):
                for e in range(2):
                    part = None
                    for n in range(N):
                        d = dot(t[n, e], wt[0, minus(w[1], n), e], ((1,), (0,)))
                        part = d if part is None else part + d
                    if i == 0:
                        acc[e] = part
                    elif i < N - 1:
                        acc[e] += part
                    else:
                        kv[e] = (acc[e] + part).astype(BF)
                for j in range(N):

                    @pl.when(minus(minus(w[0], i), w[2]) == j)
                    def _():
                        for n in range(N):
                            rows[j][minus(w[1], n)] = t[n]

    def at(k, w):
        return (minus(w[0], k), 0, 0, 0, 0)

    quarter = (N, 2, 128, 128)
    kv, *rows = call(
        body, (where,), (N,),
        [whole(quarter)] * N + [pl.BlockSpec((1, N, 2, 128, 512), at)],
        [whole((2, 128, 512))] + [whole(quarter)] * N,
        [jax.ShapeDtypeStruct((2, 128, 512), BF)] + [jax.ShapeDtypeStruct(quarter, BF)] * N,
        "project", (2 * 256 * 2048 * 512, 6 << 20), [pltpu.VMEM((2, 128, 512), F32)],
    )(where, *pieces, weight.reshape(N, N, 2, 128, 512))
    return kv.reshape(256, 512), rows


def attend(order, first, where, src, lengths, moved, kvs, into, wait):
    count = len(order)
    scale = 1.0 / math.sqrt(HEAD)

    def body(w, src, lengths, sent, *refs):
        kvs, kv, total = refs[:count], refs[-2], refs[-1]
        out, grads = refs[-3 - count], refs[-2 - count : -2]
        p = pl.program_id(0)
        cols = pl.ds(pl.multiple_of(pl.program_id(1) * 256, 256), 256)
        for i in range(count):

            @pl.when(p == i)
            def _(i=i):
                kv[...] = kvs[i][:, cols]

        sample = src[w[2] * N + w[3]]
        row = lax.broadcasted_iota(jnp.int32, (256, 256), 0)
        valid = row < jnp.where(row < 128, lengths[2 * sample], lengths[2 * sample + 1] + 128)
        key, value = kv[:, :HEAD], kv[:, HEAD:]
        grad_key = grad_value = None
        for x in range(N):
            q, g = sent[x, 0, 0], sent[x, 1, 0]
            scores = dot(key, q, ((1,), (1,))) * scale
            scores = jnp.where(valid, scores, -1e30)
            weights = jnp.exp(scores - jnp.max(scores, axis=0, keepdims=True))
            probs = weights * (1.0 / jnp.sum(weights, axis=0, keepdims=True))
            low = probs.astype(BF)
            out[x, 0, 0] = dot(low, value, ((0,), (0,))).astype(BF)
            grad_probs = dot(value, g, ((1,), (1,)))
            delta = jnp.sum(probs * grad_probs, axis=0, keepdims=True)
            grad_scores = (probs * (grad_probs - delta) * scale).astype(BF)
            out[x, 1, 0] = dot(grad_scores, key, ((0,), (0,))).astype(BF)
            dk = dot(grad_scores, q, ((1,), (0,)))
            dv = dot(low, g, ((1,), (0,)))
            grad_key = dk if x == 0 else grad_key + dk
            grad_value = dv if x == 0 else grad_value + dv
        total[:, :HEAD] = grad_key
        total[:, HEAD:] = grad_value
        for i in range(count):

            @pl.when(p == i)
            def _(i=i):
                grads[i][:, cols] = total[...].astype(grads[i].dtype)

    res = call(
        body, (where, src, lengths), (count, 2),
        [pl.BlockSpec((N, 2, 1, 256, HEAD), lambda p, l, *_: (0, 0, p + first, 0, l))]
        + [whole((256, 512))] * count + [ANY] * (len(into) + len(wait)),
        [pl.BlockSpec((N, 2, 1, 256, HEAD), lambda p, l, *_: (0, 0, p + first, 0, l))]
        + [whole((256, 512))] * count,
        [jax.ShapeDtypeStruct((N, 2, 2, 256, 256), BF)]
        + [
            jax.ShapeDtypeStruct((256, 512), BF if m else F32)
            for m in order
        ],
        "attend", (count * 6_000_000_000, (4 << 20) * count),
        [pltpu.VMEM((256, 256), BF), pltpu.VMEM((256, 256), F32)],
        {4 + count: 0} if into else {},
    )(where, src, lengths, moved, *kvs, *into, *wait)
    return res[0], res[1:]


def add_up(own, others, after):
    def body(a, b, c, d, *rest):
        rest[-1][...] = (a[...] + (b[...].astype(F32) + c[...] + d[...])).astype(BF)

    return small(
        body, (), [own, *others], after, jax.ShapeDtypeStruct((256, 512), BF), "add_up"
    )


def rows_to_send(where, came):
    def body(w, *refs):
        for n in range(N):
            for k in range(N):
                refs[N + n][k] = refs[k][minus(w[3], n)]

    return small(
        body, (where,), came, (), [jax.ShapeDtypeStruct((N, 2, 128, 128), BF)] * N,
        "rows_to_send",
    )


def weight_gradient(where, pieces, grads):
    def body(w, t0, t1, t2, t3, d, out):
        n = pl.program_id(0)
        for i, t in enumerate((t0, t1, t2, t3)):

            @pl.when(n == i)
            def _(t=t, i=i):
                for e in range(2):
                    part = None
                    for k in range(N):
                        p = dot(t[k, e], d[minus(w[2], k), 0, e], ((0,), (0,)))
                        part = p if part is None else part + p
                    if i == 0:
                        out[e] = part
                    else:
                        out[e] += part

    return call(
        body, (where,), (N,),
        [whole((N, 2, 128, 128))] * N
        + [pl.BlockSpec((N, 1, 2, 128, 512), lambda n, w: (0, lax.rem(w[3] + n, N), 0, 0, 0))],
        whole((2, 128, 512)), jax.ShapeDtypeStruct((2, 128, 512), F32), "weight_gradient",
        (2 * 256 * 2048 * 512, 6 << 20),
    )(where, *pieces, grads.reshape(N, N, 2, 128, 512))


def place(where, parts):
    rows = 64

    def body(w, *refs):
        outs = refs[-2:]
        slots = [(part, at) for part in refs[:2] for at in range(2)]
        for m, (part, at) in zip(ORDER, slots):
            for x in range(N):
                col = pl.multiple_of((x * N + minus(w[1], m)) * 256, 256)
                for a in range(2):
                    outs[a][:, pl.ds(col, 256)] = part[x, a, at]

    return call(
        body, (where,), (256 // rows,),
        [pl.BlockSpec((N, 2, 2, rows, 256), lambda i, w: (0, 0, 0, i, 0))] * 2,
        [pl.BlockSpec((rows, 4096), lambda i, w: (i, 0))] * 2,
        [jax.ShapeDtypeStruct((256, 4096), BF)] * 2, "place", (0, 8 << 20),
    )(where, *parts)


def per_device(text, src, lengths, kv_weight, queries, grad_out):
    group = lax.axis_index("dp")
    ctx = lax.axis_index("ctx")
    where = jnp.stack([ctx // N, ctx % N, group // N, group % N]).astype(jnp.int32)
    lengths = lengths.reshape(32)
    text, q, g = text[0], queries[0], grad_out[0]

    weight = lax.all_gather(jnp.swapaxes(kv_weight, 0, 1), "dp", axis=0)
    near = [text] + [r_shift(text, N - n) for n in (1, 2, 3)]
    packed = pack(ORDER[:2], where, q, g, [tiny(a) for a in near[1:]])
    moved = [exchange_x(packed)]
    packed = pack(ORDER[2:], where, q, g, [tiny(packed)])
    sends = text_to_send(where, src, near)
    picked = text_that_came(
        where, src, [sends[0]] + [y_shift(sends[k], k) for k in (1, 2, 3)]
    )
    along_z = jnp.stack([picked] + [z_shift(picked, n) for n in (1, 2, 3)])
    pieces = [along_z] + [x_shift(along_z, k) for k in (1, 2, 3)]

    kv, rows = project(where, pieces, weight)
    packed, kv = lax.optimization_barrier((packed, kv))
    moved.append(exchange_x(packed))
    kvs = [kv] + [z_shift(kv, m) for m in ORDER[1:]]
    rows = [rows[0]] + [y_shift(rows[k], k) for k in (1, 2, 3)]
    by_r = rows_to_send(where, rows)
    own_rows = [by_r[0]] + [r_shift(by_r[n], N - n) for n in (1, 2, 3)]
    waits = ([], [kvs[2], *rows[1:]], [], own_rows[1:])

    outs, grads, done = [None, None], [], 0
    for which, first, count in PARTS:
        part = slice(done, done + count)
        into = [outs[which]] if first else []
        wait = [tiny(a) for a in waits[done]]
        outs[which], d = attend(
            ORDER[part], first, where, src, lengths, moved[which], kvs[part], into, wait
        )
        for m, a in zip(ORDER[part], d):
            grads.append(z_shift(a, N - m) if m else a)
        done += count

    outs = [exchange_x(a) for a in outs]
    total = add_up(grads[0], grads[1:], [tiny(outs[0])])
    every_grad = lax.all_gather(total.reshape(2, 128, 512), "dp", axis=0)
    grad_weight = weight_gradient(where, own_rows, every_grad)
    attended, grad_queries = place(where, outs)
    return (attended[None], grad_queries[None], jnp.swapaxes(grad_weight, 0, 1))


def solution(mesh):
    placed = (
        P("dp", None, None, "ctx"),
        P(),
        P(),
        P("dp", None, "ctx"),
        P("dp", "ctx", None),
        P("dp", "ctx", None),
    )
    return jax.shard_map(
        per_device,
        mesh=mesh,
        in_specs=placed,
        out_specs=(P("dp", "ctx", None), P("dp", "ctx", None), P("dp", None, "ctx")),
        check_vma=False,
    )
```

time: 415 us -> 224 us (0.54)
  waiting for transfers between devices: 182 us -> 49 us
  local copies, waits for them, and re-layouts: 80.4 us -> 16.3 us
  matrix products: 59.5 us -> 0 us
  Pallas kernels: 0 us -> 57.2 us
  blocking collectives: 0 us -> 26.1 us
  other arithmetic: 15.7 us -> 0.63 us
    all_to_all x5 -> x3, waiting for transfers between devices: 147 us -> 1.81 us  [exchange_x(): lax.all_to_all(a, 'ctx', split_axis=0, concat_axis=0, tiled=True, axis_in...]
    pallas_call x0 -> x13, Pallas kernels: none -> 57.2 us  [the longest x4 27.2 us: attend(): call(body, (where, src, lengths), (count, 2), [pl.BlockSpec((N, 2, 1, 256...]
    dot_general x7 -> x0, matrix products: 50.9 us -> none  [the longest x1 15.4 us: attend(): jnp.einsum('bhlj,blhd->bjhd', grad_scores, q_rows, preferred_element_type...]
    ppermute x0 -> x24, starting transfers between devices: none -> 41.5 us  [the longest x9 19.6 us: z_shift(): lax.ppermute(a, 'ctx', [(4 * x + z, 4 * x + (z + m) % N) for x in range(N...]
    all_to_all x5 -> x3, starting transfers between devices: 55.1 us -> 16.5 us  [exchange_x(): lax.all_to_all(a, 'ctx', split_axis=0, concat_axis=0, tiled=True, axis_in...]
    ppermute x0 -> x24, waiting for transfers between devices: none -> 37.6 us  [the longest x9 29 us: z_shift(): lax.ppermute(a, 'ctx', [(4 * x + z, 4 * x + (z + m) % N) for x in range(N...]
    all_gather x2, waiting for transfers between devices: 35.8 us -> 9.59 us  [the longest x1 9.59 us: per_device(): every_grad = lax.all_gather(total.reshape(2, 128, 512), 'dp', axis=0)]
    all_to_all x0 -> x1, blocking collectives: none -> 26.1 us  [exchange_x(): lax.all_to_all(a, 'ctx', split_axis=0, concat_axis=0, tiled=True, axis_in...]
  transfers between devices with their start and end apart: 7 -> 29, of which waited for: 5 -> 12; matrix products, arithmetic and copies ran while one was open for 32% -> 5% of each run, Pallas kernels for 0% -> 23%
where the time goes in v3:
time: 224 us; the launch traced here: 222 us
  starting transfers between devices  58.1 us (26%)
  Pallas kernels  57.2 us (26%)
  waiting for transfers between devices  49 us (22%)
  blocking collectives  26.1 us (12%)
  local copies, waits for them, and re-layouts  16.3 us (7%)
  between operations  14.2 us (6%)
    ppermute x9, waiting for transfers between devices, z_shift(): lax.ppermute(a, 'ctx', [(4 * x + z, 4 * x + (z + m) % N) for x in range(N...  29 us
    pallas_call x4, Pallas kernels, attend(): call(body, (where, src, lengths), (count, 2), [pl.BlockSpec((N, 2, 1, 256...  27.2 us
    all_to_all x1, blocking collectives, exchange_x(): lax.all_to_all(a, 'ctx', split_axis=0, concat_axis=0, tiled=True, axis_in...  26.1 us
    ppermute x9, starting transfers between devices, z_shift(): lax.ppermute(a, 'ctx', [(4 * x + z, 4 * x + (z + m) % N) for x in range(N...  19.6 us
    all_to_all x3, starting transfers between devices, exchange_x(): lax.all_to_all(a, 'ctx', split_axis=0, concat_axis=0, tiled=True, axis_in...  16.5 us
    ppermute x6, starting transfers between devices, y_shift(): lax.ppermute(a, 'dp', [(i, (i // N + k) % N * N + i % N) for i in range(1...  10.4 us
    pallas_call x2, Pallas kernels, pack(): call(body, (where,), (256 // rows,), [pl.BlockSpec((rows, 4096), lambda i...  9.85 us
    all_gather x1, waiting for transfers between devices, per_device(): every_grad = lax.all_gather(total.reshape(2, 128, 512), 'dp', axis=0)  9.59 us
  transfers between devices with their start and end apart: 29, of which 12 were waited for; matrix products, arithmetic and copies ran while one was open for 5% of the time, Pallas kernels for 23%

profile of v3, /device:TPU:11, one launch (start us, length us, event | category | flops | bytes accessed | tf_op | source)
XLA Modules:
  0.0 221.5 jit_solution(15219317987218627164)
XLA Ops:
  7.2 1.7 copy.21
  8.9 2.3 %collective-permute-start.2 = (bf16[2,128,128]{2,1,0:T(8,128)(2,1)}, bf16[2,128,128]{2,1,0:T(8,128)(2,1)S(1)}, u32[]{:S(2)}, u32[]{:S(2)}) collective-permute-start(bf16[2,128,128]{2,1,0:T(8,128)(2,1)} %bitcast.44), channel_id=1, source_target_pairs={{0,16},{16,32},{32,48},{48,0},{64,80},{80,96},{96,112},{112,64},{1... | collective-permute-start | bytes 196616 | tf_op jit(solution)/shard_map/ppermute | solution.py:38
  13.4 1.2 collective-permute-done.1.refs_2_
  15.9 4.9 %pack.2 = bf16[4,2,2,256,256]{4,3,2,1,0:T(8,128)(2,1)} custom-call(s32[4]{0:T(128)} %pad_add_fusion.w, bf16[256,4096]{1,0:T(8,128)(2,1)} %bitcast.48, bf16[256,4096]{1,0:T(8,128)(2,1)} %bitcast.50, bf16[16,128]{1,0:T(8,128)(2,1)} %slice_bitcast_fusion.10.rest_0_, bf16[16,128]{1,0:T(8,128)(2,1)} %slice_bitcast_fusion.9.rest_1_, ...), custom_call_target="tpu_custom_call" | custom-call | bytes 6291456 | tf_op jit(solution)/shard_map/pack/pallas_call | solution.py:134
  20.8 4.4 %all-to-all-start = ((bf16[4,2,2,256,256]{4,3,2,1,0:T(8,128)(2,1)}), bf16[4,2,2,256,256]{4,3,2,1,0:T(8,128)(2,1)S(1)}, u32[]{:S(2)}, u32[]{:S(2)}) async-start(bf16[4,2,2,256,256]{4,3,2,1,0:T(8,128)(2,1)} %pack.2), calls=%async_computation | async-start | bytes 4194304 | tf_op jit(solution)/shard_map/all_to_all | solution.py:42
  25.2 0.7 text_to_send.1
  25.9 1.4 collective-permute-start.3
  27.2 1.8 collective-permute-start.4
  29.1 1.0 collective-permute-start.5
  30.2 3.6 %collective-permute-done.4.refs_2_ = bf16[2,128,128]{2,1,0:T(8,128)(2,1)S(1)} collective-permute-done((bf16[2,128,128]{2,1,0:T(8,128)(2,1)S(1)}, bf16[2,128,128]{2,1,0:T(8,128)(2,1)S(1)}, u32[]{:S(2)}, u32[]{:S(2)}) %collective-permute-start.4) | collective-permute-done | bytes 65568 | tf_op jit(solution)/shard_map/ppermute | solution.py:34
  33.8 1.3 collective-permute-done.5.refs_3_
  35.6 5.3 %collective-permute-start.8 = (bf16[2,128,128]{2,1,0:T(8,128)(2,1)S(1)}, bf16[2,128,128]{2,1,0:T(8,128)(2,1)S(1)}, u32[]{:S(2)}, u32[]{:S(2)}) collective-permute-start(bf16[2,128,128]{2,1,0:T(8,128)(2,1)S(1)} %text_that_came.1), channel_id=1, source_target_pairs={{0,3},{1,0},{2,1},{3,2},{4,7},{5,4},{6,5},{7,6},{8,11},{9,8},{10,9... | collective-permute-start | bytes 196616 | tf_op jit(solution)/shard_map/ppermute | solution.py:28
  41.3 2.3 %collective-permute-start.6 = (bf16[2,128,128]{2,1,0:T(8,128)(2,1)S(1)}, bf16[2,128,128]{2,1,0:T(8,128)(2,1)S(1)}, u32[]{:S(2)}, u32[]{:S(2)}) collective-permute-start(bf16[2,128,128]{2,1,0:T(8,128)(2,1)S(1)} %text_that_came.1), channel_id=1, source_target_pairs={{0,1},{1,2},{2,3},{3,0},{4,5},{5,6},{6,7},{7,4},{8,9},{9,10},{10,1... | collective-permute-start | bytes 196616 | tf_op jit(solution)/shard_map/ppermute | solution.py:28
  43.6 4.9 %collective-permute-done.7 = bf16[2,128,128]{2,1,0:T(8,128)(2,1)S(1)} collective-permute-done((bf16[2,128,128]{2,1,0:T(8,128)(2,1)S(1)}, bf16[2,128,128]{2,1,0:T(8,128)(2,1)S(1)}, u32[]{:S(2)}, u32[]{:S(2)}) %collective-permute-start.7) | collective-permute-done | bytes 65568 | tf_op jit(solution)/shard_map/ppermute | solution.py:28
  48.9 2.1 collective-permute-start.10
  51.0 1.5 collective-permute-start.9
  53.2 0.9 slice_bitcast_fusion.1
  54.7 5.0 %pack.3 = bf16[4,2,2,256,256]{4,3,2,1,0:T(8,128)(2,1)} custom-call(s32[4]{0:T(128)} %pad_add_fusion.w, bf16[256,4096]{1,0:T(8,128)(2,1)} %bitcast.49, bf16[256,4096]{1,0:T(8,128)(2,1)} %bitcast.51, bf16[16,128]{1,0:T(8,128)(2,1)} %slice.114.rest_0_), custom_call_target="tpu_custom_call" | custom-call | bytes 6291456 | tf_op jit(solution)/shard_map/pack/pallas_call | solution.py:134
  59.8 1.8 collective-permute-done.9.t1
  61.6 0.7 copy-done.14
  62.2 6.2 %project.1 = (bf16[2,128,512]{2,1,0:T(8,128)(2,1)}, bf16[4,2,128,128]{3,2,1,0:T(8,128)(2,1)}, bf16[4,2,128,128]{3,2,1,0:T(8,128)(2,1)}, bf16[4,2,128,128]{3,2,1,0:T(8,128)(2,1)}, bf16[4,2,128,128]{3,2,1,0:T(8,128)(2,1)}) custom-call(s32[4]{0:T(128)} %pad_add_fusion.w, bf16[4,2,128,128]{3,2,1,0:T(8,128)(2,1)} %copy-done.9, ...), custom_call_target="tpu_custom_call" | custom-call | flops 536870912 | bytes 6291456 | tf_op jit(solution)/shard_map/project/pallas_call | solution.py:172
  68.4 5.9 %collective-permute-start.17 = (bf16[256,512]{1,0:T(8,128)(2,1)}, bf16[256,512]{1,0:T(8,128)(2,1)}, u32[]{:S(2)}, u32[]{:S(2)}) collective-permute-start(bf16[256,512]{1,0:T(8,128)(2,1)} %bitcast.17.refs_0_), channel_id=1, source_target_pairs={{0,2},{1,3},{2,0},{3,1},{4,6},{5,7},{6,4},{7,5},{8,10},{9,11},{10,... | collective-permute-start | bytes 786440 | tf_op jit(solution)/shard_map/ppermute | solution.py:28
  74.6 6.0 %collective-permute-start.15 = (bf16[4,2,128,128]{3,2,1,0:T(8,128)(2,1)}, bf16[4,2,128,128]{3,2,1,0:T(8,128)(2,1)S(1)}, u32[]{:S(2)}, u32[]{:S(2)}) collective-permute-start(bf16[4,2,128,128]{3,2,1,0:T(8,128)(2,1)} %get-tuple-element.36), channel_id=1, source_target_pairs={{0,128},{16,144},{32,160},{48,176},{64,192},{80,208},{96,224},{112... | collective-permute-start | bytes 786440 | tf_op jit(solution)/shard_map/ppermute | solution.py:34
  80.6 7.9 %all-to-all-start.2 = ((bf16[4,2,2,256,256]{4,3,2,1,0:T(8,128)(2,1)}), bf16[4,2,2,256,256]{4,3,2,1,0:T(8,128)(2,1)}, u32[]{:S(2)}, u32[]{:S(2)}) async-start(bf16[4,2,2,256,256]{4,3,2,1,0:T(8,128)(2,1)} %pack.3), calls=%async_computation.2 | async-start | bytes 4194304 | tf_op jit(solution)/shard_map/all_to_all | solution.py:42
  88.5 6.9 %attend.4 = (bf16[4,2,2,256,256]{4,3,2,1,0:T(8,128)(2,1)}, f32[256,512]{1,0:T(8,128)}) custom-call(s32[4]{0:T(128)} %pad_add_fusion.w, s32[16]{0:T(128)} %src.11, s32[32]{0:T(128)} %reshape.27.lengths, bf16[4,2,2,256,256]{4,3,2,1,0:T(8,128)(2,1)} %copy-done.8, bf16[256,512]{1,0:T(8,128)(2,1)} %bitcast.17.refs_0_), custom_call_target="tpu_custom_call" | custom-call | flops 6000000000 | bytes 4194304 | tf_op jit(solution)/shard_map/attend/pallas_call | solution.py:226
  95.4 1.4 collective-permute-start.12
  97.4 0.7 copy-done.1
  98.1 3.2 %collective-permute-start.18 = (bf16[4,2,128,128]{3,2,1,0:T(8,128)(2,1)S(1)}, bf16[4,2,128,128]{3,2,1,0:T(8,128)(2,1)S(1)}, u32[]{:S(2)}, u32[]{:S(2)}) collective-permute-start(bf16[4,2,128,128]{3,2,1,0:T(8,128)(2,1)S(1)} %get-tuple-element.42), channel_id=1, source_target_pairs={{0,48},{16,0},{32,16},{48,32},{64,112},{80,64},{96,80},{112,96},{1... | collective-permute-start | bytes 786440 | tf_op jit(solution)/shard_map/ppermute | solution.py:38
  102.5 1.6 collective-permute-start.20
  104.1 1.3 slice.115.refs_2_
  106.0 3.5 %collective-permute-done.12.refs_0_ = bf16[256,512]{1,0:T(8,128)(2,1)S(1)} collective-permute-done((bf16[256,512]{1,0:T(8,128)(2,1)}, bf16[256,512]{1,0:T(8,128)(2,1)S(1)}, u32[]{:S(2)}, u32[]{:S(2)}) %collective-permute-start.12) | collective-permute-done | bytes 262176 | tf_op jit(solution)/shard_map/ppermute | solution.py:28
  109.5 0.7 copy-done.16
  110.2 6.7 %attend.5 = (bf16[4,2,2,256,256]{4,3,2,1,0:T(8,128)(2,1)}, bf16[256,512]{1,0:T(8,128)(2,1)}) custom-call(s32[4]{0:T(128)} %pad_add_fusion.w, s32[16]{0:T(128)} %src.11, s32[32]{0:T(128)} %reshape.27.lengths, bf16[4,2,2,256,256]{4,3,2,1,0:T(8,128)(2,1)} %copy-done.8, bf16[256,512]{1,0:T(8,128)(2,1)} %copy-done.16, ...), custom_call_target="tpu_custom_call", output_to_operand_aliasing={{0}: (5, {})} | custom-call | flops 6000000000 | bytes 4194304 | tf_op jit(solution)/shard_map/attend/pallas_call | solution.py:226
  117.2 0.7 copy-done.10
  118.5 4.2 %all-to-all-start.1 = ((bf16[4,2,2,256,256]{4,3,2,1,0:T(8,128)(2,1)}), bf16[4,2,2,256,256]{4,3,2,1,0:T(8,128)(2,1)S(1)}, u32[]{:S(2)}, u32[]{:S(2)}) async-start(bf16[4,2,2,256,256]{4,3,2,1,0:T(8,128)(2,1)} %get-tuple-element.38), calls=%async_computation.1 | async-start | bytes 4194304 | tf_op jit(solution)/shard_map/all_to_all | solution.py:42
  122.8 1.3 slice_bitcast_fusion.3.refs_3_
  124.6 6.7 %attend.6 = (bf16[4,2,2,256,256]{4,3,2,1,0:T(8,128)(2,1)}, bf16[256,512]{1,0:T(8,128)(2,1)}) custom-call(s32[4]{0:T(128)} %pad_add_fusion.w, s32[16]{0:T(128)} %src.11, s32[32]{0:T(128)} %reshape.27.lengths, bf16[4,2,2,256,256]{4,3,2,1,0:T(8,128)(2,1)} %all-to-all-done.2.sent, bf16[256,512]{1,0:T(8,128)(2,1)} %collective-permute-done.13.refs_0_), custom_call_target="tpu_custom_call" | custom-call | flops 6000000000 | bytes 4194304 | tf_op jit(solution)/shard_map/attend/pallas_call | solution.py:226
  131.4 6.8 %attend.7 = (bf16[4,2,2,256,256]{4,3,2,1,0:T(8,128)(2,1)}, bf16[256,512]{1,0:T(8,128)(2,1)}) custom-call(s32[4]{0:T(128)} %pad_add_fusion.w, s32[16]{0:T(128)} %src.11, s32[32]{0:T(128)} %reshape.27.lengths, bf16[4,2,2,256,256]{4,3,2,1,0:T(8,128)(2,1)} %all-to-all-done.2.sent, ...), custom_call_target="tpu_custom_call", output_to_operand_aliasing={{0}: (5, {})} | custom-call | flops 6000000000 | bytes 4194304 | tf_op jit(solution)/shard_map/attend/pallas_call | solution.py:226
  138.2 4.0 %collective-permute-start.23 = (bf16[256,512]{1,0:T(8,128)(2,1)}, bf16[256,512]{1,0:T(8,128)(2,1)S(1)}, u32[]{:S(2)}, u32[]{:S(2)}) collective-permute-start(bf16[256,512]{1,0:T(8,128)(2,1)} %get-tuple-element.52), channel_id=1, source_target_pairs={{0,2},{1,3},{2,0},{3,1},{4,6},{5,7},{6,4},{7,5},{8,10},{9,11},{10,... | collective-permute-start | bytes 786440 | tf_op jit(solution)/shard_map/ppermute | solution.py:28
  142.2 1.8 all-to-all-done.1.refs_0_
  144.1 12.1 %collective-permute-done.23.d = bf16[256,512]{1,0:T(8,128)(2,1)S(1)} collective-permute-done((bf16[256,512]{1,0:T(8,128)(2,1)}, bf16[256,512]{1,0:T(8,128)(2,1)S(1)}, u32[]{:S(2)}, u32[]{:S(2)}) %collective-permute-start.23) | collective-permute-done | bytes 262176 | tf_op jit(solution)/shard_map/ppermute | solution.py:28
  156.2 8.4 %collective-permute-done.22.c = bf16[256,512]{1,0:T(8,128)(2,1)S(1)} collective-permute-done((bf16[256,512]{1,0:T(8,128)(2,1)}, bf16[256,512]{1,0:T(8,128)(2,1)S(1)}, u32[]{:S(2)}, u32[]{:S(2)}) %collective-permute-start.22) | collective-permute-done | bytes 262176 | tf_op jit(solution)/shard_map/ppermute | solution.py:28
  164.6 0.8 add_up.1
  165.5 26.1 %all_to_all.20.refs_1_ = bf16[4,2,2,256,256]{4,3,2,1,0:T(8,128)(2,1)} all-to-all(bf16[4,2,2,256,256]{4,3,2,1,0:T(8,128)(2,1)} %get-tuple-element.45), channel_id=1, replica_groups={{0,4,8,12},{1,5,9,13},{2,6,10,14},{3,7,11,15},{16,20,24,28},{17,21,25,2..., dimensions={0} | all-to-all | bytes 4194304 | tf_op jit(solution)/shard_map/all_to_all | solution.py:42
  191.6 5.5 %place.1 = (bf16[256,4096]{1,0:T(8,128)(2,1)}, bf16[256,4096]{1,0:T(8,128)(2,1)}) custom-call(s32[4]{0:T(128)} %pad_add_fusion.w, bf16[4,2,2,256,256]{4,3,2,1,0:T(8,128)(2,1)} %copy-done.7, bf16[4,2,2,256,256]{4,3,2,1,0:T(8,128)(2,1)} %all_to_all.20.refs_1_), custom_call_target="tpu_custom_call" | custom-call | bytes 8388608 | tf_op jit(solution)/shard_map/place/pallas_call | solution.py:303
  197.1 9.6 %all-gather.4.cloned.1.call-done = bf16[16,2,128,512]{3,2,1,0:T(8,128)(2,1)} async-done(((bf16[1,2,128,512]{3,2,1,0:T(8,128)(2,1)}), bf16[16,2,128,512]{3,2,1,0:T(8,128)(2,1)}) %all-gather.4.cloned.1.call-update) | async-done | bytes 4194320 | tf_op jit(solution)/shard_map/all_gather | solution.py:353
  206.7 5.8 %weight_gradient.1 = f32[2,128,512]{2,1,0:T(8,128)} custom-call(s32[4]{0:T(128)} %pad_add_fusion.w, bf16[4,2,128,128]{3,2,1,0:T(8,128)(2,1)} %copy-done.1, bf16[4,2,128,128]{3,2,1,0:T(8,128)(2,1)} %copy-done.10, bf16[4,2,128,128]{3,2,1,0:T(8,128)(2,1)} %collective-permute-done.19.t2, bf16[4,2,128,128]{3,2,1,0:T(8,128)(2,1)} %copy-done.11, ...), custom_call_target="tpu_custom_call" | custom-call | flops 536870912 | bytes 6291456 | tf_op jit(solution)/shard_map/weight_gradient/pallas_call | solution.py:282
  212.4 2.2 %copy.19 = f32[128,2,512]{2,1,0:T(2,128)} copy(f32[128,2,512]{2,0,1:T(8,128)} %bitcast.54) | data formatting | bytes 1048576
  (80 shorter events, 10.4 us)
Async XLA Ops:
  7.2 54.4 %all-gather.6.cloned.1.call-start = ((), (), s32[]{:S(2)}) async-start(), calls=%async_computation.5 | async-start | bytes 4456448 | tf_op jit(solution)/shard_map/all_gather | solution.py:318
  8.9 3.9 %collective-permute-start.2 = (bf16[2,128,128]{2,1,0:T(8,128)(2,1)}, bf16[2,128,128]{2,1,0:T(8,128)(2,1)S(1)}, u32[]{:S(2)}, u32[]{:S(2)}) collective-permute-start(bf16[2,128,128]{2,1,0:T(8,128)(2,1)} %bitcast.44), channel_id=1, source_target_pairs={{0,16},{16,32},{32,48},{48,0},{64,80},{80,96},{96,112},{112,64},{1... | collective-permute-start | bytes 196616 | tf_op jit(solution)/shard_map/ppermute | solution.py:38
  11.2 3.5 %collective-permute-start.1 = (bf16[2,128,128]{2,1,0:T(8,128)(2,1)}, bf16[2,128,128]{2,1,0:T(8,128)(2,1)S(1)}, u32[]{:S(2)}, u32[]{:S(2)}) collective-permute-start(bf16[2,128,128]{2,1,0:T(8,128)(2,1)} %bitcast.45), channel_id=1, source_target_pairs={{0,32},{16,48},{32,0},{48,16},{64,96},{80,112},{96,64},{112,80},{1... | collective-permute-start | bytes 196616 | tf_op jit(solution)/shard_map/ppermute | solution.py:38
  11.2 4.1 %collective-permute-start = (bf16[2,128,128]{2,1,0:T(8,128)(2,1)}, bf16[2,128,128]{2,1,0:T(8,128)(2,1)S(1)}, u32[]{:S(2)}, u32[]{:S(2)}) collective-permute-start(bf16[2,128,128]{2,1,0:T(8,128)(2,1)} %bitcast.46), channel_id=1, source_target_pairs={{0,48},{16,0},{32,16},{48,32},{64,112},{80,64},{96,80},{112,96},{1... | collective-permute-start | bytes 196616 | tf_op jit(solution)/shard_map/ppermute | solution.py:38
  20.7 4.4 %copy-start.3 = (bf16[1,2,128,128]{3,2,1,0:T(8,128)(2,1)S(1)}, bf16[1,2,128,128]{3,2,1,0:T(8,128)(2,1)}, u32[]{:S(2)}) copy-start(bf16[1,2,128,128]{3,2,1,0:T(8,128)(2,1)} %param.6) | copy-start | bytes 196612
  20.7 4.4 %copy-start.4 = (s32[4]{0:T(128)S(1)}, s32[4]{0:T(128)}, u32[]{:S(2)}) copy-start(s32[4]{0:T(128)} %pad_add_fusion.w) | copy-start | bytes 52
  20.7 4.4 %copy-start.6 = (s32[16]{0:T(128)S(1)}, s32[16]{0:T(128)}, u32[]{:S(2)}) copy-start(s32[16]{0:T(128)} %src.11) | copy-start | bytes 196
  20.7 31.8 %copy-start.15 = (s32[16,2]{0,1:T(2,128)S(1)}, s32[16,2]{0,1:T(2,128)}, u32[]{:S(2)}) copy-start(s32[16,2]{0,1:T(2,128)} %param.8) | copy-start | bytes 388
  20.8 59.8 %all-to-all-start = ((bf16[4,2,2,256,256]{4,3,2,1,0:T(8,128)(2,1)}), bf16[4,2,2,256,256]{4,3,2,1,0:T(8,128)(2,1)S(1)}, u32[]{:S(2)}, u32[]{:S(2)}) async-start(bf16[4,2,2,256,256]{4,3,2,1,0:T(8,128)(2,1)} %pack.2), calls=%async_computation | async-start | bytes 4194304 | tf_op jit(solution)/shard_map/all_to_all | solution.py:42
  25.9 4.3 %collective-permute-start.3 = (bf16[2,128,128]{2,1,0:T(8,128)(2,1)S(1)}, bf16[2,128,128]{2,1,0:T(8,128)(2,1)S(1)}, u32[]{:S(2)}, u32[]{:S(2)}) collective-permute-start(bf16[2,128,128]{2,1,0:T(8,128)(2,1)S(1)} %get-tuple-element.29), channel_id=1, source_target_pairs={{0,64},{16,80},{32,96},{48,112},{64,128},{80,144},{96,160},{112,17... | collective-permute-start | bytes 196616 | tf_op jit(solution)/shard_map/ppermute | solution.py:34
  27.2 6.5 %collective-permute-start.4 = (bf16[2,128,128]{2,1,0:T(8,128)(2,1)S(1)}, bf16[2,128,128]{2,1,0:T(8,128)(2,1)S(1)}, u32[]{:S(2)}, u32[]{:S(2)}) collective-permute-start(bf16[2,128,128]{2,1,0:T(8,128)(2,1)S(1)} %get-tuple-element.30), channel_id=1, source_target_pairs={{0,128},{16,144},{32,160},{48,176},{64,192},{80,208},{96,224},{112... | collective-permute-start | bytes 196616 | tf_op jit(solution)/shard_map/ppermute | solution.py:34
  29.1 6.0 %collective-permute-start.5 = (bf16[2,128,128]{2,1,0:T(8,128)(2,1)S(1)}, bf16[2,128,128]{2,1,0:T(8,128)(2,1)S(1)}, u32[]{:S(2)}, u32[]{:S(2)}) collective-permute-start(bf16[2,128,128]{2,1,0:T(8,128)(2,1)S(1)} %get-tuple-element.31), channel_id=1, source_target_pairs={{0,192},{16,208},{32,224},{48,240},{64,0},{80,16},{96,32},{112,48}... | collective-permute-start | bytes 196616 | tf_op jit(solution)/shard_map/ppermute | solution.py:34
  35.6 7.9 %collective-permute-start.8 = (bf16[2,128,128]{2,1,0:T(8,128)(2,1)S(1)}, bf16[2,128,128]{2,1,0:T(8,128)(2,1)S(1)}, u32[]{:S(2)}, u32[]{:S(2)}) collective-permute-start(bf16[2,128,128]{2,1,0:T(8,128)(2,1)S(1)} %text_that_came.1), channel_id=1, source_target_pairs={{0,3},{1,0},{2,1},{3,2},{4,7},{5,4},{6,5},{7,6},{8,11},{9,8},{10,9... | collective-permute-start | bytes 196616 | tf_op jit(solution)/shard_map/ppermute | solution.py:28
  40.9 7.6 %collective-permute-start.7 = (bf16[2,128,128]{2,1,0:T(8,128)(2,1)S(1)}, bf16[2,128,128]{2,1,0:T(8,128)(2,1)S(1)}, u32[]{:S(2)}, u32[]{:S(2)}) collective-permute-start(bf16[2,128,128]{2,1,0:T(8,128)(2,1)S(1)} %text_that_came.1), channel_id=1, source_target_pairs={{0,2},{1,3},{2,0},{3,1},{4,6},{5,7},{6,4},{7,5},{8,10},{9,11},{10,... | collective-permute-start | bytes 196616 | tf_op jit(solution)/shard_map/ppermute | solution.py:28
  41.3 7.2 %collective-permute-start.6 = (bf16[2,128,128]{2,1,0:T(8,128)(2,1)S(1)}, bf16[2,128,128]{2,1,0:T(8,128)(2,1)S(1)}, u32[]{:S(2)}, u32[]{:S(2)}) collective-permute-start(bf16[2,128,128]{2,1,0:T(8,128)(2,1)S(1)} %text_that_came.1), channel_id=1, source_target_pairs={{0,1},{1,2},{2,3},{3,0},{4,5},{5,6},{6,7},{7,4},{8,9},{9,10},{10,1... | collective-permute-start | bytes 196616 | tf_op jit(solution)/shard_map/ppermute | solution.py:28
  48.5 11.2 %copy-start.9 = (bf16[4,2,128,128]{3,2,1,0:T(8,128)(2,1)}, bf16[4,2,128,128]{3,2,1,0:T(8,128)(2,1)S(1)}, u32[]{:S(2)}) copy-start(bf16[4,2,128,128]{3,2,1,0:T(8,128)(2,1)S(1)} %pad_maximum_fusion.t0) | copy-start | bytes 786436
  48.6 11.2 %collective-permute-start.11 = (bf16[4,2,128,128]{3,2,1,0:T(8,128)(2,1)S(1)}, bf16[4,2,128,128]{3,2,1,0:T(8,128)(2,1)S(1)}, u32[]{:S(2)}, u32[]{:S(2)}) collective-permute-start(bf16[4,2,128,128]{3,2,1,0:T(8,128)(2,1)S(1)} %pad_maximum_fusion.t0), channel_id=1, source_target_pairs={{0,12},{1,13},{2,14},{3,15},{4,0},{5,1},{6,2},{7,3},{8,4},{9,5},{1... | collective-permute-start | bytes 786440 | tf_op jit(solution)/shard_map/ppermute | solution.py:22
  48.9 10.9 %collective-permute-start.10 = (bf16[4,2,128,128]{3,2,1,0:T(8,128)(2,1)S(1)}, bf16[4,2,128,128]{3,2,1,0:T(8,128)(2,1)S(1)}, u32[]{:S(2)}, u32[]{:S(2)}) collective-permute-start(bf16[4,2,128,128]{3,2,1,0:T(8,128)(2,1)S(1)} %pad_maximum_fusion.t0), channel_id=1, source_target_pairs={{0,8},{1,9},{2,10},{3,11},{4,12},{5,13},{6,14},{7,15},{8,0},{9,1},... | collective-permute-start | bytes 786440 | tf_op jit(solution)/shard_map/ppermute | solution.py:22
  51.0 10.5 %collective-permute-start.9 = (bf16[4,2,128,128]{3,2,1,0:T(8,128)(2,1)S(1)}, bf16[4,2,128,128]{3,2,1,0:T(8,128)(2,1)S(1)}, u32[]{:S(2)}, u32[]{:S(2)}) collective-permute-start(bf16[4,2,128,128]{3,2,1,0:T(8,128)(2,1)S(1)} %pad_maximum_fusion.t0), channel_id=1, source_target_pairs={{0,4},{1,5},{2,6},{3,7},{4,8},{5,9},{6,10},{7,11},{8,12},{9,13},{1... | collective-permute-start | bytes 786440 | tf_op jit(solution)/shard_map/ppermute | solution.py:22
  59.7 1.8 copy-start.12
  59.8 1.8 copy-start.13
  61.5 0.7 copy-start.14
  68.4 62.9 %collective-permute-start.17 = (bf16[256,512]{1,0:T(8,128)(2,1)}, bf16[256,512]{1,0:T(8,128)(2,1)}, u32[]{:S(2)}, u32[]{:S(2)}) collective-permute-start(bf16[256,512]{1,0:T(8,128)(2,1)} %bitcast.17.refs_0_), channel_id=1, source_target_pairs={{0,2},{1,3},{2,0},{3,1},{4,6},{5,7},{6,4},{7,5},{8,10},{9,11},{10,... | collective-permute-start | bytes 786440 | tf_op jit(solution)/shard_map/ppermute | solution.py:28
  74.4 28.1 %collective-permute-start.13 = (bf16[256,512]{1,0:T(8,128)(2,1)}, bf16[256,512]{1,0:T(8,128)(2,1)}, u32[]{:S(2)}, u32[]{:S(2)}) collective-permute-start(bf16[256,512]{1,0:T(8,128)(2,1)} %bitcast.17.refs_0_), channel_id=1, source_target_pairs={{0,3},{1,0},{2,1},{3,2},{4,7},{5,4},{6,5},{7,6},{8,11},{9,8},{10,9... | collective-permute-start | bytes 786440 | tf_op jit(solution)/shard_map/ppermute | solution.py:28
  74.4 21.0 %collective-permute-start.14 = (bf16[4,2,128,128]{3,2,1,0:T(8,128)(2,1)}, bf16[4,2,128,128]{3,2,1,0:T(8,128)(2,1)S(1)}, u32[]{:S(2)}, u32[]{:S(2)}) collective-permute-start(bf16[4,2,128,128]{3,2,1,0:T(8,128)(2,1)} %get-tuple-element.35), channel_id=1, source_target_pairs={{0,64},{16,80},{32,96},{48,112},{64,128},{80,144},{96,160},{112,17... | collective-permute-start | bytes 786440 | tf_op jit(solution)/shard_map/ppermute | solution.py:34
  74.6 22.2 %collective-permute-start.15 = (bf16[4,2,128,128]{3,2,1,0:T(8,128)(2,1)}, bf16[4,2,128,128]{3,2,1,0:T(8,128)(2,1)S(1)}, u32[]{:S(2)}, u32[]{:S(2)}) collective-permute-start(bf16[4,2,128,128]{3,2,1,0:T(8,128)(2,1)} %get-tuple-element.36), channel_id=1, source_target_pairs={{0,128},{16,144},{32,160},{48,176},{64,192},{80,208},{96,224},{112... | collective-permute-start | bytes 786440 | tf_op jit(solution)/shard_map/ppermute | solution.py:34
  80.6 16.2 %collective-permute-start.16 = (bf16[4,2,128,128]{3,2,1,0:T(8,128)(2,1)}, bf16[4,2,128,128]{3,2,1,0:T(8,128)(2,1)S(1)}, u32[]{:S(2)}, u32[]{:S(2)}) collective-permute-start(bf16[4,2,128,128]{3,2,1,0:T(8,128)(2,1)} %get-tuple-element.37), channel_id=1, source_target_pairs={{0,192},{16,208},{32,224},{48,240},{64,0},{80,16},{96,32},{112,48}... | collective-permute-start | bytes 786440 | tf_op jit(solution)/shard_map/ppermute | solution.py:34
  80.6 7.9 %copy-start.8 = (bf16[4,2,2,256,256]{4,3,2,1,0:T(8,128)(2,1)}, bf16[4,2,2,256,256]{4,3,2,1,0:T(8,128)(2,1)S(1)}, u32[]{:S(2)}) copy-start(bf16[4,2,2,256,256]{4,3,2,1,0:T(8,128)(2,1)S(1)} %all-to-all-done.sent) | copy-start | bytes 6291460
  80.6 37.9 %all-to-all-start.2 = ((bf16[4,2,2,256,256]{4,3,2,1,0:T(8,128)(2,1)}), bf16[4,2,2,256,256]{4,3,2,1,0:T(8,128)(2,1)}, u32[]{:S(2)}, u32[]{:S(2)}) async-start(bf16[4,2,2,256,256]{4,3,2,1,0:T(8,128)(2,1)} %pack.3), calls=%async_computation.2 | async-start | bytes 4194304 | tf_op jit(solution)/shard_map/all_to_all | solution.py:42
  88.5 8.3 %copy-start.2 = (bf16[4,2,128,128]{3,2,1,0:T(8,128)(2,1)S(1)}, bf16[4,2,128,128]{3,2,1,0:T(8,128)(2,1)}, u32[]{:S(2)}) copy-start(bf16[4,2,128,128]{3,2,1,0:T(8,128)(2,1)} %get-tuple-element.41.refs_0_) | copy-start | bytes 786436
  88.5 8.3 %copy-start.5 = (s32[4]{0:T(128)S(1)}, s32[4]{0:T(128)}, u32[]{:S(2)}) copy-start(s32[4]{0:T(128)} %pad_add_fusion.w) | copy-start | bytes 52
  95.4 14.1 %collective-permute-start.12 = (bf16[256,512]{1,0:T(8,128)(2,1)}, bf16[256,512]{1,0:T(8,128)(2,1)S(1)}, u32[]{:S(2)}, u32[]{:S(2)}) collective-permute-start(bf16[256,512]{1,0:T(8,128)(2,1)} %bitcast.17.refs_0_), channel_id=1, source_target_pairs={{0,1},{1,2},{2,3},{3,0},{4,5},{5,6},{6,7},{7,4},{8,9},{9,10},{10,1... | collective-permute-start | bytes 786440 | tf_op jit(solution)/shard_map/ppermute | solution.py:28
  97.4 0.7 copy-start.1
  98.1 19.1 %collective-permute-start.18 = (bf16[4,2,128,128]{3,2,1,0:T(8,128)(2,1)S(1)}, bf16[4,2,128,128]{3,2,1,0:T(8,128)(2,1)S(1)}, u32[]{:S(2)}, u32[]{:S(2)}) collective-permute-start(bf16[4,2,128,128]{3,2,1,0:T(8,128)(2,1)S(1)} %get-tuple-element.42), channel_id=1, source_target_pairs={{0,48},{16,0},{32,16},{48,32},{64,112},{80,64},{96,80},{112,96},{1... | collective-permute-start | bytes 786440 | tf_op jit(solution)/shard_map/ppermute | solution.py:38
  101.3 21.4 %collective-permute-start.19 = (bf16[4,2,128,128]{3,2,1,0:T(8,128)(2,1)S(1)}, bf16[4,2,128,128]{3,2,1,0:T(8,128)(2,1)}, u32[]{:S(2)}, u32[]{:S(2)}) collective-permute-start(bf16[4,2,128,128]{3,2,1,0:T(8,128)(2,1)S(1)} %get-tuple-element.43), channel_id=1, source_target_pairs={{0,32},{16,48},{32,0},{48,16},{64,96},{80,112},{96,64},{112,80},{1... | collective-permute-start | bytes 786440 | tf_op jit(solution)/shard_map/ppermute | solution.py:38
  102.5 21.5 %collective-permute-start.20 = (bf16[4,2,128,128]{3,2,1,0:T(8,128)(2,1)S(1)}, bf16[4,2,128,128]{3,2,1,0:T(8,128)(2,1)S(1)}, u32[]{:S(2)}, u32[]{:S(2)}) collective-permute-start(bf16[4,2,128,128]{3,2,1,0:T(8,128)(2,1)S(1)} %get-tuple-element.44), channel_id=1, source_target_pairs={{0,16},{16,32},{32,48},{48,0},{64,80},{80,96},{96,112},{112,64},{1... | collective-permute-start | bytes 786440 | tf_op jit(solution)/shard_map/ppermute | solution.py:38
  109.5 0.7 copy-start.16
  116.9 27.1 %collective-permute-start.21 = (bf16[256,512]{1,0:T(8,128)(2,1)}, bf16[256,512]{1,0:T(8,128)(2,1)S(1)}, u32[]{:S(2)}, u32[]{:S(2)}) collective-permute-start(bf16[256,512]{1,0:T(8,128)(2,1)} %get-tuple-element.50), channel_id=1, source_target_pairs={{0,3},{1,0},{2,1},{3,2},{4,7},{5,4},{6,5},{7,6},{8,11},{9,8},{10,9... | collective-permute-start | bytes 786440 | tf_op jit(solution)/shard_map/ppermute | solution.py:28
  117.2 0.7 copy-start.10
  118.5 25.5 %all-to-all-start.1 = ((bf16[4,2,2,256,256]{4,3,2,1,0:T(8,128)(2,1)}), bf16[4,2,2,256,256]{4,3,2,1,0:T(8,128)(2,1)S(1)}, u32[]{:S(2)}, u32[]{:S(2)}) async-start(bf16[4,2,2,256,256]{4,3,2,1,0:T(8,128)(2,1)} %get-tuple-element.38), calls=%async_computation.1 | async-start | bytes 4194304 | tf_op jit(solution)/shard_map/all_to_all | solution.py:42
  122.8 83.9 %all-gather.4.cloned.1.call-start = ((), (), s32[]{:S(2)}) async-start(), calls=%async_computation.4 | async-start | bytes 4456448 | tf_op jit(solution)/shard_map/all_gather | solution.py:353
  124.0 7.3 %copy-start.11 = (bf16[4,2,128,128]{3,2,1,0:T(8,128)(2,1)}, bf16[4,2,128,128]{3,2,1,0:T(8,128)(2,1)S(1)}, u32[]{:S(2)}) copy-start(bf16[4,2,128,128]{3,2,1,0:T(8,128)(2,1)S(1)} %collective-permute-done.20.t3) | copy-start | bytes 786436
  131.4 33.3 %copy-start = (f32[256,512]{1,0:T(8,128)S(1)}, f32[256,512]{1,0:T(8,128)}, u32[]{:S(2)}) copy-start(f32[256,512]{1,0:T(8,128)} %get-tuple-element.49.a) | copy-start | bytes 1572868
  138.2 18.0 %collective-permute-start.23 = (bf16[256,512]{1,0:T(8,128)(2,1)}, bf16[256,512]{1,0:T(8,128)(2,1)S(1)}, u32[]{:S(2)}, u32[]{:S(2)}) collective-permute-start(bf16[256,512]{1,0:T(8,128)(2,1)} %get-tuple-element.52), channel_id=1, source_target_pairs={{0,2},{1,3},{2,0},{3,1},{4,6},{5,7},{6,4},{7,5},{8,10},{9,11},{10,... | collective-permute-start | bytes 786440 | tf_op jit(solution)/shard_map/ppermute | solution.py:28
  142.2 22.4 %collective-permute-start.22 = (bf16[256,512]{1,0:T(8,128)(2,1)}, bf16[256,512]{1,0:T(8,128)(2,1)S(1)}, u32[]{:S(2)}, u32[]{:S(2)}) collective-permute-start(bf16[256,512]{1,0:T(8,128)(2,1)} %get-tuple-element.51), channel_id=1, source_target_pairs={{0,1},{1,2},{2,3},{3,0},{4,5},{5,6},{6,7},{7,4},{8,9},{9,10},{10,1... | collective-permute-start | bytes 786440 | tf_op jit(solution)/shard_map/ppermute | solution.py:28
  144.0 47.5 %copy-start.7 = (bf16[4,2,2,256,256]{4,3,2,1,0:T(8,128)(2,1)}, bf16[4,2,2,256,256]{4,3,2,1,0:T(8,128)(2,1)S(1)}, u32[]{:S(2)}) copy-start(bf16[4,2,2,256,256]{4,3,2,1,0:T(8,128)(2,1)S(1)} %all-to-all-done.1.refs_0_) | copy-start | bytes 6291460
Sparse Core Ops, SparseCore 0:
  9.8 48.9 all-gather.5
  165.6 41.0 all-gather.3

commit v4 on v3

--- a/solution.py
+++ b/solution.py
@@ -15,7 +15,7 @@
 PARAMS = pltpu.CompilerParams(vmem_limit_bytes=60 << 20)
 ANY = pl.BlockSpec(memory_space=pl.ANY)
 ORDER = (0, 1, 3, 2)
-PARTS = ((0, 0, 1), (0, 1, 1), (1, 0, 1), (1, 1, 1))
+PARTS = ((0, 0), (0, 1), (1, 0), (1, 1))
 
 
 def x_shift(a, k):
@@ -56,7 +56,7 @@
     return pl.BlockSpec(shape, lambda *_: (0,) * len(shape))
 
 
-def call(body, scalars, grid, in_specs, out_specs, out_shape, name, cost, scratch=(), alias=()):
+def call(body, scalars, grid, in_specs, out_specs, out_shape, name, cost, scratch=(), alias=(), params=PARAMS):
     return pl.pallas_call(
         body,
         grid_spec=pltpu.PrefetchScalarGridSpec(
@@ -69,12 +69,12 @@
         out_shape=out_shape,
         input_output_aliases=dict(alias),
         cost_estimate=pl.CostEstimate(flops=cost[0], bytes_accessed=cost[1], transcendentals=0),
-        compiler_params=PARAMS,
+        compiler_params=params,
         name=name,
     )
 
 
-def small(body, scalars, arrays, after, out_shape, name):
+def small(body, scalars, arrays, after, out_shape, name, cost=1 << 19):
     here = pl.BlockSpec(memory_space=pltpu.VMEM)
     return pl.pallas_call(
         body,
@@ -82,7 +82,7 @@
         + [here] * len(arrays) + [ANY] * len(after),
         out_specs=jax.tree.map(lambda _: here, out_shape),
         out_shape=out_shape,
-        cost_estimate=pl.CostEstimate(flops=0, bytes_accessed=1 << 19, transcendentals=0),
+        cost_estimate=pl.CostEstimate(flops=0, bytes_accessed=cost, transcendentals=0),
         compiler_params=pltpu.CompilerParams(vmem_limit_bytes=16 << 20),
         name=name,
     )(*scalars, *arrays, *after)
@@ -103,17 +103,18 @@
     return small(body, (where, src), near, (), [one] * N, "text_to_send")
 
 
-def text_that_came(where, src, came):
+def text_that_came(where, src, came, after):
     def body(w, src, *refs):
+        out = refs[-1]
         at = minus(w[2], src[w[2] * N + w[3]] // N)
         for k in range(N):
 
             @pl.when(at == k)
             def _(k=k):
-                refs[N][...] = refs[k][...]
+                out[...] = refs[k][...]
 
     one = jax.ShapeDtypeStruct((2, 128, 128), BF)
-    return small(body, (where, src), came, (), one, "text_that_came")
+    return small(body, (where, src), came, after, one, "text_that_came")
 
 
 def tiny(a):
@@ -135,7 +136,7 @@
         body, (where,), (256 // rows,),
         [pl.BlockSpec((rows, 4096), lambda i, w: (i, 0))] * 2 + [ANY] * len(after),
         pl.BlockSpec((N, 2, len(order), rows, 256), lambda i, w: (0, 0, 0, i, 0)),
-        jax.ShapeDtypeStruct((N, 2, len(order), 256, 256), BF), "pack", (0, 6 << 20),
+        jax.ShapeDtypeStruct((N, 2, len(order), 256, 256), BF), "pack", (0, 18 << 20),
     )(where, queries, grad_out, *after)
 
 
@@ -175,25 +176,16 @@
         [whole((2, 128, 512))] + [whole(quarter)] * N,
         [jax.ShapeDtypeStruct((2, 128, 512), BF)] + [jax.ShapeDtypeStruct(quarter, BF)] * N,
         "project", (2 * 256 * 2048 * 512, 6 << 20), [pltpu.VMEM((2, 128, 512), F32)],
+        params=pltpu.CompilerParams(vmem_limit_bytes=16 << 20),
     )(where, *pieces, weight.reshape(N, N, 2, 128, 512))
     return kv.reshape(256, 512), rows
 
 
-def attend(order, first, where, src, lengths, moved, kvs, into, wait):
-    count = len(order)
+def attend(m, piece, where, src, lengths, moved, kv, into, wait):
     scale = 1.0 / math.sqrt(HEAD)
 
-    def body(w, src, lengths, sent, *refs):
-        kvs, kv, total = refs[:count], refs[-2], refs[-1]
-        out, grads = refs[-3 - count], refs[-2 - count : -2]
-        p = pl.program_id(0)
-        cols = pl.ds(pl.multiple_of(pl.program_id(1) * 256, 256), 256)
-        for i in range(count):
-
-            @pl.when(p == i)
-            def _(i=i):
-                kv[...] = kvs[i][:, cols]
-
+    def body(w, src, lengths, sent, kv, *refs):
+        out, grads = refs[-2:]
         sample = src[w[2] * N + w[3]]
         row = lax.broadcasted_iota(jnp.int32, (256, 256), 0)
         valid = row < jnp.where(row < 128, lengths[2 * sample], lengths[2 * sample + 1] + 128)
@@ -215,38 +207,39 @@
             dv = dot(low, g, ((1,), (0,)))
             grad_key = dk if x == 0 else grad_key + dk
             grad_value = dv if x == 0 else grad_value + dv
-        total[:, :HEAD] = grad_key
-        total[:, HEAD:] = grad_value
-        for i in range(count):
-
-            @pl.when(p == i)
-            def _(i=i):
-                grads[i][:, cols] = total[...].astype(grads[i].dtype)
-
-    res = call(
-        body, (where, src, lengths), (count, 2),
-        [pl.BlockSpec((N, 2, 1, 256, HEAD), lambda p, l, *_: (0, 0, p + first, 0, l))]
-        + [whole((256, 512))] * count + [ANY] * (len(into) + len(wait)),
-        [pl.BlockSpec((N, 2, 1, 256, HEAD), lambda p, l, *_: (0, 0, p + first, 0, l))]
-        + [whole((256, 512))] * count,
-        [jax.ShapeDtypeStruct((N, 2, 2, 256, 256), BF)]
-        + [
-            jax.ShapeDtypeStruct((256, 512), BF if m else F32)
-            for m in order
+        grads[:, :HEAD] = grad_key.astype(grads.dtype)
+        grads[:, HEAD:] = grad_value.astype(grads.dtype)
+
+    by_head = pl.BlockSpec((N, 2, 1, 256, HEAD), lambda l, *_: (0, 0, piece, 0, l))
+    columns = pl.BlockSpec((256, 256), lambda l, *_: (0, l))
+    return call(
+        body, (where, src, lengths), (2,),
+        [by_head, columns] + [ANY] * (len(into) + len(wait)),
+        [by_head, columns],
+        [
+            jax.ShapeDtypeStruct((N, 2, 2, 256, 256), BF),
+            jax.ShapeDtypeStruct((256, 512), BF if m else F32),
         ],
-        "attend", (count * 6_000_000_000, (4 << 20) * count),
-        [pltpu.VMEM((256, 256), BF), pltpu.VMEM((256, 256), F32)],
-        {4 + count: 0} if into else {},
-    )(where, src, lengths, moved, *kvs, *into, *wait)
-    return res[0], res[1:]
-
-
-def add_up(own, others, after):
-    def body(a, b, c, d, *rest):
-        rest[-1][...] = (a[...] + (b[...].astype(F32) + c[...] + d[...])).astype(BF)
+        "attend", (6_000_000_000, 4 << 20), (), {5: 0} if into else {},
+    )(where, src, lengths, moved, kv, *into, *wait)
+
+
+def add_first(own, others):
+    def body(a, b, c, out):
+        out[...] = a[...] + (b[...].astype(F32) + c[...])
 
     return small(
-        body, (), [own, *others], after, jax.ShapeDtypeStruct((256, 512), BF), "add_up"
+        body, (), [own, *others], (), jax.ShapeDtypeStruct((256, 512), F32), "add_first",
+        16 << 20,
+    )
+
+
+def add_last(most, last, after):
+    def body(a, b, *rest):
+        rest[-1][...] = (a[...] + b[...]).astype(BF)
+
+    return small(
+        body, (), [most, last], after, jax.ShapeDtypeStruct((256, 512), BF), "add_last"
     )
 
 
@@ -254,7 +247,8 @@
     def body(w, *refs):
         for n in range(N):
             for k in range(N):
-                refs[N + n][k] = refs[k][minus(w[3], n)]
+                for e in range(2):
+                    refs[N + n][k, e] = refs[k][minus(w[3], n), e].T
 
     return small(
         body, (where,), came, (), [jax.ShapeDtypeStruct((N, 2, 128, 128), BF)] * N,
@@ -263,7 +257,7 @@
 
 
 def weight_gradient(where, pieces, grads):
-    def body(w, t0, t1, t2, t3, d, out):
+    def body(w, t0, t1, t2, t3, d, out, acc):
         n = pl.program_id(0)
         for i, t in enumerate((t0, t1, t2, t3)):
 
@@ -272,19 +266,21 @@
                 for e in range(2):
                     part = None
                     for k in range(N):
-                        p = dot(t[k, e], d[minus(w[2], k), 0, e], ((0,), (0,)))
+                        p = dot(t[k, e], d[minus(w[2], k), 0, e], ((1,), (0,)))
                         part = p if part is None else part + p
                     if i == 0:
-                        out[e] = part
+                        acc[e] = part
+                    elif i < N - 1:
+                        acc[e] += part
                     else:
-                        out[e] += part
+                        out[:, e, :] = acc[e] + part
 
     return call(
         body, (where,), (N,),
         [whole((N, 2, 128, 128))] * N
         + [pl.BlockSpec((N, 1, 2, 128, 512), lambda n, w: (0, lax.rem(w[3] + n, N), 0, 0, 0))],
-        whole((2, 128, 512)), jax.ShapeDtypeStruct((2, 128, 512), F32), "weight_gradient",
-        (2 * 256 * 2048 * 512, 6 << 20),
+        whole((128, 2, 512)), jax.ShapeDtypeStruct((128, 2, 512), F32), "weight_gradient",
+        (2 * 256 * 2048 * 512, 6 << 20), [pltpu.VMEM((2, 128, 512), F32)],
     )(where, *pieces, grads.reshape(N, N, 2, 128, 512))
 
 
@@ -317,43 +313,42 @@
 
     weight = lax.all_gather(jnp.swapaxes(kv_weight, 0, 1), "dp", axis=0)
     near = [text] + [r_shift(text, N - n) for n in (1, 2, 3)]
-    packed = pack(ORDER[:2], where, q, g, [tiny(a) for a in near[1:]])
+    sends = text_to_send(where, src, near)
+    packed = pack(ORDER[:2], where, q, g, [tiny(sends[0])])
     moved = [exchange_x(packed)]
+    picked = text_that_came(
+        where, src, [sends[0]] + [y_shift(sends[k], k) for k in (1, 2, 3)], [tiny(packed)]
+    )
     packed = pack(ORDER[2:], where, q, g, [tiny(packed)])
-    sends = text_to_send(where, src, near)
-    picked = text_that_came(
-        where, src, [sends[0]] + [y_shift(sends[k], k) for k in (1, 2, 3)]
-    )
     along_z = jnp.stack([picked] + [z_shift(picked, n) for n in (1, 2, 3)])
     pieces = [along_z] + [x_shift(along_z, k) for k in (1, 2, 3)]
 
+    packed, *pieces = lax.optimization_barrier((packed, *pieces))
+    moved.append(exchange_x(packed))
     kv, rows = project(where, pieces, weight)
-    packed, kv = lax.optimization_barrier((packed, kv))
-    moved.append(exchange_x(packed))
     kvs = [kv] + [z_shift(kv, m) for m in ORDER[1:]]
+
     rows = [rows[0]] + [y_shift(rows[k], k) for k in (1, 2, 3)]
     by_r = rows_to_send(where, rows)
     own_rows = [by_r[0]] + [r_shift(by_r[n], N - n) for n in (1, 2, 3)]
-    waits = ([], [kvs[2], *rows[1:]], [], own_rows[1:])
-
-    outs, grads, done = [None, None], [], 0
-    for which, first, count in PARTS:
-        part = slice(done, done + count)
+
+    outs, grads = [None, None], []
+    for i, (which, first) in enumerate(PARTS):
         into = [outs[which]] if first else []
-        wait = [tiny(a) for a in waits[done]]
+        wait = ([], [kvs[2], *rows[1:]], [], own_rows[1:])[i]
         outs[which], d = attend(
-            ORDER[part], first, where, src, lengths, moved[which], kvs[part], into, wait
+            ORDER[i], first, where, src, lengths, moved[which], kvs[i], into,
+            [tiny(a) for a in wait],
         )
-        for m, a in zip(ORDER[part], d):
-            grads.append(z_shift(a, N - m) if m else a)
-        done += count
+        grads.append(z_shift(d, N - ORDER[i]) if i else d)
 
     outs = [exchange_x(a) for a in outs]
-    total = add_up(grads[0], grads[1:], [tiny(outs[0])])
+    after = [tiny(a) for a in [outs[0]]]
+    total = add_last(add_first(grads[0], grads[1:3]), grads[3], after)
     every_grad = lax.all_gather(total.reshape(2, 128, 512), "dp", axis=0)
     grad_weight = weight_gradient(where, own_rows, every_grad)
     attended, grad_queries = place(where, outs)
-    return (attended[None], grad_queries[None], jnp.swapaxes(grad_weight, 0, 1))
+    return (attended[None], grad_queries[None], grad_weight)
 
 
 def solution(mesh):

time: 224 us -> 212 us (0.946)
  waiting for transfers between devices: 49 us -> 39.1 us
  Pallas kernels: 57.2 us -> 53.4 us
    ppermute x9, waiting for transfers between devices: 29 us -> 18.3 us  [z_shift(): lax.ppermute(a, 'ctx', [(4 * x + z, 4 * x + (z + m) % N) for x in range(N...]
    pallas_call x1, Pallas kernels: 6.19 us -> 2.63 us  [project(): call(body, (where,), (N,), [whole(quarter)] * N + [pl.BlockSpec((1, N, 2,...]
    slice x12 -> x10, local copies, waits for them, and re-layouts: 7.89 us -> 4.78 us  [tiny(): return a[(0,) * (a.ndim - 2)][:16, :128]]
    all_gather x1, waiting for transfers between devices: 9.59 us -> 6.58 us  [per_device(): every_grad = lax.all_gather(total.reshape(2, 128, 512), 'dp', axis=0)]
    unnamed x37 -> x46, local copies, waits for them, and re-layouts: 6.9 us -> 7.58 us
  transfers between devices with their start and end apart: 29 -> 29, of which waited for: 12 -> 14; matrix products, arithmetic and copies ran while one was open for 5% -> 4% of each run, Pallas kernels for 23% -> 22%
where the time goes in v4:
time: 212 us; the launch traced here: 210 us
  starting transfers between devices  60.3 us (28%)
  Pallas kernels  53.4 us (25%)
  waiting for transfers between devices  39.1 us (18%)
  blocking collectives  28.1 us (13%)
  local copies, waits for them, and re-layouts  14.9 us (7%)
  between operations  14.2 us (7%)
    all_to_all x1, blocking collectives, exchange_x(): lax.all_to_all(a, 'ctx', split_axis=0, concat_axis=0, tiled=True, axis_in...  28.1 us
    pallas_call x4, Pallas kernels, attend(): call(body, (where, src, lengths), (2,), [by_head, columns] + [ANY] * (len...  26.8 us
    ppermute x9, starting transfers between devices, z_shift(): lax.ppermute(a, 'ctx', [(4 * x + z, 4 * x + (z + m) % N) for x in range(N...  20.6 us
    ppermute x9, waiting for transfers between devices, z_shift(): lax.ppermute(a, 'ctx', [(4 * x + z, 4 * x + (z + m) % N) for x in range(N...  18.3 us
    all_to_all x3, starting transfers between devices, exchange_x(): lax.all_to_all(a, 'ctx', split_axis=0, concat_axis=0, tiled=True, axis_in...  17.9 us
    ppermute x6, starting transfers between devices, y_shift(): lax.ppermute(a, 'dp', [(i, (i // N + k) % N * N + i % N) for i in range(1...  10.8 us
    pallas_call x2, Pallas kernels, pack(): call(body, (where,), (256 // rows,), [pl.BlockSpec((rows, 4096), lambda i...  9.87 us
    unnamed x46, local copies, waits for them, and re-layouts  7.58 us
  transfers between devices with their start and end apart: 29, of which 14 were waited for; matrix products, arithmetic and copies ran while one was open for 4% of the time, Pallas kernels for 22%

profile of v4, /device:TPU:11, one launch (start us, length us, event | category | flops | bytes accessed | tf_op | source)
XLA Modules:
  0.0 210.1 jit_solution(13396815282888115502)
XLA Ops:
  7.2 1.7 copy.18
  8.9 2.3 %collective-permute-start.2 = (bf16[2,128,128]{2,1,0:T(8,128)(2,1)}, bf16[2,128,128]{2,1,0:T(8,128)(2,1)S(1)}, u32[]{:S(2)}, u32[]{:S(2)}) collective-permute-start(bf16[2,128,128]{2,1,0:T(8,128)(2,1)} %bitcast.40), channel_id=1, source_target_pairs={{0,16},{16,32},{32,48},{48,0},{64,80},{80,96},{96,112},{112,64},{1... | collective-permute-start | bytes 196616 | tf_op jit(solution)/shard_map/ppermute | solution.py:38
  11.8 1.1 collective-permute-done.2.refs_3_
  12.8 1.8 collective-permute-done.1.refs_2_
  15.2 0.8 copy-done.3
  18.0 4.9 %pack.2 = bf16[4,2,2,256,256]{4,3,2,1,0:T(8,128)(2,1)} custom-call(s32[4]{0:T(128)} %copy-done.4, bf16[256,4096]{1,0:T(8,128)(2,1)} %bitcast.48, bf16[256,4096]{1,0:T(8,128)(2,1)} %bitcast.50, bf16[16,128]{1,0:T(8,128)(2,1)} %slice_bitcast_fusion.8.rest_0_), custom_call_target="tpu_custom_call" | custom-call | bytes 18874368 | tf_op jit(solution)/shard_map/pack/pallas_call | solution.py:135
  22.9 4.9 %all-to-all-start = ((bf16[4,2,2,256,256]{4,3,2,1,0:T(8,128)(2,1)}), bf16[4,2,2,256,256]{4,3,2,1,0:T(8,128)(2,1)}, u32[]{:S(2)}, u32[]{:S(2)}) async-start(bf16[4,2,2,256,256]{4,3,2,1,0:T(8,128)(2,1)} %pack.2), calls=%async_computation | async-start | bytes 4194304 | tf_op jit(solution)/shard_map/all_to_all | solution.py:42
  27.8 1.3 collective-permute-start.3
  29.0 2.1 %collective-permute-start.4 = (bf16[2,128,128]{2,1,0:T(8,128)(2,1)S(1)}, bf16[2,128,128]{2,1,0:T(8,128)(2,1)S(1)}, u32[]{:S(2)}, u32[]{:S(2)}) collective-permute-start(bf16[2,128,128]{2,1,0:T(8,128)(2,1)S(1)} %get-tuple-element.33), channel_id=1, source_target_pairs={{0,128},{16,144},{32,160},{48,176},{64,192},{80,208},{96,224},{112... | collective-permute-start | bytes 196616 | tf_op jit(solution)/shard_map/ppermute | solution.py:34
  31.8 0.9 slice_bitcast_fusion.1
  33.1 2.3 %collective-permute-done.4.refs_2_ = bf16[2,128,128]{2,1,0:T(8,128)(2,1)S(1)} collective-permute-done((bf16[2,128,128]{2,1,0:T(8,128)(2,1)S(1)}, bf16[2,128,128]{2,1,0:T(8,128)(2,1)S(1)}, u32[]{:S(2)}, u32[]{:S(2)}) %collective-permute-start.4) | collective-permute-done | bytes 65568 | tf_op jit(solution)/shard_map/ppermute | solution.py:34
  35.5 1.7 collective-permute-done.5.refs_3_
  37.7 5.1 %collective-permute-start.8 = (bf16[2,128,128]{2,1,0:T(8,128)(2,1)S(1)}, bf16[2,128,128]{2,1,0:T(8,128)(2,1)S(1)}, u32[]{:S(2)}, u32[]{:S(2)}) collective-permute-start(bf16[2,128,128]{2,1,0:T(8,128)(2,1)S(1)} %text_that_came.1), channel_id=1, source_target_pairs={{0,3},{1,0},{2,1},{3,2},{4,7},{5,4},{6,5},{7,6},{8,11},{9,8},{10,9... | collective-permute-start | bytes 196616 | tf_op jit(solution)/shard_map/ppermute | solution.py:28
  42.8 1.1 collective-permute-start.7
  43.9 2.3 %collective-permute-start.6 = (bf16[2,128,128]{2,1,0:T(8,128)(2,1)S(1)}, bf16[2,128,128]{2,1,0:T(8,128)(2,1)S(1)}, u32[]{:S(2)}, u32[]{:S(2)}) collective-permute-start(bf16[2,128,128]{2,1,0:T(8,128)(2,1)S(1)} %text_that_came.1), channel_id=1, source_target_pairs={{0,1},{1,2},{2,3},{3,0},{4,5},{5,6},{6,7},{7,4},{8,9},{9,10},{10,1... | collective-permute-start | bytes 196616 | tf_op jit(solution)/shard_map/ppermute | solution.py:28
  46.2 3.8 %collective-permute-done.7 = bf16[2,128,128]{2,1,0:T(8,128)(2,1)S(1)} collective-permute-done((bf16[2,128,128]{2,1,0:T(8,128)(2,1)S(1)}, bf16[2,128,128]{2,1,0:T(8,128)(2,1)S(1)}, u32[]{:S(2)}, u32[]{:S(2)}) %collective-permute-start.7) | collective-permute-done | bytes 65568 | tf_op jit(solution)/shard_map/ppermute | solution.py:28
  49.9 1.2 collective-permute-done.6
  51.5 2.2 %collective-permute-start.10 = (bf16[4,2,128,128]{3,2,1,0:T(8,128)(2,1)S(1)}, bf16[4,2,128,128]{3,2,1,0:T(8,128)(2,1)S(1)}, u32[]{:S(2)}, u32[]{:S(2)}) collective-permute-start(bf16[4,2,128,128]{3,2,1,0:T(8,128)(2,1)S(1)} %pad_maximum_fusion.t0), channel_id=1, source_target_pairs={{0,8},{1,9},{2,10},{3,11},{4,12},{5,13},{6,14},{7,15},{8,0},{9,1},... | collective-permute-start | bytes 786440 | tf_op jit(solution)/shard_map/ppermute | solution.py:22
  53.7 1.8 collective-permute-start.9
  56.3 5.0 %pack.3 = bf16[4,2,2,256,256]{4,3,2,1,0:T(8,128)(2,1)} custom-call(s32[4]{0:T(128)} %copy-done.4, bf16[256,4096]{1,0:T(8,128)(2,1)} %bitcast.49, bf16[256,4096]{1,0:T(8,128)(2,1)} %bitcast.51, bf16[16,128]{1,0:T(8,128)(2,1)} %copy-done.8), custom_call_target="tpu_custom_call" | custom-call | bytes 18874368 | tf_op jit(solution)/shard_map/pack/pallas_call | solution.py:135
  61.3 2.4 %collective-permute-done.10.t2 = bf16[4,2,128,128]{3,2,1,0:T(8,128)(2,1)S(1)} collective-permute-done((bf16[4,2,128,128]{3,2,1,0:T(8,128)(2,1)S(1)}, bf16[4,2,128,128]{3,2,1,0:T(8,128)(2,1)S(1)}, u32[]{:S(2)}, u32[]{:S(2)}) %collective-permute-start.10) | collective-permute-done | bytes 262176 | tf_op jit(solution)/shard_map/ppermute | solution.py:22
  63.7 1.5 collective-permute-done.9.t1
  65.2 2.2 %copy-done = bf16[32,128,512]{2,1,0:T(8,128)(2,1)S(1)} copy-done((bf16[32,128,512]{2,1,0:T(8,128)(2,1)S(1)}, bf16[32,128,512]{2,1,0:T(8,128)(2,1)}, u32[]{:S(2)}) %copy-start) | copy-done | bytes 4194328
  67.4 2.6 %project.1 = (bf16[2,128,512]{2,1,0:T(8,128)(2,1)S(1)}, bf16[4,2,128,128]{3,2,1,0:T(8,128)(2,1)S(1)}, bf16[4,2,128,128]{3,2,1,0:T(8,128)(2,1)S(1)}, bf16[4,2,128...) custom-call(s32[4]{0:T(128)S(1)} %copy-done.6, bf16[4,2,128,128]{3,2,1,0:T(8,128)(2,1)S(1)} %pad_maximum_fusion.t0, ...), custom_call_target="tpu_custom_call" | custom-call | flops 536870912 | bytes 6291456 | tf_op jit(solution)/shard_map/project/pallas_call | solution.py:173
  70.0 5.4 %collective-permute-start.17 = (bf16[256,512]{1,0:T(8,128)(2,1)S(1)}, bf16[256,512]{1,0:T(8,128)(2,1)S(1)}, u32[]{:S(2)}, u32[]{:S(2)}) collective-permute-start(bf16[256,512]{1,0:T(8,128)(2,1)S(1)} %bitcast.44), channel_id=1, source_target_pairs={{0,2},{1,3},{2,0},{3,1},{4,6},{5,7},{6,4},{7,5},{8,10},{9,11},{10,... | collective-permute-start | bytes 786440 | tf_op jit(solution)/shard_map/ppermute | solution.py:28
  75.4 1.7 collective-permute-start.14
  77.1 5.0 %collective-permute-start.15 = (bf16[4,2,128,128]{3,2,1,0:T(8,128)(2,1)S(1)}, bf16[4,2,128,128]{3,2,1,0:T(8,128)(2,1)S(1)}, u32[]{:S(2)}, u32[]{:S(2)}) collective-permute-start(bf16[4,2,128,128]{3,2,1,0:T(8,128)(2,1)S(1)} %get-tuple-element.42), channel_id=1, source_target_pairs={{0,128},{16,144},{32,160},{48,176},{64,192},{80,208},{96,224},{112... | collective-permute-start | bytes 786440 | tf_op jit(solution)/shard_map/ppermute | solution.py:34
  82.2 7.8 %all-to-all-start.2 = ((bf16[4,2,2,256,256]{4,3,2,1,0:T(8,128)(2,1)}), bf16[4,2,2,256,256]{4,3,2,1,0:T(8,128)(2,1)}, u32[]{:S(2)}, u32[]{:S(2)}) async-start(bf16[4,2,2,256,256]{4,3,2,1,0:T(8,128)(2,1)} %pack.3), calls=%async_computation.2 | async-start | bytes 4194304 | tf_op jit(solution)/shard_map/all_to_all | solution.py:42
  90.0 6.8 %attend.4 = (bf16[4,2,2,256,256]{4,3,2,1,0:T(8,128)(2,1)}, f32[256,512]{1,0:T(8,128)}) custom-call(s32[4]{0:T(128)} %copy-done.4, s32[16]{0:T(128)} %src.11, s32[32]{0:T(128)} %reshape.25.lengths, bf16[4,2,2,256,256]{4,3,2,1,0:T(8,128)(2,1)} %all-to-all-done.sent, bf16[256,512]{1,0:T(8,128)(2,1)} %bitcast.46), custom_call_target="tpu_custom_call" | custom-call | flops 6000000000 | bytes 4194304 | tf_op jit(solution)/shard_map/attend/pallas_call | solution.py:215
  96.8 1.5 collective-permute-start.12
  98.3 0.9 rows_to_send.1
  99.9 2.2 %collective-permute-start.18 = (bf16[4,2,128,128]{3,2,1,0:T(8,128)(2,1)S(1)}, bf16[4,2,128,128]{3,2,1,0:T(8,128)(2,1)S(1)}, u32[]{:S(2)}, u32[]{:S(2)}) collective-permute-start(bf16[4,2,128,128]{3,2,1,0:T(8,128)(2,1)S(1)} %get-tuple-element.48), channel_id=1, source_target_pairs={{0,48},{16,0},{32,16},{48,32},{64,112},{80,64},{96,80},{112,96},{1... | collective-permute-start | bytes 786440 | tf_op jit(solution)/shard_map/ppermute | solution.py:38
  103.2 1.6 collective-permute-start.20
  106.0 3.1 %collective-permute-done.12.kv = bf16[256,512]{1,0:T(8,128)(2,1)S(1)} collective-permute-done((bf16[256,512]{1,0:T(8,128)(2,1)S(1)}, bf16[256,512]{1,0:T(8,128)(2,1)S(1)}, u32[]{:S(2)}, u32[]{:S(2)}) %collective-permute-start.12) | collective-permute-done | bytes 262176 | tf_op jit(solution)/shard_map/ppermute | solution.py:28
  109.8 6.6 %attend.5 = (bf16[4,2,2,256,256]{4,3,2,1,0:T(8,128)(2,1)}, bf16[256,512]{1,0:T(8,128)(2,1)}) custom-call(s32[4]{0:T(128)} %copy-done.4, s32[16]{0:T(128)} %src.11, s32[32]{0:T(128)} %reshape.25.lengths, bf16[4,2,2,256,256]{4,3,2,1,0:T(8,128)(2,1)} %all-to-all-done.sent, bf16[256,512]{1,0:T(8,128)(2,1)} %copy-done.21, ...), custom_call_target="tpu_custom_call", output_to_operand_aliasing={{0}: (5, {})} | custom-call | flops 6000000000 | bytes 4194304 | tf_op jit(solution)/shard_map/attend/pallas_call | solution.py:215
  116.4 5.2 %all-to-all-start.1 = ((bf16[4,2,2,256,256]{4,3,2,1,0:T(8,128)(2,1)}), bf16[4,2,2,256,256]{4,3,2,1,0:T(8,128)(2,1)}, u32[]{:S(2)}, u32[]{:S(2)}) async-start(bf16[4,2,2,256,256]{4,3,2,1,0:T(8,128)(2,1)} %get-tuple-element.44), calls=%async_computation.1 | async-start | bytes 4194304 | tf_op jit(solution)/shard_map/all_to_all | solution.py:42
  121.6 6.7 %attend.6 = (bf16[4,2,2,256,256]{4,3,2,1,0:T(8,128)(2,1)}, bf16[256,512]{1,0:T(8,128)(2,1)}) custom-call(s32[4]{0:T(128)} %copy-done.4, s32[16]{0:T(128)} %src.11, s32[32]{0:T(128)} %reshape.25.lengths, bf16[4,2,2,256,256]{4,3,2,1,0:T(8,128)(2,1)} %all-to-all-done.2.sent, bf16[256,512]{1,0:T(8,128)(2,1)} %copy-done.18), custom_call_target="tpu_custom_call" | custom-call | flops 6000000000 | bytes 4194304 | tf_op jit(solution)/shard_map/attend/pallas_call | solution.py:215
  128.3 1.5 collective-permute-start.22
  129.8 2.4 %collective-permute-start.21 = (bf16[256,512]{1,0:T(8,128)(2,1)S(1)}, bf16[256,512]{1,0:T(8,128)(2,1)S(1)}, u32[]{:S(2)}, u32[]{:S(2)}) collective-permute-start(bf16[256,512]{1,0:T(8,128)(2,1)S(1)} %copy-done.20), channel_id=1, source_target_pairs={{0,3},{1,0},{2,1},{3,2},{4,7},{5,4},{6,5},{7,6},{8,11},{9,8},{10,9... | collective-permute-start | bytes 786440 | tf_op jit(solution)/shard_map/ppermute | solution.py:28
  134.7 6.7 %attend.7 = (bf16[4,2,2,256,256]{4,3,2,1,0:T(8,128)(2,1)}, bf16[256,512]{1,0:T(8,128)(2,1)}) custom-call(s32[4]{0:T(128)} %copy-done.4, s32[16]{0:T(128)} %src.11, s32[32]{0:T(128)} %reshape.25.lengths, bf16[4,2,2,256,256]{4,3,2,1,0:T(8,128)(2,1)} %all-to-all-done.2.sent, bf16[256,512]{1,0:T(8,128)(2,1)} %copy-done.19, ...), custom_call_target="tpu_custom_call", output_to_operand_aliasing={{0}: (5, {})} | custom-call | flops 6000000000 | bytes 4194304 | tf_op jit(solution)/shard_map/attend/pallas_call | solution.py:215
  141.4 1.5 collective-permute-start.23
  143.0 2.4 %all-to-all-done.1.refs_0_ = bf16[4,2,2,256,256]{4,3,2,1,0:T(8,128)(2,1)} async-done(((bf16[4,2,2,256,256]{4,3,2,1,0:T(8,128)(2,1)}), bf16[4,2,2,256,256]{4,3,2,1,0:T(8,128)(2,1)}, u32[]{:S(2)}, u32[]{:S(2)}) %all-to-all-start.1) | async-done | bytes 2097184 | tf_op jit(solution)/shard_map/all_to_all | solution.py:42
  145.4 0.9 slice_bitcast_fusion
  146.3 10.3 %collective-permute-done.23.b = bf16[256,512]{1,0:T(8,128)(2,1)S(1)} collective-permute-done((bf16[256,512]{1,0:T(8,128)(2,1)}, bf16[256,512]{1,0:T(8,128)(2,1)S(1)}, u32[]{:S(2)}, u32[]{:S(2)}) %collective-permute-start.23) | collective-permute-done | bytes 262176 | tf_op jit(solution)/shard_map/ppermute | solution.py:28
  157.4 28.1 %all_to_all.20.refs_1_ = bf16[4,2,2,256,256]{4,3,2,1,0:T(8,128)(2,1)} all-to-all(bf16[4,2,2,256,256]{4,3,2,1,0:T(8,128)(2,1)S(1)} %copy-done.13), channel_id=1, replica_groups={{0,4,8,12},{1,5,9,13},{2,6,10,14},{3,7,11,15},{16,20,24,28},{17,21,25,2..., dimensions={0} | all-to-all | bytes 4194304 | tf_op jit(solution)/shard_map/all_to_all | solution.py:42
  185.5 5.5 %place.1 = (bf16[256,4096]{1,0:T(8,128)(2,1)}, bf16[256,4096]{1,0:T(8,128)(2,1)}) custom-call(s32[4]{0:T(128)} %copy-done.4, bf16[4,2,2,256,256]{4,3,2,1,0:T(8,128)(2,1)} %all-to-all-done.1.refs_0_, bf16[4,2,2,256,256]{4,3,2,1,0:T(8,128)(2,1)} %all_to_all.20.refs_1_), custom_call_target="tpu_custom_call" | custom-call | bytes 8388608 | tf_op jit(solution)/shard_map/place/pallas_call | solution.py:299
  191.0 6.6 %all-gather.4.cloned.1.call-done = bf16[16,2,128,512]{3,2,1,0:T(8,128)(2,1)} async-done(((bf16[1,2,128,512]{3,2,1,0:T(8,128)(2,1)}), bf16[16,2,128,512]{3,2,1,0:T(8,128)(2,1)}) %all-gather.4.cloned.1.call-update) | async-done | bytes 4194320 | tf_op jit(solution)/shard_map/all_gather | solution.py:348
  197.6 5.7 %weight_gradient.1 = f32[128,2,512]{2,1,0:T(2,128)} custom-call(s32[4]{0:T(128)} %copy-done.4, bf16[4,2,128,128]{3,2,1,0:T(8,128)(2,1)} %copy-done.2, bf16[4,2,128,128]{3,2,1,0:T(8,128)(2,1)} %copy-done.14, bf16[4,2,128,128]{3,2,1,0:T(8,128)(2,1)} %copy-done.15, bf16[4,2,128,128]{3,2,1,0:T(8,128)(2,1)} %copy-done.16, bf16[4,4,2,128,512]{4,3,2,1,0:T(8,128)(2,1)} %bitcast.52), custom_call_target="tpu_custom_call" | custom-call | flops 536870912 | bytes 6291456 | tf_op jit(solution)/shard_map/weight_gradient/pallas_call | solution.py:278
  (88 shorter events, 13.0 us)
Async XLA Ops:
  7.2 58.0 %all-gather.6.cloned.1.call-start = ((), (), s32[]{:S(2)}) async-start(), calls=%async_computation.5 | async-start | bytes 4456448 | tf_op jit(solution)/shard_map/all_gather | solution.py:314
  8.9 3.9 %collective-permute-start.2 = (bf16[2,128,128]{2,1,0:T(8,128)(2,1)}, bf16[2,128,128]{2,1,0:T(8,128)(2,1)S(1)}, u32[]{:S(2)}, u32[]{:S(2)}) collective-permute-start(bf16[2,128,128]{2,1,0:T(8,128)(2,1)} %bitcast.40), channel_id=1, source_target_pairs={{0,16},{16,32},{32,48},{48,0},{64,80},{80,96},{96,112},{112,64},{1... | collective-permute-start | bytes 196616 | tf_op jit(solution)/shard_map/ppermute | solution.py:38
  11.2 3.5 %collective-permute-start.1 = (bf16[2,128,128]{2,1,0:T(8,128)(2,1)}, bf16[2,128,128]{2,1,0:T(8,128)(2,1)S(1)}, u32[]{:S(2)}, u32[]{:S(2)}) collective-permute-start(bf16[2,128,128]{2,1,0:T(8,128)(2,1)} %bitcast.41), channel_id=1, source_target_pairs={{0,32},{16,48},{32,0},{48,16},{64,96},{80,112},{96,64},{112,80},{1... | collective-permute-start | bytes 196616 | tf_op jit(solution)/shard_map/ppermute | solution.py:38
  11.2 4.0 %collective-permute-start = (bf16[2,128,128]{2,1,0:T(8,128)(2,1)}, bf16[2,128,128]{2,1,0:T(8,128)(2,1)S(1)}, u32[]{:S(2)}, u32[]{:S(2)}) collective-permute-start(bf16[2,128,128]{2,1,0:T(8,128)(2,1)} %bitcast.42), channel_id=1, source_target_pairs={{0,48},{16,0},{32,16},{48,32},{64,112},{80,64},{96,80},{112,96},{1... | collective-permute-start | bytes 196616 | tf_op jit(solution)/shard_map/ppermute | solution.py:38
  11.8 6.2 %copy-start.4 = (s32[4]{0:T(128)}, s32[4]{0:T(128)S(1)}, u32[]{:S(2)}) copy-start(s32[4]{0:T(128)S(1)} %pad_add_fusion.w) | copy-start | bytes 52
  15.2 0.8 copy-start.3
  22.9 14.3 %copy-start.5 = (s32[4]{0:T(128)S(1)}, s32[4]{0:T(128)}, u32[]{:S(2)}) copy-start(s32[4]{0:T(128)} %copy-done.4) | copy-start | bytes 52
  22.9 14.3 %copy-start.10 = (s32[16]{0:T(128)S(1)}, s32[16]{0:T(128)}, u32[]{:S(2)}) copy-start(s32[16]{0:T(128)} %src.11) | copy-start | bytes 196
  22.9 32.6 %copy-start.17 = (s32[16,2]{0,1:T(2,128)S(1)}, s32[16,2]{0,1:T(2,128)}, u32[]{:S(2)}) copy-start(s32[16,2]{0,1:T(2,128)} %param.8) | copy-start | bytes 388
  22.9 59.3 %all-to-all-start = ((bf16[4,2,2,256,256]{4,3,2,1,0:T(8,128)(2,1)}), bf16[4,2,2,256,256]{4,3,2,1,0:T(8,128)(2,1)}, u32[]{:S(2)}, u32[]{:S(2)}) async-start(bf16[4,2,2,256,256]{4,3,2,1,0:T(8,128)(2,1)} %pack.2), calls=%async_computation | async-start | bytes 4194304 | tf_op jit(solution)/shard_map/all_to_all | solution.py:42
  27.8 5.4 %collective-permute-start.3 = (bf16[2,128,128]{2,1,0:T(8,128)(2,1)S(1)}, bf16[2,128,128]{2,1,0:T(8,128)(2,1)S(1)}, u32[]{:S(2)}, u32[]{:S(2)}) collective-permute-start(bf16[2,128,128]{2,1,0:T(8,128)(2,1)S(1)} %get-tuple-element.32), channel_id=1, source_target_pairs={{0,64},{16,80},{32,96},{48,112},{64,128},{80,144},{96,160},{112,17... | collective-permute-start | bytes 196616 | tf_op jit(solution)/shard_map/ppermute | solution.py:34
  29.0 6.4 %collective-permute-start.4 = (bf16[2,128,128]{2,1,0:T(8,128)(2,1)S(1)}, bf16[2,128,128]{2,1,0:T(8,128)(2,1)S(1)}, u32[]{:S(2)}, u32[]{:S(2)}) collective-permute-start(bf16[2,128,128]{2,1,0:T(8,128)(2,1)S(1)} %get-tuple-element.33), channel_id=1, source_target_pairs={{0,128},{16,144},{32,160},{48,176},{64,192},{80,208},{96,224},{112... | collective-permute-start | bytes 196616 | tf_op jit(solution)/shard_map/ppermute | solution.py:34
  31.2 6.0 %collective-permute-start.5 = (bf16[2,128,128]{2,1,0:T(8,128)(2,1)S(1)}, bf16[2,128,128]{2,1,0:T(8,128)(2,1)S(1)}, u32[]{:S(2)}, u32[]{:S(2)}) collective-permute-start(bf16[2,128,128]{2,1,0:T(8,128)(2,1)S(1)} %get-tuple-element.34), channel_id=1, source_target_pairs={{0,192},{16,208},{32,224},{48,240},{64,0},{80,16},{96,32},{112,48}... | collective-permute-start | bytes 196616 | tf_op jit(solution)/shard_map/ppermute | solution.py:34
  32.7 23.5 %copy-start.8 = (bf16[16,128]{1,0:T(8,128)(2,1)}, bf16[16,128]{1,0:T(8,128)(2,1)S(1)}, u32[]{:S(2)}) copy-start(bf16[16,128]{1,0:T(8,128)(2,1)S(1)} %slice.93.rest_0_.refs_4_) | copy-start | bytes 12292
  37.7 8.4 %collective-permute-start.8 = (bf16[2,128,128]{2,1,0:T(8,128)(2,1)S(1)}, bf16[2,128,128]{2,1,0:T(8,128)(2,1)S(1)}, u32[]{:S(2)}, u32[]{:S(2)}) collective-permute-start(bf16[2,128,128]{2,1,0:T(8,128)(2,1)S(1)} %text_that_came.1), channel_id=1, source_target_pairs={{0,3},{1,0},{2,1},{3,2},{4,7},{5,4},{6,5},{7,6},{8,11},{9,8},{10,9... | collective-permute-start | bytes 196616 | tf_op jit(solution)/shard_map/ppermute | solution.py:28
  42.8 7.1 %collective-permute-start.7 = (bf16[2,128,128]{2,1,0:T(8,128)(2,1)S(1)}, bf16[2,128,128]{2,1,0:T(8,128)(2,1)S(1)}, u32[]{:S(2)}, u32[]{:S(2)}) collective-permute-start(bf16[2,128,128]{2,1,0:T(8,128)(2,1)S(1)} %text_that_came.1), channel_id=1, source_target_pairs={{0,2},{1,3},{2,0},{3,1},{4,6},{5,7},{6,4},{7,5},{8,10},{9,11},{10,... | collective-permute-start | bytes 196616 | tf_op jit(solution)/shard_map/ppermute | solution.py:28
  43.9 7.2 %collective-permute-start.6 = (bf16[2,128,128]{2,1,0:T(8,128)(2,1)S(1)}, bf16[2,128,128]{2,1,0:T(8,128)(2,1)S(1)}, u32[]{:S(2)}, u32[]{:S(2)}) collective-permute-start(bf16[2,128,128]{2,1,0:T(8,128)(2,1)S(1)} %text_that_came.1), channel_id=1, source_target_pairs={{0,1},{1,2},{2,3},{3,0},{4,5},{5,6},{6,7},{7,4},{8,9},{9,10},{10,1... | collective-permute-start | bytes 196616 | tf_op jit(solution)/shard_map/ppermute | solution.py:28
  51.2 10.1 %collective-permute-start.11 = (bf16[4,2,128,128]{3,2,1,0:T(8,128)(2,1)S(1)}, bf16[4,2,128,128]{3,2,1,0:T(8,128)(2,1)S(1)}, u32[]{:S(2)}, u32[]{:S(2)}) collective-permute-start(bf16[4,2,128,128]{3,2,1,0:T(8,128)(2,1)S(1)} %pad_maximum_fusion.t0), channel_id=1, source_target_pairs={{0,12},{1,13},{2,14},{3,15},{4,0},{5,1},{6,2},{7,3},{8,4},{9,5},{1... | collective-permute-start | bytes 786440 | tf_op jit(solution)/shard_map/ppermute | solution.py:22
  51.5 12.2 %collective-permute-start.10 = (bf16[4,2,128,128]{3,2,1,0:T(8,128)(2,1)S(1)}, bf16[4,2,128,128]{3,2,1,0:T(8,128)(2,1)S(1)}, u32[]{:S(2)}, u32[]{:S(2)}) collective-permute-start(bf16[4,2,128,128]{3,2,1,0:T(8,128)(2,1)S(1)} %pad_maximum_fusion.t0), channel_id=1, source_target_pairs={{0,8},{1,9},{2,10},{3,11},{4,12},{5,13},{6,14},{7,15},{8,0},{9,1},... | collective-permute-start | bytes 786440 | tf_op jit(solution)/shard_map/ppermute | solution.py:22
  53.7 11.5 %collective-permute-start.9 = (bf16[4,2,128,128]{3,2,1,0:T(8,128)(2,1)S(1)}, bf16[4,2,128,128]{3,2,1,0:T(8,128)(2,1)S(1)}, u32[]{:S(2)}, u32[]{:S(2)}) collective-permute-start(bf16[4,2,128,128]{3,2,1,0:T(8,128)(2,1)S(1)} %pad_maximum_fusion.t0), channel_id=1, source_target_pairs={{0,4},{1,5},{2,6},{3,7},{4,8},{5,9},{6,10},{7,11},{8,12},{9,13},{1... | collective-permute-start | bytes 786440 | tf_op jit(solution)/shard_map/ppermute | solution.py:22
  56.3 8.9 %copy-start.6 = (s32[4]{0:T(128)S(1)}, s32[4]{0:T(128)}, u32[]{:S(2)}) copy-start(s32[4]{0:T(128)} %copy-done.4) | copy-start | bytes 52
  65.2 2.2 %copy-start = (bf16[32,128,512]{2,1,0:T(8,128)(2,1)S(1)}, bf16[32,128,512]{2,1,0:T(8,128)(2,1)}, u32[]{:S(2)}) copy-start(bf16[32,128,512]{2,1,0:T(8,128)(2,1)} %all-gather.6.cloned.1.call-done) | copy-start | bytes 12582916
  70.0 12.2 %copy-start.11 = (bf16[2,128,512]{2,1,0:T(8,128)(2,1)}, bf16[2,128,512]{2,1,0:T(8,128)(2,1)S(1)}, u32[]{:S(2)}) copy-start(bf16[2,128,512]{2,1,0:T(8,128)(2,1)S(1)} %get-tuple-element.39) | copy-start | bytes 786436
  70.0 64.0 %collective-permute-start.17 = (bf16[256,512]{1,0:T(8,128)(2,1)S(1)}, bf16[256,512]{1,0:T(8,128)(2,1)S(1)}, u32[]{:S(2)}, u32[]{:S(2)}) collective-permute-start(bf16[256,512]{1,0:T(8,128)(2,1)S(1)} %bitcast.44), channel_id=1, source_target_pairs={{0,2},{1,3},{2,0},{3,1},{4,6},{5,7},{6,4},{7,5},{8,10},{9,11},{10,... | collective-permute-start | bytes 786440 | tf_op jit(solution)/shard_map/ppermute | solution.py:28
  75.4 27.8 %collective-permute-start.13 = (bf16[256,512]{1,0:T(8,128)(2,1)S(1)}, bf16[256,512]{1,0:T(8,128)(2,1)S(1)}, u32[]{:S(2)}, u32[]{:S(2)}) collective-permute-start(bf16[256,512]{1,0:T(8,128)(2,1)S(1)} %bitcast.45), channel_id=1, source_target_pairs={{0,3},{1,0},{2,1},{3,2},{4,7},{5,4},{6,5},{7,6},{8,11},{9,8},{10,9... | collective-permute-start | bytes 786440 | tf_op jit(solution)/shard_map/ppermute | solution.py:28
  75.4 21.4 %collective-permute-start.14 = (bf16[4,2,128,128]{3,2,1,0:T(8,128)(2,1)S(1)}, bf16[4,2,128,128]{3,2,1,0:T(8,128)(2,1)S(1)}, u32[]{:S(2)}, u32[]{:S(2)}) collective-permute-start(bf16[4,2,128,128]{3,2,1,0:T(8,128)(2,1)S(1)} %get-tuple-element.41), channel_id=1, source_target_pairs={{0,64},{16,80},{32,96},{48,112},{64,128},{80,144},{96,160},{112,17... | collective-permute-start | bytes 786440 | tf_op jit(solution)/shard_map/ppermute | solution.py:34
  77.1 21.1 %collective-permute-start.15 = (bf16[4,2,128,128]{3,2,1,0:T(8,128)(2,1)S(1)}, bf16[4,2,128,128]{3,2,1,0:T(8,128)(2,1)S(1)}, u32[]{:S(2)}, u32[]{:S(2)}) collective-permute-start(bf16[4,2,128,128]{3,2,1,0:T(8,128)(2,1)S(1)} %get-tuple-element.42), channel_id=1, source_target_pairs={{0,128},{16,144},{32,160},{48,176},{64,192},{80,208},{96,224},{112... | collective-permute-start | bytes 786440 | tf_op jit(solution)/shard_map/ppermute | solution.py:34
  82.2 16.1 %collective-permute-start.16 = (bf16[4,2,128,128]{3,2,1,0:T(8,128)(2,1)S(1)}, bf16[4,2,128,128]{3,2,1,0:T(8,128)(2,1)S(1)}, u32[]{:S(2)}, u32[]{:S(2)}) collective-permute-start(bf16[4,2,128,128]{3,2,1,0:T(8,128)(2,1)S(1)} %get-tuple-element.43), channel_id=1, source_target_pairs={{0,192},{16,208},{32,224},{48,240},{64,0},{80,16},{96,32},{112,48}... | collective-permute-start | bytes 786440 | tf_op jit(solution)/shard_map/ppermute | solution.py:34
  82.2 34.2 %all-to-all-start.2 = ((bf16[4,2,2,256,256]{4,3,2,1,0:T(8,128)(2,1)}), bf16[4,2,2,256,256]{4,3,2,1,0:T(8,128)(2,1)}, u32[]{:S(2)}, u32[]{:S(2)}) async-start(bf16[4,2,2,256,256]{4,3,2,1,0:T(8,128)(2,1)} %pack.3), calls=%async_computation.2 | async-start | bytes 4194304 | tf_op jit(solution)/shard_map/all_to_all | solution.py:42
  90.0 6.8 %copy-start.12 = (bf16[2,128,512]{2,1,0:T(8,128)(2,1)S(1)}, bf16[2,128,512]{2,1,0:T(8,128)(2,1)}, u32[]{:S(2)}) copy-start(bf16[2,128,512]{2,1,0:T(8,128)(2,1)} %copy-done.11) | copy-start | bytes 786436
  90.0 8.3 %copy-start.7 = (s32[4]{0:T(128)S(1)}, s32[4]{0:T(128)}, u32[]{:S(2)}) copy-start(s32[4]{0:T(128)} %copy-done.4) | copy-start | bytes 52
  96.8 12.3 %collective-permute-start.12 = (bf16[256,512]{1,0:T(8,128)(2,1)S(1)}, bf16[256,512]{1,0:T(8,128)(2,1)S(1)}, u32[]{:S(2)}, u32[]{:S(2)}) collective-permute-start(bf16[256,512]{1,0:T(8,128)(2,1)S(1)} %bitcast.47), channel_id=1, source_target_pairs={{0,1},{1,2},{2,3},{3,0},{4,5},{5,6},{6,7},{7,4},{8,9},{9,10},{10,1... | collective-permute-start | bytes 786440 | tf_op jit(solution)/shard_map/ppermute | solution.py:28
  99.2 0.7 copy-start.2
  99.9 29.9 %collective-permute-start.18 = (bf16[4,2,128,128]{3,2,1,0:T(8,128)(2,1)S(1)}, bf16[4,2,128,128]{3,2,1,0:T(8,128)(2,1)S(1)}, u32[]{:S(2)}, u32[]{:S(2)}) collective-permute-start(bf16[4,2,128,128]{3,2,1,0:T(8,128)(2,1)S(1)} %get-tuple-element.48), channel_id=1, source_target_pairs={{0,48},{16,0},{32,16},{48,32},{64,112},{80,64},{96,80},{112,96},{1... | collective-permute-start | bytes 786440 | tf_op jit(solution)/shard_map/ppermute | solution.py:38
  102.0 30.7 %collective-permute-start.19 = (bf16[4,2,128,128]{3,2,1,0:T(8,128)(2,1)S(1)}, bf16[4,2,128,128]{3,2,1,0:T(8,128)(2,1)S(1)}, u32[]{:S(2)}, u32[]{:S(2)}) collective-permute-start(bf16[4,2,128,128]{3,2,1,0:T(8,128)(2,1)S(1)} %get-tuple-element.49), channel_id=1, source_target_pairs={{0,32},{16,48},{32,0},{48,16},{64,96},{80,112},{96,64},{112,80},{1... | collective-permute-start | bytes 786440 | tf_op jit(solution)/shard_map/ppermute | solution.py:38
  103.2 13.2 %copy-start.18 = (bf16[256,512]{1,0:T(8,128)(2,1)}, bf16[256,512]{1,0:T(8,128)(2,1)S(1)}, u32[]{:S(2)}) copy-start(bf16[256,512]{1,0:T(8,128)(2,1)S(1)} %collective-permute-done.13.kv) | copy-start | bytes 786436
  103.2 30.2 %collective-permute-start.20 = (bf16[4,2,128,128]{3,2,1,0:T(8,128)(2,1)S(1)}, bf16[4,2,128,128]{3,2,1,0:T(8,128)(2,1)S(1)}, u32[]{:S(2)}, u32[]{:S(2)}) collective-permute-start(bf16[4,2,128,128]{3,2,1,0:T(8,128)(2,1)S(1)} %get-tuple-element.50), channel_id=1, source_target_pairs={{0,16},{16,32},{32,48},{48,0},{64,80},{80,96},{96,112},{112,64},{1... | collective-permute-start | bytes 786440 | tf_op jit(solution)/shard_map/ppermute | solution.py:38
  116.4 29.0 %all-to-all-start.1 = ((bf16[4,2,2,256,256]{4,3,2,1,0:T(8,128)(2,1)}), bf16[4,2,2,256,256]{4,3,2,1,0:T(8,128)(2,1)}, u32[]{:S(2)}, u32[]{:S(2)}) async-start(bf16[4,2,2,256,256]{4,3,2,1,0:T(8,128)(2,1)} %get-tuple-element.44), calls=%async_computation.1 | async-start | bytes 4194304 | tf_op jit(solution)/shard_map/all_to_all | solution.py:42
  121.6 8.2 %copy-start.20 = (bf16[256,512]{1,0:T(8,128)(2,1)S(1)}, bf16[256,512]{1,0:T(8,128)(2,1)}, u32[]{:S(2)}) copy-start(bf16[256,512]{1,0:T(8,128)(2,1)} %get-tuple-element.56) | copy-start | bytes 786436
  121.6 76.0 %all-gather.4.cloned.1.call-start = ((), (), s32[]{:S(2)}) async-start(), calls=%async_computation.4 | async-start | bytes 4456448 | tf_op jit(solution)/shard_map/all_gather | solution.py:348
  128.3 14.6 %collective-permute-start.22 = (bf16[256,512]{1,0:T(8,128)(2,1)}, bf16[256,512]{1,0:T(8,128)(2,1)S(1)}, u32[]{:S(2)}, u32[]{:S(2)}) collective-permute-start(bf16[256,512]{1,0:T(8,128)(2,1)} %get-tuple-element.57), channel_id=1, source_target_pairs={{0,1},{1,2},{2,3},{3,0},{4,5},{5,6},{6,7},{7,4},{8,9},{9,10},{10,1... | collective-permute-start | bytes 786440 | tf_op jit(solution)/shard_map/ppermute | solution.py:28
  129.8 4.3 %copy-start.14 = (bf16[4,2,128,128]{3,2,1,0:T(8,128)(2,1)}, bf16[4,2,128,128]{3,2,1,0:T(8,128)(2,1)S(1)}, u32[]{:S(2)}) copy-start(bf16[4,2,128,128]{3,2,1,0:T(8,128)(2,1)S(1)} %collective-permute-done.18.t1) | copy-start | bytes 786436
  129.8 13.2 %collective-permute-start.21 = (bf16[256,512]{1,0:T(8,128)(2,1)S(1)}, bf16[256,512]{1,0:T(8,128)(2,1)S(1)}, u32[]{:S(2)}, u32[]{:S(2)}) collective-permute-start(bf16[256,512]{1,0:T(8,128)(2,1)S(1)} %copy-done.20), channel_id=1, source_target_pairs={{0,3},{1,0},{2,1},{3,2},{4,7},{5,4},{6,5},{7,6},{8,11},{9,8},{10,9... | collective-permute-start | bytes 786440 | tf_op jit(solution)/shard_map/ppermute | solution.py:28
  132.8 1.2 copy-start.15
  133.4 0.7 copy-start.16
  134.7 8.2 %copy-start.1 = (f32[256,512]{1,0:T(8,128)S(1)}, f32[256,512]{1,0:T(8,128)}, u32[]{:S(2)}) copy-start(f32[256,512]{1,0:T(8,128)} %get-tuple-element.55.a) | copy-start | bytes 1572868
  141.4 16.0 %copy-start.13 = (bf16[4,2,2,256,256]{4,3,2,1,0:T(8,128)(2,1)S(1)}, bf16[4,2,2,256,256]{4,3,2,1,0:T(8,128)(2,1)}, u32[]{:S(2)}) copy-start(bf16[4,2,2,256,256]{4,3,2,1,0:T(8,128)(2,1)} %get-tuple-element.51) | copy-start | bytes 6291460
  141.4 15.2 %collective-permute-start.23 = (bf16[256,512]{1,0:T(8,128)(2,1)}, bf16[256,512]{1,0:T(8,128)(2,1)S(1)}, u32[]{:S(2)}, u32[]{:S(2)}) collective-permute-start(bf16[256,512]{1,0:T(8,128)(2,1)} %get-tuple-element.58), channel_id=1, source_target_pairs={{0,2},{1,3},{2,0},{3,1},{4,6},{5,7},{6,4},{7,5},{8,10},{9,11},{10,... | collective-permute-start | bytes 786440 | tf_op jit(solution)/shard_map/ppermute | solution.py:28
  (3 other events, 2.0 us)
Sparse Core Ops, SparseCore 0:
  10.4 49.2 all-gather.5
  157.5 40.0 all-gather.3

commit v5 on v4

--- a/solution.py
+++ b/solution.py
@@ -15,7 +15,7 @@
 PARAMS = pltpu.CompilerParams(vmem_limit_bytes=60 << 20)
 ANY = pl.BlockSpec(memory_space=pl.ANY)
 ORDER = (0, 1, 3, 2)
-PARTS = ((0, 0), (0, 1), (1, 0), (1, 1))
+PARTS = ((0, 0, 0, 0), (0, 1, 0, 1), (0, 2, 1, 0), (1, 0, 1, 1))
 
 
 def x_shift(a, k):
@@ -181,7 +181,7 @@
     return kv.reshape(256, 512), rows
 
 
-def attend(m, piece, where, src, lengths, moved, kv, into, wait):
+def attend(m, piece, slot, where, src, lengths, moved, kv, into, wait):
     scale = 1.0 / math.sqrt(HEAD)
 
     def body(w, src, lengths, sent, kv, *refs):
@@ -210,12 +210,14 @@
         grads[:, :HEAD] = grad_key.astype(grads.dtype)
         grads[:, HEAD:] = grad_value.astype(grads.dtype)
 
-    by_head = pl.BlockSpec((N, 2, 1, 256, HEAD), lambda l, *_: (0, 0, piece, 0, l))
+    def by_head(at):
+        return pl.BlockSpec((N, 2, 1, 256, HEAD), lambda l, *_: (0, 0, at, 0, l))
+
     columns = pl.BlockSpec((256, 256), lambda l, *_: (0, l))
     return call(
         body, (where, src, lengths), (2,),
-        [by_head, columns] + [ANY] * (len(into) + len(wait)),
-        [by_head, columns],
+        [by_head(piece), columns] + [ANY] * (len(into) + len(wait)),
+        [by_head(slot), columns],
         [
             jax.ShapeDtypeStruct((N, 2, 2, 256, 256), BF),
             jax.ShapeDtypeStruct((256, 512), BF if m else F32),
@@ -241,6 +243,13 @@
     return small(
         body, (), [most, last], after, jax.ShapeDtypeStruct((256, 512), BF), "add_last"
     )
+
+
+def relay(a, after):
+    def body(a, *rest):
+        rest[-1][...] = a[...]
+
+    return small(body, (), [a], after, jax.ShapeDtypeStruct(a.shape, a.dtype), "relay")
 
 
 def rows_to_send(where, came):
@@ -314,33 +323,35 @@
     weight = lax.all_gather(jnp.swapaxes(kv_weight, 0, 1), "dp", axis=0)
     near = [text] + [r_shift(text, N - n) for n in (1, 2, 3)]
     sends = text_to_send(where, src, near)
-    packed = pack(ORDER[:2], where, q, g, [tiny(sends[0])])
+    packed = pack(ORDER[:3], where, q, g, [tiny(sends[0])])
     moved = [exchange_x(packed)]
     picked = text_that_came(
         where, src, [sends[0]] + [y_shift(sends[k], k) for k in (1, 2, 3)], [tiny(packed)]
     )
-    packed = pack(ORDER[2:], where, q, g, [tiny(packed)])
+    packed = pack(ORDER[3:], where, q, g, [tiny(packed)])
     along_z = jnp.stack([picked] + [z_shift(picked, n) for n in (1, 2, 3)])
     pieces = [along_z] + [x_shift(along_z, k) for k in (1, 2, 3)]
 
     packed, *pieces = lax.optimization_barrier((packed, *pieces))
     moved.append(exchange_x(packed))
     kv, rows = project(where, pieces, weight)
-    kvs = [kv] + [z_shift(kv, m) for m in ORDER[1:]]
+    kvs = [kv] + [z_shift(kv, m) for m in ORDER[1:3]]
 
     rows = [rows[0]] + [y_shift(rows[k], k) for k in (1, 2, 3)]
     by_r = rows_to_send(where, rows)
     own_rows = [by_r[0]] + [r_shift(by_r[n], N - n) for n in (1, 2, 3)]
 
     outs, grads = [None, None], []
-    for i, (which, first) in enumerate(PARTS):
-        into = [outs[which]] if first else []
+    for i, (came, piece, which, slot) in enumerate(PARTS):
+        into = [outs[which]] if slot else []
         wait = ([], [kvs[2], *rows[1:]], [], own_rows[1:])[i]
         outs[which], d = attend(
-            ORDER[i], first, where, src, lengths, moved[which], kvs[i], into,
+            ORDER[i], piece, slot, where, src, lengths, moved[came], kvs[i], into,
             [tiny(a) for a in wait],
         )
         grads.append(z_shift(d, N - ORDER[i]) if i else d)
+        if i == 0:
+            kvs.append(z_shift(relay(kv, [tiny(d)]), ORDER[3]))
 
     outs = [exchange_x(a) for a in outs]
     after = [tiny(a) for a in [outs[0]]]

time: 212 us -> 226 us (1.066)
  waiting for transfers between devices: 39.1 us -> 60.4 us
  blocking collectives: 28.1 us -> 20.7 us
  starting transfers between devices: 60.3 us -> 57.6 us
    ppermute x3, waiting for transfers between devices: 3.91 us -> 19.3 us  [x_shift(): lax.ppermute(a, 'ctx', [(4 * x + z, 4 * ((x + k) % N) + z) for x in range...]
    all_gather x1, waiting for transfers between devices: 6.58 us -> 21.6 us  [per_device(): every_grad = lax.all_gather(total.reshape(2, 128, 512), 'dp', axis=0)]
    ppermute x9, waiting for transfers between devices: 18.3 us -> 9.05 us  [z_shift(): lax.ppermute(a, 'ctx', [(4 * x + z, 4 * x + (z + m) % N) for x in range(N...]
    all_to_all x1, blocking collectives: 28.1 us -> 20.7 us  [exchange_x(): lax.all_to_all(a, 'ctx', split_axis=0, concat_axis=0, tiled=True, axis_in...]
    ppermute x6, waiting for transfers between devices: 3.46 us -> 7.58 us  [r_shift(): lax.ppermute(a, 'dp', [(i, i // N * N + (i % N + n) % N) for i in range(1...]
    all_to_all x3, starting transfers between devices: 17.9 us -> 14.3 us  [exchange_x(): lax.all_to_all(a, 'ctx', split_axis=0, concat_axis=0, tiled=True, axis_in...]
    ppermute x6, starting transfers between devices: 10.8 us -> 8.11 us  [y_shift(): lax.ppermute(a, 'dp', [(i, (i // N + k) % N * N + i % N) for i in range(1...]
    ppermute x9, starting transfers between devices: 20.6 us -> 23.2 us  [z_shift(): lax.ppermute(a, 'ctx', [(4 * x + z, 4 * x + (z + m) % N) for x in range(N...]
  transfers between devices with their start and end apart: 29 -> 29, of which waited for: 14 -> 12; matrix products, arithmetic and copies ran while one was open for 4% -> 4% of each run, Pallas kernels for 22% -> 21%
where the time goes in v5:
time: 226 us; the launch traced here: 223 us
  waiting for transfers between devices  60.4 us (27%)
  starting transfers between devices  57.6 us (25%)
  Pallas kernels  53.5 us (24%)
  blocking collectives  20.7 us (9%)
  local copies, waits for them, and re-layouts  16.9 us (7%)
  between operations  14.2 us (6%)
    pallas_call x4, Pallas kernels, attend(): call(body, (where, src, lengths), (2,), [by_head(piece), columns] + [ANY]...  26.7 us
    ppermute x9, starting transfers between devices, z_shift(): lax.ppermute(a, 'ctx', [(4 * x + z, 4 * x + (z + m) % N) for x in range(N...  23.2 us
    all_gather x1, waiting for transfers between devices, per_device(): every_grad = lax.all_gather(total.reshape(2, 128, 512), 'dp', axis=0)  21.6 us
    all_to_all x1, blocking collectives, exchange_x(): lax.all_to_all(a, 'ctx', split_axis=0, concat_axis=0, tiled=True, axis_in...  20.7 us
    ppermute x3, waiting for transfers between devices, x_shift(): lax.ppermute(a, 'ctx', [(4 * x + z, 4 * ((x + k) % N) + z) for x in range...  19.3 us
    all_to_all x3, starting transfers between devices, exchange_x(): lax.all_to_all(a, 'ctx', split_axis=0, concat_axis=0, tiled=True, axis_in...  14.3 us
    pallas_call x2, Pallas kernels, pack(): call(body, (where,), (256 // rows,), [pl.BlockSpec((rows, 4096), lambda i...  10 us
    ppermute x9, waiting for transfers between devices, z_shift(): lax.ppermute(a, 'ctx', [(4 * x + z, 4 * x + (z + m) % N) for x in range(N...  9.05 us
  transfers between devices with their start and end apart: 29, of which 12 were waited for; matrix products, arithmetic and copies ran while one was open for 4% of the time, Pallas kernels for 21%

profile of v5, /device:TPU:11, one launch (start us, length us, event | category | flops | bytes accessed | tf_op | source)
XLA Modules:
  0.0 223.5 jit_solution(14234059316619913861)
XLA Ops:
  7.2 1.7 copy.18
  9.7 1.7 collective-permute-start.1
  11.3 1.3 collective-permute-start.2
  12.7 1.1 collective-permute-done.refs_1_
  13.9 1.0 collective-permute-done.2.refs_3_
  17.6 5.3 %pack.2 = bf16[4,2,3,256,256]{4,3,2,1,0:T(8,128)(2,1)} custom-call(s32[4]{0:T(128)} %copy-done.6, bf16[256,4096]{1,0:T(8,128)(2,1)} %bitcast.48, bf16[256,4096]{1,0:T(8,128)(2,1)} %bitcast.50, bf16[16,128]{1,0:T(8,128)(2,1)} %slice_bitcast_fusion.8.rest_0_), custom_call_target="tpu_custom_call" | custom-call | bytes 18874368 | tf_op jit(solution)/shard_map/pack/pallas_call | solution.py:135
  22.9 5.1 %all-to-all-start = ((bf16[4,2,3,256,256]{4,3,2,1,0:T(8,128)(2,1)}), bf16[4,2,3,256,256]{4,3,2,1,0:T(8,128)(2,1)}, u32[]{:S(2)}, u32[]{:S(2)}) async-start(bf16[4,2,3,256,256]{4,3,2,1,0:T(8,128)(2,1)} %pack.2), calls=%async_computation | async-start | bytes 6291456 | tf_op jit(solution)/shard_map/all_to_all | solution.py:42
  28.0 1.3 collective-permute-start.3
  29.3 1.1 collective-permute-start.4
  30.4 1.7 collective-permute-start.5
  32.0 0.9 slice_bitcast_fusion.1
  33.0 2.2 collective-permute-done.4.refs_2_
  36.3 2.4 %collective-permute-start.6 = (bf16[2,128,128]{2,1,0:T(8,128)(2,1)S(1)}, bf16[2,128,128]{2,1,0:T(8,128)(2,1)S(1)}, u32[]{:S(2)}, u32[]{:S(2)}) collective-permute-start(bf16[2,128,128]{2,1,0:T(8,128)(2,1)S(1)} %text_that_came.1), channel_id=1, source_target_pairs={{0,1},{1,2},{2,3},{3,0},{4,5},{5,6},{6,7},{7,4},{8,9},{9,10},{10,1... | collective-permute-start | bytes 196616 | tf_op jit(solution)/shard_map/ppermute | solution.py:28
  38.8 4.4 %collective-permute-start.7 = (bf16[2,128,128]{2,1,0:T(8,128)(2,1)S(1)}, bf16[2,128,128]{2,1,0:T(8,128)(2,1)S(1)}, u32[]{:S(2)}, u32[]{:S(2)}) collective-permute-start(bf16[2,128,128]{2,1,0:T(8,128)(2,1)S(1)} %text_that_came.1), channel_id=1, source_target_pairs={{0,2},{1,3},{2,0},{3,1},{4,6},{5,7},{6,4},{7,5},{8,10},{9,11},{10,... | collective-permute-start | bytes 196616 | tf_op jit(solution)/shard_map/ppermute | solution.py:28
  43.2 2.8 %collective-permute-start.8 = (bf16[2,128,128]{2,1,0:T(8,128)(2,1)S(1)}, bf16[2,128,128]{2,1,0:T(8,128)(2,1)S(1)}, u32[]{:S(2)}, u32[]{:S(2)}) collective-permute-start(bf16[2,128,128]{2,1,0:T(8,128)(2,1)S(1)} %text_that_came.1), channel_id=1, source_target_pairs={{0,3},{1,0},{2,1},{3,2},{4,7},{5,4},{6,5},{7,6},{8,11},{9,8},{10,9... | collective-permute-start | bytes 196616 | tf_op jit(solution)/shard_map/ppermute | solution.py:28
  46.0 2.0 collective-permute-done.8
  48.0 1.8 collective-permute-start.10
  49.8 1.6 collective-permute-start.11
  52.1 4.8 %pack.3 = bf16[4,2,1,256,256]{4,3,2,1,0:T(8,128)(2,1)} custom-call(s32[4]{0:T(128)} %copy-done.6, bf16[256,4096]{1,0:T(8,128)(2,1)} %bitcast.49, bf16[256,4096]{1,0:T(8,128)(2,1)} %bitcast.51, bf16[16,128]{1,0:T(8,128)(2,1)} %copy-done.10), custom_call_target="tpu_custom_call" | custom-call | bytes 18874368 | tf_op jit(solution)/shard_map/pack/pallas_call | solution.py:135
  56.8 11.9 %collective-permute-done.10.t2 = bf16[4,2,128,128]{3,2,1,0:T(8,128)(2,1)S(1)} collective-permute-done((bf16[4,2,128,128]{3,2,1,0:T(8,128)(2,1)S(1)}, bf16[4,2,128,128]{3,2,1,0:T(8,128)(2,1)S(1)}, u32[]{:S(2)}, u32[]{:S(2)}) %collective-permute-start.10) | collective-permute-done | bytes 262176 | tf_op jit(solution)/shard_map/ppermute | solution.py:22
  68.8 7.3 %collective-permute-done.11.t3 = bf16[4,2,128,128]{3,2,1,0:T(8,128)(2,1)S(1)} collective-permute-done((bf16[4,2,128,128]{3,2,1,0:T(8,128)(2,1)S(1)}, bf16[4,2,128,128]{3,2,1,0:T(8,128)(2,1)S(1)}, u32[]{:S(2)}, u32[]{:S(2)}) %collective-permute-start.11) | collective-permute-done | bytes 262176 | tf_op jit(solution)/shard_map/ppermute | solution.py:22
  76.1 2.2 copy-done
  78.3 2.6 %project.1 = (bf16[2,128,512]{2,1,0:T(8,128)(2,1)S(1)}, bf16[4,2,128,128]{3,2,1,0:T(8,128)(2,1)S(1)}, bf16[4,2,128,128]{3,2,1,0:T(8,128)(2,1)S(1)}, bf16[4,2,128...) custom-call(s32[4]{0:T(128)S(1)} %copy-done.8, bf16[4,2,128,128]{3,2,1,0:T(8,128)(2,1)S(1)} %pad_maximum_fusion.t0, ...), custom_call_target="tpu_custom_call" | custom-call | flops 536870912 | bytes 6291456 | tf_op jit(solution)/shard_map/project/pallas_call | solution.py:173
  81.0 5.2 %collective-permute-start.13 = (bf16[256,512]{1,0:T(8,128)(2,1)S(1)}, bf16[256,512]{1,0:T(8,128)(2,1)}, u32[]{:S(2)}, u32[]{:S(2)}) collective-permute-start(bf16[256,512]{1,0:T(8,128)(2,1)S(1)} %bitcast.39), channel_id=1, source_target_pairs={{0,3},{1,0},{2,1},{3,2},{4,7},{5,4},{6,5},{7,6},{8,11},{9,8},{10,9... | collective-permute-start | bytes 786440 | tf_op jit(solution)/shard_map/ppermute | solution.py:28
  86.3 2.3 %collective-permute-start.15 = (bf16[4,2,128,128]{3,2,1,0:T(8,128)(2,1)S(1)}, bf16[4,2,128,128]{3,2,1,0:T(8,128)(2,1)S(1)}, u32[]{:S(2)}, u32[]{:S(2)}) collective-permute-start(bf16[4,2,128,128]{3,2,1,0:T(8,128)(2,1)S(1)} %get-tuple-element.42), channel_id=1, source_target_pairs={{0,128},{16,144},{32,160},{48,176},{64,192},{80,208},{96,224},{112... | collective-permute-start | bytes 786440 | tf_op jit(solution)/shard_map/ppermute | solution.py:34
  88.6 1.6 collective-permute-start.14
  90.2 4.7 %all-to-all-start.2 = ((bf16[4,2,1,256,256]{4,3,2,1,0:T(8,128)(2,1)}), bf16[4,2,1,256,256]{4,3,2,1,0:T(8,128)(2,1)S(1)}, u32[]{:S(2)}, u32[]{:S(2)}) async-start(bf16[4,2,1,256,256]{4,3,2,1,0:T(8,128)(2,1)} %pack.3), calls=%async_computation.2 | async-start | bytes 2097152 | tf_op jit(solution)/shard_map/all_to_all | solution.py:42
  94.9 6.6 %attend.4 = (bf16[4,2,2,256,256]{4,3,2,1,0:T(8,128)(2,1)}, f32[256,512]{1,0:T(8,128)}) custom-call(s32[4]{0:T(128)} %copy-done.6, s32[16]{0:T(128)} %src.11, s32[32]{0:T(128)} %reshape.25.lengths, bf16[4,2,3,256,256]{4,3,2,1,0:T(8,128)(2,1)} %all-to-all-done.sent, bf16[256,512]{1,0:T(8,128)(2,1)} %bitcast.41), custom_call_target="tpu_custom_call" | custom-call | flops 6000000000 | bytes 4194304 | tf_op jit(solution)/shard_map/attend/pallas_call | solution.py:217
  102.2 0.9 copy-done.4
  103.2 3.3 %collective-permute-start.17 = (bf16[256,512]{1,0:T(8,128)(2,1)S(1)}, bf16[256,512]{1,0:T(8,128)(2,1)}, u32[]{:S(2)}, u32[]{:S(2)}) collective-permute-start(bf16[256,512]{1,0:T(8,128)(2,1)S(1)} %relay.1), channel_id=1, source_target_pairs={{0,2},{1,3},{2,0},{3,1},{4,6},{5,7},{6,4},{7,5},{8,10},{9,11},{10,... | collective-permute-start | bytes 786440 | tf_op jit(solution)/shard_map/ppermute | solution.py:28
  107.7 1.3 slice.98.refs_1_
  109.6 6.7 %attend.5 = (bf16[4,2,2,256,256]{4,3,2,1,0:T(8,128)(2,1)}, bf16[256,512]{1,0:T(8,128)(2,1)}) custom-call(s32[4]{0:T(128)} %copy-done.6, s32[16]{0:T(128)} %src.11, s32[32]{0:T(128)} %reshape.25.lengths, bf16[4,2,3,256,256]{4,3,2,1,0:T(8,128)(2,1)} %all-to-all-done.sent, ...), custom_call_target="tpu_custom_call", output_to_operand_aliasing={{0}: (5, {})} | custom-call | flops 6000000000 | bytes 4194304 | tf_op jit(solution)/shard_map/attend/pallas_call | solution.py:217
  116.3 1.5 collective-permute-start.21
  119.4 3.4 %collective-permute-start.20 = (bf16[4,2,128,128]{3,2,1,0:T(8,128)(2,1)S(1)}, bf16[4,2,128,128]{3,2,1,0:T(8,128)(2,1)S(1)}, u32[]{:S(2)}, u32[]{:S(2)}) collective-permute-start(bf16[4,2,128,128]{3,2,1,0:T(8,128)(2,1)S(1)} %get-tuple-element.51), channel_id=1, source_target_pairs={{0,16},{16,32},{32,48},{48,0},{64,80},{80,96},{96,112},{112,64},{1... | collective-permute-start | bytes 786440 | tf_op jit(solution)/shard_map/ppermute | solution.py:38
  123.4 1.0 copy-done.14
  124.5 4.5 %all-to-all-start.1 = ((bf16[4,2,2,256,256]{4,3,2,1,0:T(8,128)(2,1)}), bf16[4,2,2,256,256]{4,3,2,1,0:T(8,128)(2,1)}, u32[]{:S(2)}, u32[]{:S(2)}) async-start(bf16[4,2,2,256,256]{4,3,2,1,0:T(8,128)(2,1)} %get-tuple-element.44), calls=%async_computation.1 | async-start | bytes 4194304 | tf_op jit(solution)/shard_map/all_to_all | solution.py:42
  129.1 6.6 %attend.6 = (bf16[4,2,2,256,256]{4,3,2,1,0:T(8,128)(2,1)}, bf16[256,512]{1,0:T(8,128)(2,1)}) custom-call(s32[4]{0:T(128)} %copy-done.6, s32[16]{0:T(128)} %src.11, s32[32]{0:T(128)} %reshape.25.lengths, bf16[4,2,3,256,256]{4,3,2,1,0:T(8,128)(2,1)} %all-to-all-done.sent, bf16[256,512]{1,0:T(8,128)(2,1)} %collective-permute-done.13.kv), custom_call_target="tpu_custom_call" | custom-call | flops 6000000000 | bytes 4194304 | tf_op jit(solution)/shard_map/attend/pallas_call | solution.py:217
  135.6 0.9 collective-permute-start.22
  138.0 4.5 %collective-permute-done.19.t2 = bf16[4,2,128,128]{3,2,1,0:T(8,128)(2,1)S(1)} collective-permute-done((bf16[4,2,128,128]{3,2,1,0:T(8,128)(2,1)S(1)}, bf16[4,2,128,128]{3,2,1,0:T(8,128)(2,1)S(1)}, u32[]{:S(2)}, u32[]{:S(2)}) %collective-permute-start.19) | collective-permute-done | bytes 262176 | tf_op jit(solution)/shard_map/ppermute | solution.py:38
  143.2 0.9 collective-permute-done.18.t1
  144.8 6.7 %attend.7 = (bf16[4,2,2,256,256]{4,3,2,1,0:T(8,128)(2,1)}, bf16[256,512]{1,0:T(8,128)(2,1)}) custom-call(s32[4]{0:T(128)} %copy-done.6, s32[16]{0:T(128)} %src.11, s32[32]{0:T(128)} %reshape.25.lengths, bf16[4,2,1,256,256]{4,3,2,1,0:T(8,128)(2,1)} %copy-done.14, bf16[256,512]{1,0:T(8,128)(2,1)} %collective-permute-done.17.kv, ...), custom_call_target="tpu_custom_call", output_to_operand_aliasing={{0}: (5, {})} | custom-call | flops 6000000000 | bytes 4194304 | tf_op jit(solution)/shard_map/attend/pallas_call | solution.py:217
  151.6 2.6 %collective-permute-start.23 = (bf16[256,512]{1,0:T(8,128)(2,1)}, bf16[256,512]{1,0:T(8,128)(2,1)S(1)}, u32[]{:S(2)}, u32[]{:S(2)}) collective-permute-start(bf16[256,512]{1,0:T(8,128)(2,1)} %get-tuple-element.58), channel_id=1, source_target_pairs={{0,2},{1,3},{2,0},{3,1},{4,6},{5,7},{6,4},{7,5},{8,10},{9,11},{10,... | collective-permute-start | bytes 786440 | tf_op jit(solution)/shard_map/ppermute | solution.py:28
  154.4 0.9 slice_bitcast_fusion
  155.3 7.1 %collective-permute-done.23.b = bf16[256,512]{1,0:T(8,128)(2,1)S(1)} collective-permute-done((bf16[256,512]{1,0:T(8,128)(2,1)}, bf16[256,512]{1,0:T(8,128)(2,1)S(1)}, u32[]{:S(2)}, u32[]{:S(2)}) %collective-permute-start.23) | collective-permute-done | bytes 262176 | tf_op jit(solution)/shard_map/ppermute | solution.py:28
  163.2 20.7 %all_to_all.20.refs_1_ = bf16[4,2,2,256,256]{4,3,2,1,0:T(8,128)(2,1)} all-to-all(bf16[4,2,2,256,256]{4,3,2,1,0:T(8,128)(2,1)S(1)} %copy-done.13), channel_id=1, replica_groups={{0,4,8,12},{1,5,9,13},{2,6,10,14},{3,7,11,15},{16,20,24,28},{17,21,25,2..., dimensions={0} | all-to-all | bytes 4194304 | tf_op jit(solution)/shard_map/all_to_all | solution.py:42
  183.9 5.5 %place.1 = (bf16[256,4096]{1,0:T(8,128)(2,1)}, bf16[256,4096]{1,0:T(8,128)(2,1)}) custom-call(s32[4]{0:T(128)} %copy-done.6, bf16[4,2,2,256,256]{4,3,2,1,0:T(8,128)(2,1)} %all-to-all-done.1.refs_0_, bf16[4,2,2,256,256]{4,3,2,1,0:T(8,128)(2,1)} %all_to_all.20.refs_1_), custom_call_target="tpu_custom_call" | custom-call | bytes 8388608 | tf_op jit(solution)/shard_map/place/pallas_call | solution.py:308
  189.4 21.6 %all-gather.4.cloned.1.call-done = bf16[16,2,128,512]{3,2,1,0:T(8,128)(2,1)} async-done(((bf16[1,2,128,512]{3,2,1,0:T(8,128)(2,1)}), bf16[16,2,128,512]{3,2,1,0:T(8,128)(2,1)}) %all-gather.4.cloned.1.call-update) | async-done | bytes 4194320 | tf_op jit(solution)/shard_map/all_gather | solution.py:359
  211.0 5.7 %weight_gradient.1 = f32[128,2,512]{2,1,0:T(2,128)} custom-call(s32[4]{0:T(128)} %copy-done.6, bf16[4,2,128,128]{3,2,1,0:T(8,128)(2,1)} %copy-done.2, bf16[4,2,128,128]{3,2,1,0:T(8,128)(2,1)} %copy-done.17, bf16[4,2,128,128]{3,2,1,0:T(8,128)(2,1)} %copy-done.16, bf16[4,2,128,128]{3,2,1,0:T(8,128)(2,1)} %copy-done.15, bf16[4,4,2,128,512]{4,3,2,1,0:T(8,128)(2,1)} %bitcast.52), custom_call_target="tpu_custom_call" | custom-call | flops 536870912 | bytes 6291456 | tf_op jit(solution)/shard_map/weight_gradient/pallas_call | solution.py:287
  (84 shorter events, 14.3 us)
Async XLA Ops:
  7.2 68.9 %all-gather.6.cloned.1.call-start = ((), (), s32[]{:S(2)}) async-start(), calls=%async_computation.5 | async-start | bytes 4456448 | tf_op jit(solution)/shard_map/all_gather | solution.py:323
  8.9 5.0 %collective-permute-start = (bf16[2,128,128]{2,1,0:T(8,128)(2,1)}, bf16[2,128,128]{2,1,0:T(8,128)(2,1)S(1)}, u32[]{:S(2)}, u32[]{:S(2)}) collective-permute-start(bf16[2,128,128]{2,1,0:T(8,128)(2,1)} %bitcast.44), channel_id=1, source_target_pairs={{0,48},{16,0},{32,16},{48,32},{64,112},{80,64},{96,80},{112,96},{1... | collective-permute-start | bytes 196616 | tf_op jit(solution)/shard_map/ppermute | solution.py:38
  9.7 4.2 %collective-permute-start.1 = (bf16[2,128,128]{2,1,0:T(8,128)(2,1)}, bf16[2,128,128]{2,1,0:T(8,128)(2,1)S(1)}, u32[]{:S(2)}, u32[]{:S(2)}) collective-permute-start(bf16[2,128,128]{2,1,0:T(8,128)(2,1)} %bitcast.45), channel_id=1, source_target_pairs={{0,32},{16,48},{32,0},{48,16},{64,96},{80,112},{96,64},{112,80},{1... | collective-permute-start | bytes 196616 | tf_op jit(solution)/shard_map/ppermute | solution.py:38
  11.3 3.5 %collective-permute-start.2 = (bf16[2,128,128]{2,1,0:T(8,128)(2,1)}, bf16[2,128,128]{2,1,0:T(8,128)(2,1)S(1)}, u32[]{:S(2)}, u32[]{:S(2)}) collective-permute-start(bf16[2,128,128]{2,1,0:T(8,128)(2,1)} %bitcast.46), channel_id=1, source_target_pairs={{0,16},{16,32},{32,48},{48,0},{64,80},{80,96},{96,112},{112,64},{1... | collective-permute-start | bytes 196616 | tf_op jit(solution)/shard_map/ppermute | solution.py:38
  12.7 4.9 %copy-start.6 = (s32[4]{0:T(128)}, s32[4]{0:T(128)S(1)}, u32[]{:S(2)}) copy-start(s32[4]{0:T(128)S(1)} %pad_add_fusion.w) | copy-start | bytes 52
  14.8 0.8 copy-start.5
  15.7 0.7 copy-start.11
  22.9 12.8 %copy-start.7 = (s32[4]{0:T(128)S(1)}, s32[4]{0:T(128)}, u32[]{:S(2)}) copy-start(s32[4]{0:T(128)} %copy-done.6) | copy-start | bytes 52
  22.9 12.8 %copy-start.12 = (s32[16]{0:T(128)S(1)}, s32[16]{0:T(128)}, u32[]{:S(2)}) copy-start(s32[16]{0:T(128)} %src.11) | copy-start | bytes 196
  22.9 28.4 %copy-start.18 = (s32[16,2]{0,1:T(2,128)S(1)}, s32[16,2]{0,1:T(2,128)}, u32[]{:S(2)}) copy-start(s32[16,2]{0,1:T(2,128)} %param.8) | copy-start | bytes 388
  22.9 67.3 %all-to-all-start = ((bf16[4,2,3,256,256]{4,3,2,1,0:T(8,128)(2,1)}), bf16[4,2,3,256,256]{4,3,2,1,0:T(8,128)(2,1)}, u32[]{:S(2)}, u32[]{:S(2)}) async-start(bf16[4,2,3,256,256]{4,3,2,1,0:T(8,128)(2,1)} %pack.2), calls=%async_computation | async-start | bytes 6291456 | tf_op jit(solution)/shard_map/all_to_all | solution.py:42
  28.0 5.0 %collective-permute-start.3 = (bf16[2,128,128]{2,1,0:T(8,128)(2,1)S(1)}, bf16[2,128,128]{2,1,0:T(8,128)(2,1)S(1)}, u32[]{:S(2)}, u32[]{:S(2)}) collective-permute-start(bf16[2,128,128]{2,1,0:T(8,128)(2,1)S(1)} %get-tuple-element.32), channel_id=1, source_target_pairs={{0,64},{16,80},{32,96},{48,112},{64,128},{80,144},{96,160},{112,17... | collective-permute-start | bytes 196616 | tf_op jit(solution)/shard_map/ppermute | solution.py:34
  29.3 5.9 %collective-permute-start.4 = (bf16[2,128,128]{2,1,0:T(8,128)(2,1)S(1)}, bf16[2,128,128]{2,1,0:T(8,128)(2,1)S(1)}, u32[]{:S(2)}, u32[]{:S(2)}) collective-permute-start(bf16[2,128,128]{2,1,0:T(8,128)(2,1)S(1)} %get-tuple-element.33), channel_id=1, source_target_pairs={{0,128},{16,144},{32,160},{48,176},{64,192},{80,208},{96,224},{112... | collective-permute-start | bytes 196616 | tf_op jit(solution)/shard_map/ppermute | solution.py:34
  30.4 5.4 %collective-permute-start.5 = (bf16[2,128,128]{2,1,0:T(8,128)(2,1)S(1)}, bf16[2,128,128]{2,1,0:T(8,128)(2,1)S(1)}, u32[]{:S(2)}, u32[]{:S(2)}) collective-permute-start(bf16[2,128,128]{2,1,0:T(8,128)(2,1)S(1)} %get-tuple-element.34), channel_id=1, source_target_pairs={{0,192},{16,208},{32,224},{48,240},{64,0},{80,16},{96,32},{112,48}... | collective-permute-start | bytes 196616 | tf_op jit(solution)/shard_map/ppermute | solution.py:34
  33.0 19.1 %copy-start.10 = (bf16[16,128]{1,0:T(8,128)(2,1)}, bf16[16,128]{1,0:T(8,128)(2,1)S(1)}, u32[]{:S(2)}) copy-start(bf16[16,128]{1,0:T(8,128)(2,1)S(1)} %slice.97.rest_0_.refs_4_) | copy-start | bytes 12292
  36.3 9.6 %collective-permute-start.6 = (bf16[2,128,128]{2,1,0:T(8,128)(2,1)S(1)}, bf16[2,128,128]{2,1,0:T(8,128)(2,1)S(1)}, u32[]{:S(2)}, u32[]{:S(2)}) collective-permute-start(bf16[2,128,128]{2,1,0:T(8,128)(2,1)S(1)} %text_that_came.1), channel_id=1, source_target_pairs={{0,1},{1,2},{2,3},{3,0},{4,5},{5,6},{6,7},{7,4},{8,9},{9,10},{10,1... | collective-permute-start | bytes 196616 | tf_op jit(solution)/shard_map/ppermute | solution.py:28
  38.8 7.2 %collective-permute-start.7 = (bf16[2,128,128]{2,1,0:T(8,128)(2,1)S(1)}, bf16[2,128,128]{2,1,0:T(8,128)(2,1)S(1)}, u32[]{:S(2)}, u32[]{:S(2)}) collective-permute-start(bf16[2,128,128]{2,1,0:T(8,128)(2,1)S(1)} %text_that_came.1), channel_id=1, source_target_pairs={{0,2},{1,3},{2,0},{3,1},{4,6},{5,7},{6,4},{7,5},{8,10},{9,11},{10,... | collective-permute-start | bytes 196616 | tf_op jit(solution)/shard_map/ppermute | solution.py:28
  43.2 4.7 %collective-permute-start.8 = (bf16[2,128,128]{2,1,0:T(8,128)(2,1)S(1)}, bf16[2,128,128]{2,1,0:T(8,128)(2,1)S(1)}, u32[]{:S(2)}, u32[]{:S(2)}) collective-permute-start(bf16[2,128,128]{2,1,0:T(8,128)(2,1)S(1)} %text_that_came.1), channel_id=1, source_target_pairs={{0,3},{1,0},{2,1},{3,2},{4,7},{5,4},{6,5},{7,6},{8,11},{9,8},{10,9... | collective-permute-start | bytes 196616 | tf_op jit(solution)/shard_map/ppermute | solution.py:28
  48.0 20.8 %collective-permute-start.10 = (bf16[4,2,128,128]{3,2,1,0:T(8,128)(2,1)S(1)}, bf16[4,2,128,128]{3,2,1,0:T(8,128)(2,1)S(1)}, u32[]{:S(2)}, u32[]{:S(2)}) collective-permute-start(bf16[4,2,128,128]{3,2,1,0:T(8,128)(2,1)S(1)} %pad_maximum_fusion.t0), channel_id=1, source_target_pairs={{0,8},{1,9},{2,10},{3,11},{4,12},{5,13},{6,14},{7,15},{8,0},{9,1},... | collective-permute-start | bytes 786440 | tf_op jit(solution)/shard_map/ppermute | solution.py:22
  49.8 26.3 %collective-permute-start.11 = (bf16[4,2,128,128]{3,2,1,0:T(8,128)(2,1)S(1)}, bf16[4,2,128,128]{3,2,1,0:T(8,128)(2,1)S(1)}, u32[]{:S(2)}, u32[]{:S(2)}) collective-permute-start(bf16[4,2,128,128]{3,2,1,0:T(8,128)(2,1)S(1)} %pad_maximum_fusion.t0), channel_id=1, source_target_pairs={{0,12},{1,13},{2,14},{3,15},{4,0},{5,1},{6,2},{7,3},{8,4},{9,5},{1... | collective-permute-start | bytes 786440 | tf_op jit(solution)/shard_map/ppermute | solution.py:22
  51.4 24.7 %collective-permute-start.9 = (bf16[4,2,128,128]{3,2,1,0:T(8,128)(2,1)S(1)}, bf16[4,2,128,128]{3,2,1,0:T(8,128)(2,1)S(1)}, u32[]{:S(2)}, u32[]{:S(2)}) collective-permute-start(bf16[4,2,128,128]{3,2,1,0:T(8,128)(2,1)S(1)} %pad_maximum_fusion.t0), channel_id=1, source_target_pairs={{0,4},{1,5},{2,6},{3,7},{4,8},{5,9},{6,10},{7,11},{8,12},{9,13},{1... | collective-permute-start | bytes 786440 | tf_op jit(solution)/shard_map/ppermute | solution.py:22
  52.1 24.0 %copy-start.8 = (s32[4]{0:T(128)S(1)}, s32[4]{0:T(128)}, u32[]{:S(2)}) copy-start(s32[4]{0:T(128)} %copy-done.6) | copy-start | bytes 52
  76.1 2.2 copy-start
  80.9 14.0 %copy-start.3 = (bf16[2,128,512]{2,1,0:T(8,128)(2,1)}, bf16[2,128,512]{2,1,0:T(8,128)(2,1)S(1)}, u32[]{:S(2)}) copy-start(bf16[2,128,512]{2,1,0:T(8,128)(2,1)S(1)} %get-tuple-element.39) | copy-start | bytes 786436
  81.0 26.8 %collective-permute-start.13 = (bf16[256,512]{1,0:T(8,128)(2,1)S(1)}, bf16[256,512]{1,0:T(8,128)(2,1)}, u32[]{:S(2)}, u32[]{:S(2)}) collective-permute-start(bf16[256,512]{1,0:T(8,128)(2,1)S(1)} %bitcast.39), channel_id=1, source_target_pairs={{0,3},{1,0},{2,1},{3,2},{4,7},{5,4},{6,5},{7,6},{8,11},{9,8},{10,9... | collective-permute-start | bytes 786440 | tf_op jit(solution)/shard_map/ppermute | solution.py:28
  86.2 23.5 %collective-permute-start.12 = (bf16[256,512]{1,0:T(8,128)(2,1)S(1)}, bf16[256,512]{1,0:T(8,128)(2,1)}, u32[]{:S(2)}, u32[]{:S(2)}) collective-permute-start(bf16[256,512]{1,0:T(8,128)(2,1)S(1)} %bitcast.40), channel_id=1, source_target_pairs={{0,1},{1,2},{2,3},{3,0},{4,5},{5,6},{6,7},{7,4},{8,9},{9,10},{10,1... | collective-permute-start | bytes 786440 | tf_op jit(solution)/shard_map/ppermute | solution.py:28
  86.2 17.0 %collective-permute-start.16 = (bf16[4,2,128,128]{3,2,1,0:T(8,128)(2,1)S(1)}, bf16[4,2,128,128]{3,2,1,0:T(8,128)(2,1)S(1)}, u32[]{:S(2)}, u32[]{:S(2)}) collective-permute-start(bf16[4,2,128,128]{3,2,1,0:T(8,128)(2,1)S(1)} %get-tuple-element.43), channel_id=1, source_target_pairs={{0,192},{16,208},{32,224},{48,240},{64,0},{80,16},{96,32},{112,48}... | collective-permute-start | bytes 786440 | tf_op jit(solution)/shard_map/ppermute | solution.py:34
  86.3 20.8 %collective-permute-start.15 = (bf16[4,2,128,128]{3,2,1,0:T(8,128)(2,1)S(1)}, bf16[4,2,128,128]{3,2,1,0:T(8,128)(2,1)S(1)}, u32[]{:S(2)}, u32[]{:S(2)}) collective-permute-start(bf16[4,2,128,128]{3,2,1,0:T(8,128)(2,1)S(1)} %get-tuple-element.42), channel_id=1, source_target_pairs={{0,128},{16,144},{32,160},{48,176},{64,192},{80,208},{96,224},{112... | collective-permute-start | bytes 786440 | tf_op jit(solution)/shard_map/ppermute | solution.py:34
  88.6 20.4 %collective-permute-start.14 = (bf16[4,2,128,128]{3,2,1,0:T(8,128)(2,1)S(1)}, bf16[4,2,128,128]{3,2,1,0:T(8,128)(2,1)S(1)}, u32[]{:S(2)}, u32[]{:S(2)}) collective-permute-start(bf16[4,2,128,128]{3,2,1,0:T(8,128)(2,1)S(1)} %get-tuple-element.41), channel_id=1, source_target_pairs={{0,64},{16,80},{32,96},{48,112},{64,128},{80,144},{96,160},{112,17... | collective-permute-start | bytes 786440 | tf_op jit(solution)/shard_map/ppermute | solution.py:34
  90.2 33.2 %all-to-all-start.2 = ((bf16[4,2,1,256,256]{4,3,2,1,0:T(8,128)(2,1)}), bf16[4,2,1,256,256]{4,3,2,1,0:T(8,128)(2,1)S(1)}, u32[]{:S(2)}, u32[]{:S(2)}) async-start(bf16[4,2,1,256,256]{4,3,2,1,0:T(8,128)(2,1)} %pack.3), calls=%async_computation.2 | async-start | bytes 2097152 | tf_op jit(solution)/shard_map/all_to_all | solution.py:42
  102.2 0.9 copy-start.4
  103.2 41.5 %collective-permute-start.17 = (bf16[256,512]{1,0:T(8,128)(2,1)S(1)}, bf16[256,512]{1,0:T(8,128)(2,1)}, u32[]{:S(2)}, u32[]{:S(2)}) collective-permute-start(bf16[256,512]{1,0:T(8,128)(2,1)S(1)} %relay.1), channel_id=1, source_target_pairs={{0,2},{1,3},{2,0},{3,1},{4,6},{5,7},{6,4},{7,5},{8,10},{9,11},{10,... | collective-permute-start | bytes 786440 | tf_op jit(solution)/shard_map/ppermute | solution.py:28
  109.6 8.2 %copy-start.9 = (s32[4]{0:T(128)S(1)}, s32[4]{0:T(128)}, u32[]{:S(2)}) copy-start(s32[4]{0:T(128)} %copy-done.6) | copy-start | bytes 52
  116.3 37.8 %collective-permute-start.21 = (bf16[256,512]{1,0:T(8,128)(2,1)}, bf16[256,512]{1,0:T(8,128)(2,1)S(1)}, u32[]{:S(2)}, u32[]{:S(2)}) collective-permute-start(bf16[256,512]{1,0:T(8,128)(2,1)} %get-tuple-element.56), channel_id=1, source_target_pairs={{0,3},{1,0},{2,1},{3,2},{4,7},{5,4},{6,5},{7,6},{8,11},{9,8},{10,9... | collective-permute-start | bytes 786440 | tf_op jit(solution)/shard_map/ppermute | solution.py:28
  118.7 0.7 copy-start.2
  119.4 17.2 %collective-permute-start.20 = (bf16[4,2,128,128]{3,2,1,0:T(8,128)(2,1)S(1)}, bf16[4,2,128,128]{3,2,1,0:T(8,128)(2,1)S(1)}, u32[]{:S(2)}, u32[]{:S(2)}) collective-permute-start(bf16[4,2,128,128]{3,2,1,0:T(8,128)(2,1)S(1)} %get-tuple-element.51), channel_id=1, source_target_pairs={{0,16},{16,32},{32,48},{48,0},{64,80},{80,96},{96,112},{112,64},{1... | collective-permute-start | bytes 786440 | tf_op jit(solution)/shard_map/ppermute | solution.py:38
  122.8 19.8 %collective-permute-start.19 = (bf16[4,2,128,128]{3,2,1,0:T(8,128)(2,1)S(1)}, bf16[4,2,128,128]{3,2,1,0:T(8,128)(2,1)S(1)}, u32[]{:S(2)}, u32[]{:S(2)}) collective-permute-start(bf16[4,2,128,128]{3,2,1,0:T(8,128)(2,1)S(1)} %get-tuple-element.50), channel_id=1, source_target_pairs={{0,32},{16,48},{32,0},{48,16},{64,96},{80,112},{96,64},{112,80},{1... | collective-permute-start | bytes 786440 | tf_op jit(solution)/shard_map/ppermute | solution.py:38
  123.4 1.0 copy-start.14
  124.5 29.9 %all-to-all-start.1 = ((bf16[4,2,2,256,256]{4,3,2,1,0:T(8,128)(2,1)}), bf16[4,2,2,256,256]{4,3,2,1,0:T(8,128)(2,1)}, u32[]{:S(2)}, u32[]{:S(2)}) async-start(bf16[4,2,2,256,256]{4,3,2,1,0:T(8,128)(2,1)} %get-tuple-element.44), calls=%async_computation.1 | async-start | bytes 4194304 | tf_op jit(solution)/shard_map/all_to_all | solution.py:42
  129.0 82.0 %all-gather.4.cloned.1.call-start = ((), (), s32[]{:S(2)}) async-start(), calls=%async_computation.4 | async-start | bytes 4456448 | tf_op jit(solution)/shard_map/all_gather | solution.py:359
  135.6 18.5 %collective-permute-start.22 = (bf16[256,512]{1,0:T(8,128)(2,1)}, bf16[256,512]{1,0:T(8,128)(2,1)S(1)}, u32[]{:S(2)}, u32[]{:S(2)}) collective-permute-start(bf16[256,512]{1,0:T(8,128)(2,1)} %get-tuple-element.57), channel_id=1, source_target_pairs={{0,1},{1,2},{2,3},{3,0},{4,5},{5,6},{6,7},{7,4},{8,9},{9,10},{10,1... | collective-permute-start | bytes 786440 | tf_op jit(solution)/shard_map/ppermute | solution.py:28
  136.6 8.2 %copy-start.15 = (bf16[4,2,128,128]{3,2,1,0:T(8,128)(2,1)}, bf16[4,2,128,128]{3,2,1,0:T(8,128)(2,1)S(1)}, u32[]{:S(2)}) copy-start(bf16[4,2,128,128]{3,2,1,0:T(8,128)(2,1)S(1)} %collective-permute-done.20.t3) | copy-start | bytes 786436
  136.6 7.5 %collective-permute-start.18 = (bf16[4,2,128,128]{3,2,1,0:T(8,128)(2,1)S(1)}, bf16[4,2,128,128]{3,2,1,0:T(8,128)(2,1)S(1)}, u32[]{:S(2)}, u32[]{:S(2)}) collective-permute-start(bf16[4,2,128,128]{3,2,1,0:T(8,128)(2,1)S(1)} %get-tuple-element.49), channel_id=1, source_target_pairs={{0,48},{16,0},{32,16},{48,32},{64,112},{80,64},{96,80},{112,96},{1... | collective-permute-start | bytes 786440 | tf_op jit(solution)/shard_map/ppermute | solution.py:38
  142.6 2.2 copy-start.16
  144.1 0.7 copy-start.17
  144.8 9.3 %copy-start.1 = (f32[256,512]{1,0:T(8,128)S(1)}, f32[256,512]{1,0:T(8,128)}, u32[]{:S(2)}) copy-start(f32[256,512]{1,0:T(8,128)} %get-tuple-element.46.a) | copy-start | bytes 1572868
  151.6 11.6 %copy-start.13 = (bf16[4,2,2,256,256]{4,3,2,1,0:T(8,128)(2,1)S(1)}, bf16[4,2,2,256,256]{4,3,2,1,0:T(8,128)(2,1)}, u32[]{:S(2)}) copy-start(bf16[4,2,2,256,256]{4,3,2,1,0:T(8,128)(2,1)} %get-tuple-element.52) | copy-start | bytes 6291460
  151.6 10.8 %collective-permute-start.23 = (bf16[256,512]{1,0:T(8,128)(2,1)}, bf16[256,512]{1,0:T(8,128)(2,1)S(1)}, u32[]{:S(2)}, u32[]{:S(2)}) collective-permute-start(bf16[256,512]{1,0:T(8,128)(2,1)} %get-tuple-element.58), channel_id=1, source_target_pairs={{0,2},{1,3},{2,0},{3,1},{4,6},{5,7},{6,4},{7,5},{8,10},{9,11},{10,... | collective-permute-start | bytes 786440 | tf_op jit(solution)/shard_map/ppermute | solution.py:28
Sparse Core Ops, SparseCore 0:
  10.4 49.6 all-gather.5
  163.3 47.6 all-gather.3
